TPU v7x, 32 devices: a whole 2x2x4 slice. The times are simulated.
32 devices in a mesh: space: 8 (over z, x), vel: 4 (over y, core).
Axes of the slice: x: 2, y: 2, z: 4, core: 2. Of those that a mesh axis runs over, the one named last changes fastest.
Arguments:
- populations: float32 [64, 512, 2048], P('vel', 'space'), may hold values from 0.2 to 41, as said below
- shift_x: int32 [64], P('vel'), may hold values from -8 to 8, as said below
- shift_y: int32 [64], P('vel'), may hold values from -8 to 8, as said below
- frac_x: float32 [64], P('vel'), may hold values from 0 to 1
- frac_y: float32 [64], P('vel'), may hold values from 0 to 1
- inflow: float32 [64], P('vel'), may hold values from 0.5 to 2
- wall_state: float32 [64], P('vel'), may hold values from 0.5 to 2
- heights: int32 [2048], replicated, may hold values from 0 to 128
- impact_frequency_factor: float32 [], replicated, may hold values from 0.5 to 2
Outputs:
- relaxed: float32 [64, 512, 2048], P('vel', 'space')
Inputs may be any that keep to these rules, and one draw needn't show every extreme that they name: `populations`: positive. `shift_x`: the values -8 and 8 both occur. `shift_y`: the values -8 and 8 both occur.
All inputs are finite; a program needn't handle non-finite values.
Results may differ from a plain program's by a relative error of at most 0.00002.
Values sent between devices are 32-bit elements; how exact they have to be, the bound alone decides.
No kernel may reach another device: no remote copies, remote signals or barrier semaphores. Data moves between devices by JAX's collectives and lax.ppermute only.
A program may use at most 128 MiB of HBM per device.

v0:
```python
import math

import jax
import jax.numpy as jnp
from jax import lax
from jax.sharding import PartitionSpec as P

SPEED_TALLY = 64
CFL = 8


def padded_2(block, sides, width):
    for axis, dim in sides:
        count = lax.axis_size(axis)
        forward = [(i, i + 1) for i in range(count - 1)]
        backward = [(target, source) for source, target in forward]
        low = lax.ppermute(
            lax.slice_in_dim(block, block.shape[dim] - width, None, axis=dim), axis, forward
        )
        high = lax.ppermute(lax.slice_in_dim(block, 0, width, axis=dim), axis, backward)
        block = jnp.concatenate([low, block, high], axis=dim)
    return block


def pad_edges(planes, fill_value, rim_width, which_dim):
    edge_shape = list(planes.shape)
    edge_shape[which_dim] = rim_width
    border = jnp.broadcast_to(fill_value[:, None, None], tuple(edge_shape))
    return jnp.concatenate([border, planes, border], which_dim)


def slide_lines(padded, whole_part, frac_part, which_dim, length, rim_width):
    near_start = rim_width - whole_part
    total = jnp.zeros(
        padded.shape[:which_dim] + (length,) + padded.shape[which_dim + 1 :], jnp.float32
    )
    for offset in range(2 * rim_width):
        weight = jnp.where(
            near_start == offset,
            1.0 - frac_part,
            jnp.where(near_start - 1 == offset, frac_part, 0.0),
        )
        piece = lax.slice_in_dim(padded, offset, offset + length, 1, which_dim)
        total = total + weight[:, None, None] * piece
    return total


def maxwellian_profiles(
    particle_concentration, flux_x, flux_y, motion_work_share, impact_frequency_factor
):
    average_drift_horizontal = flux_x / particle_concentration
    average_drift_vertical = flux_y / particle_concentration
    cellwise_thermal_spread = 0.5 * (
        motion_work_share / particle_concentration
        - average_drift_horizontal * average_drift_horizontal
        - average_drift_vertical * average_drift_vertical
    )
    approach_weighting = 1.0 - jnp.exp(
        -impact_frequency_factor
        * particle_concentration
        / (SPEED_TALLY * jnp.sqrt(cellwise_thermal_spread))
    )
    highest_ceiling = particle_concentration / (2.0 * math.pi * cellwise_thermal_spread)
    reciprocal_doubled_thermal = 0.5 / cellwise_thermal_spread
    return (
        average_drift_horizontal,
        average_drift_vertical,
        reciprocal_doubled_thermal,
        highest_ceiling,
        approach_weighting,
    )


def relax_cells(after_move, vel_x, vel_y, impact_frequency_factor):
    planes, row_count, col_count = after_move.shape
    flat = after_move.reshape(planes, row_count * col_count)
    wide_x = vel_x[:, None]
    wide_y = vel_y[:, None]
    term_mass = jnp.sum(flat, 0)
    term_x = jnp.sum(flat * wide_x, 0)
    term_y = jnp.sum(flat * wide_y, 0)
    term_energy = jnp.sum(flat * (wide_x * wide_x + wide_y * wide_y), 0)
    aggregate_moments = lax.psum((term_mass, term_x, term_y, term_energy), "vel")
    (
        average_drift_horizontal,
        average_drift_vertical,
        reciprocal_doubled_thermal,
        highest_ceiling,
        approach_weighting,
    ) = maxwellian_profiles(
        aggregate_moments[0],
        aggregate_moments[1],
        aggregate_moments[2],
        aggregate_moments[3],
        impact_frequency_factor,
    )
    horizontal_spacing = wide_x - average_drift_horizontal[None, :]
    vertical_spacing = wide_y - average_drift_vertical[None, :]
    maxwellian_state = highest_ceiling[None, :] * jnp.exp(
        -(horizontal_spacing * horizontal_spacing + vertical_spacing * vertical_spacing)
        * reciprocal_doubled_thermal[None, :]
    )
    relaxed = flat + approach_weighting[None, :] * (maxwellian_state - flat)
    return relaxed.reshape(after_move.shape)


def per_device(
    populations,
    shift_x,
    shift_y,
    frac_x,
    frac_y,
    inflow,
    wall_state,
    heights,
    impact_frequency_factor,
):
    rim_width = CFL + 1
    vel_local, row_count, col_count = populations.shape
    space_count = lax.axis_size("space")
    vel_x = shift_x.astype(jnp.float32) + frac_x
    vel_y = shift_y.astype(jnp.float32) + frac_y
    padded = pad_edges(populations, inflow, rim_width, 2)
    moved_x = slide_lines(padded, shift_x, frac_x, 2, col_count, rim_width)
    rimmed = padded_2(moved_x, (("space", 1),), rim_width)
    row_index = (
        lax.axis_index("space") * row_count
        - rim_width
        + jnp.arange(row_count + 2 * rim_width, dtype=jnp.int32)
    )
    outside = (row_index < 0) | (row_index >= row_count * space_count)
    rimmed = jnp.where(outside[None, :, None], inflow[:, None, None], rimmed)
    moved_y = slide_lines(rimmed, shift_y, frac_y, 1, row_count, rim_width)
    global_rows = lax.axis_index("space") * row_count + jnp.arange(row_count, dtype=jnp.int32)
    solid_mask = global_rows[:, None] < heights[None, :]
    after_move = jnp.where(solid_mask[None], wall_state[:, None, None], moved_y)
    return relax_cells(after_move, vel_x, vel_y, impact_frequency_factor)


def solution(mesh):
    return jax.shard_map(
        per_device,
        mesh=mesh,
        in_specs=(
            P("vel", "space", None),
            P("vel"),
            P("vel"),
            P("vel"),
            P("vel"),
            P("vel"),
            P("vel"),
            P(),
            P(),
        ),
        out_specs=P("vel", "space", None),
        check_vma=False,
    )
```

profile of v0, /device:TPU:9, one launch (start us, length us, event | category | flops | bytes accessed | tf_op | source)
XLA Modules:
  0.0 301.4 jit_solution(10442161569191749459)
XLA Ops:
  6.6 0.0 all-reduce.3.cloned.1.call-start
  6.6 11.6 %copy.10 = f32[16,64,2048]{2,0,1:T(8,128)} copy(f32[16,64,2048]{2,1,0:T(8,128)} %param.9) | data formatting | bytes 16777216 | tf_op args[0]
  18.3 0.7 compare_select_fusion.71
  19.0 0.1 broadcast_in_dim.78
  19.1 0.0 copy-start.1
  19.1 70.6 %fusion.3 = f32[16,64,2048]{2,0,1:T(8,128)S(1)} fusion(f32[16,64,9]{2,0,1:T(8,128)S(1)} %broadcast_in_dim.78, f32[16,64,2048]{2,0,1:T(8,128)} %copy.10, f32[16]{0:T(128)S(1)} %get-tuple-element.62, f32[16]{0:T(128)S(1)} %get-tuple-element.61, f32[16]{0:T(128)S(1)} %get-tuple-element.60, f32[16]{0:T(128)S(1)} %get-tuple-element.59, ...), kind=kLoop, calls=%fused_computation.19 | loop fusion | flops 109051904 | bytes 16815232 | tf_op jit(solution)/shard_map/add | solution.py:44
  89.7 0.0 copy-start
  89.7 3.4 %copy-done = f32[16,64,2048]{2,0,1:T(8,128)} copy-done((f32[16,64,2048]{2,0,1:T(8,128)}, f32[16,64,2048]{2,0,1:T(8,128)S(1)}, u32[]{:S(2)}) %copy-start) | copy-done | bytes 8388632
  93.1 0.2 fusion.68
  93.2 3.1 %collective-permute-start = (f32[16,9,2048]{2,0,1:T(8,128)S(1)}, f32[16,9,2048]{2,0,1:T(8,128)S(1)}, u32[]{:S(2)}, u32[]{:S(2)}) collective-permute-start(f32[16,9,2048]{2,0,1:T(8,128)S(1)} %get-tuple-element.21), channel_id=1, source_target_pairs={{0,4},{4,8},{8,12},{12,16},{16,20},{20,24},{24,28},{1,5},{5,9},{9,... | collective-permute-start | bytes 3538952 | tf_op jit(solution)/shard_map/ppermute | solution.py:17
  96.4 3.2 %collective-permute-start.1 = (f32[16,9,2048]{2,0,1:T(8,128)S(1)}, f32[16,9,2048]{2,0,1:T(8,128)}, u32[]{:S(2)}, u32[]{:S(2)}) collective-permute-start(f32[16,9,2048]{2,0,1:T(8,128)S(1)} %get-tuple-element.22), channel_id=1, source_target_pairs={{4,0},{8,4},{12,8},{16,12},{20,16},{24,20},{28,24},{5,1},{9,5},{13... | collective-permute-start | bytes 3538952 | tf_op jit(solution)/shard_map/ppermute | solution.py:20
  99.7 0.0 copy-done.1
  99.7 0.1 broadcast_compare_fusion
  99.8 0.0 copy-start.3
  99.8 0.0 copy-start.4
  99.8 0.0 copy-start.5
  99.8 0.0 copy-start.6
  99.9 0.0 copy-start.7
  99.9 0.0 copy-start.8
  99.9 0.0 copy-start.9
  99.9 0.0 copy-start.10
  99.9 0.0 copy-start.11
  99.9 0.0 copy-start.12
  99.9 0.0 copy-start.13
  99.9 0.0 copy-start.14
  99.9 0.0 copy-start.15
  99.9 0.0 copy-start.16
  100.0 0.0 copy-start.17
  100.0 0.0 copy-start.18
  100.0 0.0 copy-start.19
  100.0 0.0 copy-start.20
  100.0 0.0 copy-start.21
  100.0 0.0 copy-start.26
  100.0 46.2 %collective-permute-done = f32[16,9,2048]{2,0,1:T(8,128)S(1)} collective-permute-done((f32[16,9,2048]{2,0,1:T(8,128)S(1)}, f32[16,9,2048]{2,0,1:T(8,128)S(1)}, u32[]{:S(2)}, u32[]{:S(2)}) %collective-permute-start) | collective-permute-done | bytes 1179680 | tf_op jit(solution)/shard_map/ppermute | solution.py:17
  146.3 3.0 %collective-permute-done.1 = f32[16,9,2048]{2,0,1:T(8,128)} collective-permute-done((f32[16,9,2048]{2,0,1:T(8,128)S(1)}, f32[16,9,2048]{2,0,1:T(8,128)}, u32[]{:S(2)}, u32[]{:S(2)}) %collective-permute-start.1) | collective-permute-done | bytes 1179680 | tf_op jit(solution)/shard_map/ppermute | solution.py:20
  149.3 11.3 %maximum_select_fusion = f32[16,82,2048]{2,0,1:T(8,128)} fusion(f32[16,9,2048]{2,0,1:T(8,128)} %collective-permute-done.1, f32[16,64,2048]{2,0,1:T(8,128)} %copy-done, f32[16,9,2048]{2,0,1:T(8,128)S(1)} %collective-permute-done, f32[16]{0:T(128)} %param.14, pred[82]{0:T(512)(128)(4,1)S(1)} %compare_or_fusion), kind=kLoop, calls=%fused_computation.15 | loop fusion | flops 8060928 | bytes 21495954 | tf_op jit(solution)/shard_map/jit(_where)/select_n | solution.py:132
  160.6 0.0 copy-done.4
  160.6 0.0 copy-done.5
  160.6 0.0 copy-done.6
  160.6 0.0 copy-done.7
  160.6 0.0 copy-done.8
  160.6 0.0 copy-done.9
  160.6 0.0 copy-done.10
  160.6 0.0 copy-done.11
  160.7 0.0 copy-done.12
  160.7 0.0 copy-done.13
  160.7 0.0 copy-done.14
  160.7 0.0 copy-done.15
  160.8 59.8 %multiply_reduce_fusion.2 = (f32[64,2048]{1,0:T(8,128)S(1)}, f32[64,2048]{1,0:T(8,128)S(1)}, f32[64,2048]{1,0:T(8,128)S(1)}, f32[64,2048]{1,0:T(8,128)S(1)}, f32[16,64,2048]{2,0,1:T(8,128)}) fusion(f32[16]{0:T(128)S(1)} %copy-done.20, f32[16]{0:T(128)S(1)} %get-tuple-element.43, f32[16]{0:T(128)S(1)} %get-tuple-element.44, ...), kind=kLoop, calls=%fused_computation.117 | loop fusion | flops 89653248 | bytes 161613184 | tf_op jit(solution)/shard_map/reduce_sum | solution.py:82
  220.6 0.9 copy.14
  221.4 0.9 copy.15
  222.3 0.9 copy.16
  223.2 0.9 copy.17
  224.1 0.0 all-reduce.3.cloned.1.call-update
  224.8 51.4 %all-reduce.3.cloned.1.call-done = (f32[131072]{0:T(1024)}, f32[131072]{0:T(1024)}, f32[131072]{0:T(1024)}, f32[131072]{0:T(1024)}) async-done(((f32[131072]{0:T(1024)}, f32[131072]{0:T(1024)}, f32[131072]{0:T(1024)}, f32[131072]{0:T(1024)}), (f32[131072]{0:T(1024)}, f32[131072]{0:T(1024)}, f32[131072]{0:T(1024)}, f32[131072]{0:T(1024)})) %all-reduce.3.cloned.1.call-update) | async-done | bytes 2097168 | tf_op jit(solution)/shard_map/psum | solution.py:83
  276.2 1.9 exponential_subtract_fusion
  278.1 1.2 multiply_divide_fusion
  279.4 0.1 mul.487
  279.5 0.1 mul.491
  279.5 0.1 mul.483
  279.6 0.1 sub.53
  279.7 0.1 sub.56
  279.8 6.5 %multiply_add_fusion = f32[16,64,2048]{2,0,1:T(8,128)S(1)} fusion(f32[16,64,2048]{2,0,1:T(8,128)} %get-tuple-element.17, f32[64,2048]{1,0:T(8,128)S(1)} %mul.491, f32[64,2048]{1,0:T(8,128)S(1)} %sub.56, f32[64,2048]{1,0:T(8,128)S(1)} %sub.53, f32[64,2048]{1,0:T(8,128)S(1)} %mul.487, f32[64,2048]{1,0:T(8,128)S(1)} %mul.483, f32[16]{0:T(128)S(1)} %get-tuple-element.43, ...), kind=kLoop, calls=%fused_computation.114 | loop fusion | flops 23068672 | bytes 19398784 | tf_op jit(solution)/shard_map/add | solution.py:103
  286.3 8.3 %copy.13 = f32[16,64,2048]{2,1,0:T(8,128)} copy(f32[16,64,2048]{2,0,1:T(8,128)S(1)} %multiply_add_fusion) | data formatting | bytes 16777216 | tf_op jit(solution)/shard_map/add | solution.py:103
  (20 shorter events, 0.0 us)
Async XLA Ops:
  6.5 11.7 %copy-start.25 = (s32[16]{0:T(128)S(1)}, s32[16]{0:T(128)}, u32[]{:S(2)}) copy-start(s32[16]{0:T(128)} %param.10) | copy-start | bytes 196
  6.5 11.7 %copy-start.23 = (s32[16]{0:T(128)S(1)}, s32[16]{0:T(128)}, u32[]{:S(2)}) copy-start(s32[16]{0:T(128)} %param.11) | copy-start | bytes 196
  6.5 11.7 %copy-start.24 = (f32[16]{0:T(128)S(1)}, f32[16]{0:T(128)}, u32[]{:S(2)}) copy-start(f32[16]{0:T(128)} %param.12) | copy-start | bytes 196
  6.5 11.7 %copy-start.22 = (f32[16]{0:T(128)S(1)}, f32[16]{0:T(128)}, u32[]{:S(2)}) copy-start(f32[16]{0:T(128)} %param.13) | copy-start | bytes 196
  6.5 12.5 %copy-start.2 = (f32[16]{0:T(128)S(1)}, f32[16]{0:T(128)}, u32[]{:S(2)}) copy-start(f32[16]{0:T(128)} %param.14) | copy-start | bytes 196
  6.6 269.6 %all-reduce.3.cloned.1.call-start = ((), (), s32[]{:S(2)}) async-start(), calls=%async_computation | async-start | bytes 4194304 | tf_op jit(solution)/shard_map/psum | solution.py:83
  19.1 80.6 %copy-start.1 = (s32[2048]{0:T(1024)S(1)}, s32[2048]{0:T(1024)}, u32[]{:S(2)}) copy-start(s32[2048]{0:T(1024)} %param.16) | copy-start | bytes 24580
  89.7 3.4 %copy-start = (f32[16,64,2048]{2,0,1:T(8,128)}, f32[16,64,2048]{2,0,1:T(8,128)S(1)}, u32[]{:S(2)}) copy-start(f32[16,64,2048]{2,0,1:T(8,128)S(1)} %fusion.3) | copy-start | bytes 25165828
  93.2 53.0 %collective-permute-start = (f32[16,9,2048]{2,0,1:T(8,128)S(1)}, f32[16,9,2048]{2,0,1:T(8,128)S(1)}, u32[]{:S(2)}, u32[]{:S(2)}) collective-permute-start(f32[16,9,2048]{2,0,1:T(8,128)S(1)} %get-tuple-element.21), channel_id=1, source_target_pairs={{0,4},{4,8},{8,12},{12,16},{16,20},{20,24},{24,28},{1,5},{5,9},{9,... | collective-permute-start | bytes 3538952 | tf_op jit(solution)/shard_map/ppermute | solution.py:17
  96.4 52.9 %collective-permute-start.1 = (f32[16,9,2048]{2,0,1:T(8,128)S(1)}, f32[16,9,2048]{2,0,1:T(8,128)}, u32[]{:S(2)}, u32[]{:S(2)}) collective-permute-start(f32[16,9,2048]{2,0,1:T(8,128)S(1)} %get-tuple-element.22), channel_id=1, source_target_pairs={{4,0},{8,4},{12,8},{16,12},{20,16},{24,20},{28,24},{5,1},{9,5},{13... | collective-permute-start | bytes 3538952 | tf_op jit(solution)/shard_map/ppermute | solution.py:20
  99.8 60.8 %copy-start.3 = (f32[16]{0:T(128)S(1)}, f32[16]{0:T(128)}, u32[]{:S(2)}) copy-start(f32[16]{0:T(128)} %get-tuple-element.25) | copy-start | bytes 196
  99.8 60.7 %copy-start.4 = (f32[16]{0:T(128)S(1)}, f32[16]{0:T(128)}, u32[]{:S(2)}) copy-start(f32[16]{0:T(128)} %get-tuple-element.26) | copy-start | bytes 196
  99.8 60.7 %copy-start.5 = (f32[16]{0:T(128)S(1)}, f32[16]{0:T(128)}, u32[]{:S(2)}) copy-start(f32[16]{0:T(128)} %get-tuple-element.27) | copy-start | bytes 196
  99.8 60.7 %copy-start.6 = (f32[16]{0:T(128)S(1)}, f32[16]{0:T(128)}, u32[]{:S(2)}) copy-start(f32[16]{0:T(128)} %get-tuple-element.28) | copy-start | bytes 196
  99.9 60.7 %copy-start.7 = (f32[16]{0:T(128)S(1)}, f32[16]{0:T(128)}, u32[]{:S(2)}) copy-start(f32[16]{0:T(128)} %get-tuple-element.29) | copy-start | bytes 196
  99.9 60.7 %copy-start.8 = (f32[16]{0:T(128)S(1)}, f32[16]{0:T(128)}, u32[]{:S(2)}) copy-start(f32[16]{0:T(128)} %get-tuple-element.30) | copy-start | bytes 196
  99.9 60.7 %copy-start.9 = (f32[16]{0:T(128)S(1)}, f32[16]{0:T(128)}, u32[]{:S(2)}) copy-start(f32[16]{0:T(128)} %get-tuple-element.31) | copy-start | bytes 196
  99.9 60.7 %copy-start.10 = (f32[16]{0:T(128)S(1)}, f32[16]{0:T(128)}, u32[]{:S(2)}) copy-start(f32[16]{0:T(128)} %get-tuple-element.32) | copy-start | bytes 196
  99.9 60.7 %copy-start.11 = (f32[16]{0:T(128)S(1)}, f32[16]{0:T(128)}, u32[]{:S(2)}) copy-start(f32[16]{0:T(128)} %get-tuple-element.33) | copy-start | bytes 196
  99.9 60.7 %copy-start.12 = (f32[16]{0:T(128)S(1)}, f32[16]{0:T(128)}, u32[]{:S(2)}) copy-start(f32[16]{0:T(128)} %get-tuple-element.34) | copy-start | bytes 196
  99.9 60.7 %copy-start.13 = (f32[16]{0:T(128)S(1)}, f32[16]{0:T(128)}, u32[]{:S(2)}) copy-start(f32[16]{0:T(128)} %get-tuple-element.35) | copy-start | bytes 196
  99.9 60.7 %copy-start.14 = (f32[16]{0:T(128)S(1)}, f32[16]{0:T(128)}, u32[]{:S(2)}) copy-start(f32[16]{0:T(128)} %get-tuple-element.36) | copy-start | bytes 196
  99.9 60.7 %copy-start.15 = (f32[16]{0:T(128)S(1)}, f32[16]{0:T(128)}, u32[]{:S(2)}) copy-start(f32[16]{0:T(128)} %get-tuple-element.37) | copy-start | bytes 196
  99.9 60.7 %copy-start.16 = (f32[16]{0:T(128)S(1)}, f32[16]{0:T(128)}, u32[]{:S(2)}) copy-start(f32[16]{0:T(128)} %get-tuple-element.38) | copy-start | bytes 196
  100.0 60.7 %copy-start.17 = (f32[16]{0:T(128)S(1)}, f32[16]{0:T(128)}, u32[]{:S(2)}) copy-start(f32[16]{0:T(128)} %get-tuple-element.39) | copy-start | bytes 196
  100.0 60.7 %copy-start.18 = (f32[16]{0:T(128)S(1)}, f32[16]{0:T(128)}, u32[]{:S(2)}) copy-start(f32[16]{0:T(128)} %get-tuple-element.40) | copy-start | bytes 196
  100.0 60.7 %copy-start.19 = (f32[16]{0:T(128)S(1)}, f32[16]{0:T(128)}, u32[]{:S(2)}) copy-start(f32[16]{0:T(128)} %get-tuple-element.41) | copy-start | bytes 196
  100.0 60.7 %copy-start.20 = (f32[16]{0:T(128)S(1)}, f32[16]{0:T(128)}, u32[]{:S(2)}) copy-start(f32[16]{0:T(128)} %get-tuple-element.42) | copy-start | bytes 196
  100.0 60.7 %copy-start.21 = (f32[16]{0:T(128)S(1)}, f32[16]{0:T(128)}, u32[]{:S(2)}) copy-start(f32[16]{0:T(128)} %get-tuple-element.63) | copy-start | bytes 196
  100.0 60.7 %copy-start.26 = (f32[16]{0:T(128)S(1)}, f32[16]{0:T(128)}, u32[]{:S(2)}) copy-start(f32[16]{0:T(128)} %param.15) | copy-start | bytes 196
Sparse Core Ops, SparseCore 0:
  224.3 51.8 all-reduce.2
where the time goes:
time: 303 us; the launch traced here: 301 us
  other arithmetic  152 us (50%)
  waiting for transfers between devices  101 us (33%)
  local copies, waits for them, and re-layouts  27.6 us (9%)
  between operations  14.5 us (5%)
  starting transfers between devices  6.4 us (2%)
    add x1, other arithmetic, slide_lines(): total = total + weight[:, None, None] * piece  70.6 us
    reduce_sum x1, other arithmetic, relax_cells(): term_energy = jnp.sum(flat * (wide_x * wide_x + wide_y * wide_y), 0)  59.8 us
    psum x1, waiting for transfers between devices, relax_cells(): lax.psum((term_mass, term_x, term_y, term_energy), 'vel')  51.4 us
    ppermute x1, waiting for transfers between devices, padded_2(): lax.ppermute(lax.slice_in_dim(block, block.shape[dim] - width, None, axis...  46.2 us
    unnamed x59, local copies, waits for them, and re-layouts  18.7 us
    select_n x1, other arithmetic, per_device(): rimmed = jnp.where(outside[None, :, None], inflow[:, None, None], rimmed)  11.3 us
    add x1, local copies, waits for them, and re-layouts, relax_cells(): relaxed = flat + approach_weighting[None, :] * (maxwellian_state - flat)  8.25 us
    add x1, other arithmetic, relax_cells(): relaxed = flat + approach_weighting[None, :] * (maxwellian_state - flat)  6.47 us
  transfers between devices with their start and end apart: 3, of which 3 were waited for; matrix products, arithmetic and copies ran while one was open for 0% of the time, Pallas kernels for 0%

commit v1 on v0

v1 whole, which is shorter than its diff:
```python
import functools
import math

import jax
import jax.numpy as jnp
from jax import lax
from jax.experimental import pallas as pl
from jax.experimental.pallas import tpu as pltpu
from jax.sharding import PartitionSpec as P

SPEED_TALLY = 64
CFL = 8
LOW_ROWS = CFL + 1
HIGH_ROWS = CFL
ROW = 8
LANE = 128
PAD = 24
F32 = jnp.float32
VMEM_LIMIT = 56 * 1024 * 1024

SMEM_SPEC = pl.BlockSpec(memory_space=pltpu.SMEM)
ANY_SPEC = pl.BlockSpec(memory_space=pl.ANY)
VMEM_SPEC = pl.BlockSpec(memory_space=pltpu.VMEM)


def params():
    return pltpu.CompilerParams(vmem_limit_bytes=VMEM_LIMIT)


def low_need(shift):
    return jnp.where(shift >= 0, shift + 1, 0)


def high_need(shift):
    return jnp.where(shift < 0, -shift, 0)


def pack_kernel(cuts, sy_ref, pop_ref, *refs):
    outs = refs[: len(cuts)]
    tail, head, low_pack, high_pack, sem_in, sem_out = refs[len(cuts) :]
    planes, row_tiles, lane_tiles = pop_ref.shape[:3]
    copies = [
        pltpu.make_async_copy(pop_ref.at[:, row_tiles - 2], tail.at[:, :, 0:8, :], sem_in.at[0]),
        pltpu.make_async_copy(pop_ref.at[:, row_tiles - 1], tail.at[:, :, 8:16, :], sem_in.at[1]),
        pltpu.make_async_copy(pop_ref.at[:, 0], head, sem_in.at[2]),
    ]
    for copy in copies:
        copy.start()
    for copy in copies:
        copy.wait()

    def one(v, offsets):
        low, high = offsets
        shift = sy_ref[v]

        @pl.when(shift >= 0)
        def _():
            for t in range(lane_tiles):
                low_pack[t, pl.ds(low, 8), :] = tail[v, t, pl.ds(15 - shift, 8), :]

        @pl.when(shift == CFL)
        def _():
            for t in range(lane_tiles):
                low_pack[t, pl.ds(low + 8, 8), :] = tail[v, t, pl.ds(15, 8), :]

        @pl.when(shift < 0)
        def _():
            for t in range(lane_tiles):
                high_pack[t, pl.ds(high, 8), :] = head[v, t]

        return low + low_need(shift), high + high_need(shift)

    lax.fori_loop(0, planes, one, (jnp.int32(0), jnp.int32(0)))
    copies = []
    for i, (pack, start, stop) in enumerate(cuts):
        source = (low_pack, high_pack)[pack].at[:, start:stop, :]
        copies.append(pltpu.make_async_copy(source, outs[i], sem_out.at[i]))
        copies[-1].start()
    for copy in copies:
        copy.wait()


def pack_rows(shift_y, pop, cuts):
    planes, _, lane_tiles = pop.shape[:3]
    return pl.pallas_call(
        functools.partial(pack_kernel, cuts),
        out_shape=[
            jax.ShapeDtypeStruct((lane_tiles, stop - start, LANE), F32) for _, start, stop in cuts
        ],
        in_specs=[SMEM_SPEC, ANY_SPEC],
        out_specs=[ANY_SPEC] * len(cuts),
        scratch_shapes=[
            pltpu.VMEM((planes, lane_tiles, 24, LANE), F32),
            pltpu.VMEM((planes, lane_tiles, 8, LANE), F32),
            pltpu.VMEM((lane_tiles, planes * LOW_ROWS + 16, LANE), F32),
            pltpu.VMEM((lane_tiles, planes * HIGH_ROWS + 16, LANE), F32),
            pltpu.SemaphoreType.DMA((3,)),
            pltpu.SemaphoreType.DMA((len(cuts),)),
        ],
        compiler_params=params(),
        name="pack_rows",
    )(shift_y, pop)


def load_tiles(pop_ref, padded, tiles, sems):
    lane_tiles = pop_ref.shape[2]
    copies = []
    for n, i in enumerate(tiles):
        target = padded.at[:, 1 : 1 + lane_tiles, PAD + ROW * i : PAD + ROW * (i + 1), :]
        copies.append(pltpu.make_async_copy(pop_ref.at[:, i], target, sems.at[n]))
        copies[-1].start()
    return copies


def fill_rows(padded, v, columns, start, count, value):
    block = jnp.full((ROW, LANE), value, F32)
    for t in columns:
        for r in range(start, start + count, ROW):
            padded[v, t, r : r + ROW, :] = block


def prepare_heights(heights_ref, bars):
    lane_tiles = heights_ref.shape[0]
    sublane = lax.broadcasted_iota(jnp.int32, (ROW, LANE), 0)
    for t in range(lane_tiles):
        bars[t] = jnp.broadcast_to(heights_ref[t : t + 1, :], (ROW, LANE)) - sublane


def advect_tile(padded, target, bars, v, j, first_row, scalars, solid_value):
    sx, sy, fx, fy = scalars
    lane_tiles = padded.shape[1] - 2
    lane = lax.broadcasted_iota(jnp.int32, (ROW, LANE), 1)
    start = PAD + ROW * j - sy
    near_roll = jnp.where(sx < 0, sx + LANE, sx)
    far_roll = jnp.where(sx + 1 < 0, sx + 1 + LANE, sx + 1)

    def moved(t):
        nearer = padded[v, t + 1, pl.ds(start, ROW), :]
        further = padded[v, t + 1, pl.ds(start - 1, ROW), :]
        line = (1.0 - fy) * nearer + fy * further
        return pltpu.roll(line, near_roll, 1), pltpu.roll(line, far_roll, 1)

    def finish(t, near, far):
        value = (1.0 - fx) * near + fx * far
        solid = first_row < bars[t]
        target[t] = jnp.where(solid, solid_value, value)

    @pl.when(sx >= 0)
    def _():
        own_near, own_far = lane >= sx, lane >= sx + 1
        before = moved(-1)
        for t in range(lane_tiles):
            here = moved(t)
            finish(
                t,
                jnp.where(own_near, here[0], before[0]),
                jnp.where(own_far, here[1], before[1]),
            )
            before = here

    @pl.when(sx < 0)
    def _():
        own_near, own_far = lane < sx + LANE, lane < sx + 1 + LANE
        here = moved(0)
        for t in range(lane_tiles):
            after = moved(t + 1)
            finish(
                t,
                jnp.where(own_near, here[0], after[0]),
                jnp.where(own_far, here[1], after[1]),
            )
            here = after


def velocity(sx_ref, sy_ref, fx_ref, fy_ref, v):
    return sx_ref[v].astype(F32) + fx_ref[v], sy_ref[v].astype(F32) + fy_ref[v]


def sum_moments(planes_ref, weights, lane_tile_range):
    sums = [[None] * 4 for _ in lane_tile_range]
    for v, (along_x, along_y) in enumerate(weights):
        square = along_x * along_x + along_y * along_y
        for n, t in enumerate(lane_tile_range):
            f = planes_ref[v, t]
            terms = (f, f * along_x, f * along_y, f * square)
            sums[n] = [b if a is None else a + b for a, b in zip(sums[n], terms)]
    return sums


def advance_kernel(tiles, raw_tiles, edges, meta_ref, sx_ref, sy_ref, fx_ref, fy_ref, inflow_ref,
                   wall_ref, heights_ref, pop_ref, *refs):
    if edges:
        mine_ref, theirs_ref, padded, planes_buf, moments, bars, sem_in, sem_out = refs
    else:
        planes_ref, mine_ref, theirs_ref, padded, planes_buf, moments, bars, sem_in, sem_out = refs
    planes, row_tiles, lane_tiles = pop_ref.shape[:3]
    half = lane_tiles // 2
    rows = row_tiles * ROW
    row0, first, last, core = (meta_ref[i] for i in range(4))
    loads = load_tiles(pop_ref, padded, raw_tiles, sem_in)
    prepare_heights(heights_ref, bars)

    def fill(v, _):
        value = inflow_ref[v]
        fill_rows(padded, v, (0, lane_tiles + 1), PAD, rows, value)
        if edges:
            columns = range(lane_tiles + 2)
            fill_rows(padded, v, columns, 0, PAD, jnp.where(first == 1, value, 0.0))
            fill_rows(padded, v, columns, PAD + rows, PAD, jnp.where(last == 1, value, 0.0))
        return 0

    lax.fori_loop(0, planes, fill, 0)
    for load in loads:
        load.wait()

    weights = [velocity(sx_ref, sy_ref, fx_ref, fy_ref, v) for v in range(planes)]

    def tile_planes(j, k, outside):
        def one(v, _):
            scalars = sx_ref[v], sy_ref[v], fx_ref[v], fy_ref[v]
            solid_value = jnp.where(outside, 0.0, wall_ref[v])
            advect_tile(padded, planes_buf.at[v, k], bars, v, j, row0 + ROW * j, scalars, solid_value)
            return 0

        lax.fori_loop(0, planes, one, 0)

    if not edges:
        count = len(tiles)

        def step(k, _):
            tile_planes(tiles[0] + k, k, False)
            for h in range(2):
                sums = sum_moments(planes_buf.at[:, k], weights, range(h * half, (h + 1) * half))
                slot = jnp.bitwise_xor(core, h)
                for t in range(half):
                    for m in range(4):
                        moments[slot, (k * 4 + m) * half + t] = sums[t][m]
            return 0

        lax.fori_loop(0, count, step, 0)
        copies = [
            pltpu.make_async_copy(planes_buf, planes_ref, sem_out.at[2]),
            pltpu.make_async_copy(moments.at[0], mine_ref, sem_out.at[0]),
            pltpu.make_async_copy(moments.at[1], theirs_ref, sem_out.at[1]),
        ]
    else:
        def step(k, _):
            j = jnp.where(k < 3, k - 1, row_tiles - 4 + k)
            tile_planes(j, 0, (j < 0) | (j >= row_tiles))
            for h in range(2):
                sums = sum_moments(planes_buf.at[:, 0], weights, range(h * half, (h + 1) * half))
                slot = jnp.bitwise_xor(core, h)

                @pl.when(k < 5)
                def _():
                    for t in range(half):
                        for m in range(4):
                            moments[slot, (k * 4 + m) * half + t] = sums[t][m]

                @pl.when(k == 5)
                def _():
                    for t in range(half):
                        for m in range(4):
                            moments[slot, 20 * half + m, t : t + 1, :] = sums[t][m][0:1, :]

            return 0

        lax.fori_loop(0, 6, step, 0)
        copies = [
            pltpu.make_async_copy(moments.at[0], mine_ref, sem_out.at[0]),
            pltpu.make_async_copy(moments.at[1], theirs_ref, sem_out.at[1]),
        ]
    for copy in copies:
        copy.start()
    for copy in copies:
        copy.wait()


def advance(tiles, edges, meta, small, heights, pop):
    planes, row_tiles, lane_tiles = pop.shape[:3]
    half = lane_tiles // 2
    if edges:
        raw_tiles = [0, 1, 2, row_tiles - 3, row_tiles - 2, row_tiles - 1]
        blocks = 20 * half + 4
        depth = 1
    else:
        raw_tiles = list(range(tiles[0] - 2, tiles[-1] + 2))
        blocks = len(tiles) * 4 * half
        depth = len(tiles)
    half_sums = jax.ShapeDtypeStruct((blocks, ROW, LANE), F32)
    out_shape = [half_sums, half_sums]
    if not edges:
        out_shape = [jax.ShapeDtypeStruct((planes, depth, lane_tiles, ROW, LANE), F32)] + out_shape
    return pl.pallas_call(
        functools.partial(advance_kernel, tiles, raw_tiles, edges),
        out_shape=out_shape,
        in_specs=[SMEM_SPEC] * 7 + [VMEM_SPEC, ANY_SPEC],
        out_specs=[ANY_SPEC] * len(out_shape),
        scratch_shapes=[
            pltpu.VMEM((planes, lane_tiles + 2, row_tiles * ROW + 2 * PAD, LANE), F32),
            pltpu.VMEM((planes, depth, lane_tiles, ROW, LANE), F32),
            pltpu.VMEM((2, blocks, ROW, LANE), F32),
            pltpu.VMEM((lane_tiles, ROW, LANE), jnp.int32),
            pltpu.SemaphoreType.DMA((len(raw_tiles),)),
            pltpu.SemaphoreType.DMA((3,)),
        ],
        compiler_params=params(),
        name="advance_edges" if edges else "advance_inside",
    )(meta, *small, heights, pop)


def join_kernel(edge_ref, low_ref, high_ref, out_ref):
    per_tile = high_ref.shape[0]
    half = per_tile // 4
    out_ref[0:per_tile] = edge_ref[0:per_tile] + low_ref[0:per_tile]
    out_ref[2 * per_tile :] = edge_ref[2 * per_tile :] + high_ref[...]
    top = lax.broadcasted_iota(jnp.int32, (ROW, LANE), 0) == 0
    for m in range(4):
        for t in range(half):
            n = per_tile + m * half + t
            row = jnp.broadcast_to(low_ref[per_tile + m, t : t + 1, :], (ROW, LANE))
            out_ref[n] = edge_ref[n] + jnp.where(top, row, 0.0)


def join(edge, from_low, from_high):
    return pl.pallas_call(
        join_kernel,
        out_shape=jax.ShapeDtypeStruct(edge.shape, F32),
        in_specs=[VMEM_SPEC] * 3,
        out_specs=VMEM_SPEC,
        compiler_params=params(),
        name="join_edges",
    )(edge, from_low, from_high)


def profile(density, flux_x, flux_y, energy, factor):
    inverse = 1.0 / density
    mean_x = flux_x * inverse
    mean_y = flux_y * inverse
    temperature = 0.5 * (energy * inverse - mean_x * mean_x - mean_y * mean_y)
    rate = 1.0 - jnp.exp(-factor * density / (SPEED_TALLY * jnp.sqrt(temperature)))
    height = rate * (density / (2.0 * math.pi * temperature))
    return mean_x, mean_y, -0.5 / temperature, height, 1.0 - rate


def relax_tile(get, put, sums, core, factor, weights, lane_tiles, k):
    half = lane_tiles // 2
    for t in range(lane_tiles):
        h, n = divmod(t, half)
        values = []
        for m in range(4):
            index = (k * 4 + m) * half + n
            own = sums[0][index] + sums[1][index]
            other = sums[2][index] + sums[3][index]
            values.append(jnp.where(core == h, own, other))
        mean_x, mean_y, scale, height, keep = profile(*values, factor)
        for v, (along_x, along_y) in enumerate(weights):
            gap_x = along_x - mean_x
            gap_y = along_y - mean_y
            state = height * jnp.exp((gap_x * gap_x + gap_y * gap_y) * scale)
            put(v, t, keep * get(v, t) + state)


def relax_kernel(meta_ref, sx_ref, sy_ref, fx_ref, fy_ref, factor_ref, planes_ref, s0, s1, s2, s3,
                 *refs):
    out_ref = refs[-1]
    planes, _, lane_tiles = planes_ref.shape[:3]
    weights = [velocity(sx_ref, sy_ref, fx_ref, fy_ref, v) for v in range(planes)]

    def put(v, t, value):
        out_ref[v, 0, t] = value

    relax_tile(
        lambda v, t: planes_ref[v, 0, t], put, (s0, s1, s2, s3), meta_ref[3], factor_ref[0], weights,
        lane_tiles, 0,
    )


def relax(meta, small, factor, after_move, sums, out, out_shape, first_tile):
    planes, count, lane_tiles = after_move.shape[:3]
    per_tile = 4 * lane_tiles // 2
    plane_block = (planes, 1, lane_tiles, ROW, LANE)
    operands = [meta, *small[:4], factor, after_move, *sums]
    in_specs = (
        [SMEM_SPEC] * 6
        + [pl.BlockSpec(plane_block, lambda k: (0, k, 0, 0, 0))]
        + [pl.BlockSpec((per_tile, ROW, LANE), lambda k: (k, 0, 0))] * 4
    )
    aliases = {}
    if out is not None:
        aliases = {len(operands): 0}
        operands.append(out)
        in_specs.append(ANY_SPEC)
    return pl.pallas_call(
        relax_kernel,
        grid=(count,),
        out_shape=out_shape,
        in_specs=in_specs,
        out_specs=pl.BlockSpec(plane_block, lambda k: (0, first_tile + k, 0, 0, 0)),
        input_output_aliases=aliases,
        compiler_params=params(),
        name="relax_inside",
    )(*operands)


def relax_edges_kernel(meta_ref, sx_ref, sy_ref, fx_ref, fy_ref, inflow_ref, wall_ref, factor_ref,
                       heights_ref, pop_ref, low_ref, high_ref, s0, s1, s2, s3, before_ref, out_ref,
                       padded, planes_buf, low_buf, high_buf, bars, sem_in, sem_out):
    planes, row_tiles, lane_tiles = pop_ref.shape[:3]
    rows = row_tiles * ROW
    row0, first, last, core = (meta_ref[i] for i in range(4))
    raw_tiles = [0, 1, 2, row_tiles - 3, row_tiles - 2, row_tiles - 1]
    loads = load_tiles(pop_ref, padded, raw_tiles, sem_in)
    for n, (source, buf) in enumerate(((low_ref, low_buf), (high_ref, high_buf))):
        target = buf.at[:, 16 : 16 + source.shape[1], :]
        loads.append(pltpu.make_async_copy(source, target, sem_in.at[len(raw_tiles) + n]))
        loads[-1].start()
    prepare_heights(heights_ref, bars)
    for load in loads:
        load.wait()

    def fill(v, offsets):
        low, high = offsets
        value = inflow_ref[v]
        shift = sy_ref[v]
        fill_rows(padded, v, (0, lane_tiles + 1), PAD - 16, rows + 24, value)

        @pl.when((shift >= 0) & (first == 1))
        def _():
            fill_rows(padded, v, range(1, lane_tiles + 1), PAD - 16, 16, value)

        @pl.when((shift < 0) & (last == 1))
        def _():
            fill_rows(padded, v, range(1, lane_tiles + 1), PAD + rows, 8, value)

        @pl.when((shift >= 0) & (first == 0))
        def _():
            for t in range(lane_tiles):
                for r in range(0, 16, ROW):
                    piece = low_buf[t, pl.ds(low + shift + 1 + r, ROW), :]
                    padded[v, t + 1, PAD - 16 + r : PAD - 16 + r + ROW, :] = piece

        @pl.when((shift < 0) & (last == 0))
        def _():
            for t in range(lane_tiles):
                padded[v, t + 1, PAD + rows : PAD + rows + ROW, :] = high_buf[
                    t, pl.ds(16 + high, ROW), :
                ]

        return low + low_need(shift), high + high_need(shift)

    lax.fori_loop(0, planes, fill, (jnp.int32(0), jnp.int32(0)))
    weights = [velocity(sx_ref, sy_ref, fx_ref, fy_ref, v) for v in range(planes)]

    def tile_of(k):
        return jnp.where(k < 2, k, row_tiles - 1)

    def step(k, _):
        j = tile_of(k)

        def one(v, _):
            scalars = sx_ref[v], sy_ref[v], fx_ref[v], fy_ref[v]
            advect_tile(padded, planes_buf.at[v, k], bars, v, j, row0 + ROW * j, scalars, wall_ref[v])
            return 0

        lax.fori_loop(0, planes, one, 0)

        def put(v, t, value):
            planes_buf[v, k, t] = value

        relax_tile(
            lambda v, t: planes_buf[v, k, t], put, (s0, s1, s2, s3), core, factor_ref[0], weights,
            lane_tiles, k,
        )
        return 0

    lax.fori_loop(0, 3, step, 0)
    copies = []
    for k in range(3):
        j = (0, 1, row_tiles - 1)[k]
        copies.append(pltpu.make_async_copy(planes_buf.at[:, k], out_ref.at[:, j], sem_out.at[k]))
        copies[-1].start()
    for copy in copies:
        copy.wait()


def relax_edges(meta, small, factor, heights, pop, low_rows, high_rows, sums, out):
    planes, row_tiles, lane_tiles = pop.shape[:3]
    operands = [meta, *small, factor, heights, pop, low_rows, high_rows, *sums, out]
    return pl.pallas_call(
        relax_edges_kernel,
        out_shape=jax.ShapeDtypeStruct(out.shape, F32),
        in_specs=[SMEM_SPEC] * 8 + [VMEM_SPEC] + [ANY_SPEC] * 3 + [VMEM_SPEC] * 4 + [ANY_SPEC],
        out_specs=ANY_SPEC,
        scratch_shapes=[
            pltpu.VMEM((planes, lane_tiles + 2, row_tiles * ROW + 2 * PAD, LANE), F32),
            pltpu.VMEM((planes, 3, lane_tiles, ROW, LANE), F32),
            pltpu.VMEM((lane_tiles, planes * LOW_ROWS + 32, LANE), F32),
            pltpu.VMEM((lane_tiles, planes * HIGH_ROWS + 32, LANE), F32),
            pltpu.VMEM((lane_tiles, ROW, LANE), jnp.int32),
            pltpu.SemaphoreType.DMA((8,)),
            pltpu.SemaphoreType.DMA((3,)),
        ],
        input_output_aliases={len(operands) - 1: 0},
        compiler_params=params(),
        name="relax_edges",
    )(*operands)


def per_device(populations, shift_x, shift_y, frac_x, frac_y, inflow, wall_state, heights,
               impact_frequency_factor):
    planes, row_count, col_count = populations.shape
    space_count, vel_count = lax.axis_size("space"), lax.axis_size("vel")
    row_tiles, lane_tiles = row_count // ROW, col_count // LANE
    half = lane_tiles // 2
    space, vel = lax.axis_index("space"), lax.axis_index("vel")
    forward = [(i, i + 1) for i in range(space_count - 1)]
    backward = [(target, source) for source, target in forward]
    partner = [(i, i ^ 1) for i in range(vel_count)]
    across = [(i, i ^ 2) for i in range(vel_count)]

    meta = jnp.stack(
        [space * row_count, space == 0, space == space_count - 1, vel % 2]
    ).astype(jnp.int32)
    small = (shift_x, shift_y, frac_x, frac_y, inflow, wall_state)
    factor = impact_frequency_factor.reshape(1)
    bars = heights.reshape(lane_tiles, LANE)
    pop = populations.reshape(planes, row_tiles, ROW, lane_tiles, LANE).transpose(0, 1, 3, 2, 4)

    cuts = [(0, 0, planes * LOW_ROWS), (1, 0, planes * HIGH_ROWS)]
    low_out, high_out = pack_rows(shift_y, pop, cuts)
    low_rows = lax.ppermute(low_out, "space", forward)
    high_rows = lax.ppermute(high_out, "space", backward)

    def share(mine, theirs):
        return mine + lax.ppermute(theirs, "vel", partner)

    def total(sums):
        received = lax.ppermute(sums, "vel", across)
        return (
            sums,
            received,
            lax.ppermute(sums, "vel", partner),
            lax.ppermute(received, "vel", partner),
        )

    middle = row_tiles // 2
    chunks = [list(range(2, middle)), list(range(middle, row_tiles - 1))]
    moved, sums = [], []
    edge_sums = None
    for n, tiles in enumerate(chunks):
        planes_part, mine, theirs = advance(tiles, False, meta, small, bars, pop)
        moved.append(planes_part)
        sums.append(total(share(mine, theirs)))
        if n == 0:
            edge_sums = share(*advance([], True, meta, small, bars, pop))
    per_tile = 4 * half
    from_high = lax.ppermute(edge_sums[:per_tile], "space", backward)
    from_low = lax.ppermute(edge_sums[4 * per_tile :], "space", forward)
    edge_total = total(join(edge_sums[per_tile : 4 * per_tile], from_low, from_high))

    out_shape = jax.ShapeDtypeStruct(pop.shape, F32)
    out = None
    for tiles, planes_part, parts in zip(chunks, moved, sums):
        out = relax(meta, small, factor, planes_part, parts, out, out_shape, tiles[0])
    out = relax_edges(meta, small, factor, bars, pop, low_rows, high_rows, edge_total, out)
    return out.transpose(0, 1, 3, 2, 4).reshape(planes, row_count, col_count)


def solution(mesh):
    return jax.shard_map(
        per_device,
        mesh=mesh,
        in_specs=(
            P("vel", "space", None),
            P("vel"),
            P("vel"),
            P("vel"),
            P("vel"),
            P("vel"),
            P("vel"),
            P(),
            P(),
        ),
        out_specs=P("vel", "space", None),
        check_vma=False,
    )
```

time: 303 us -> 151 us (0.50)
  other arithmetic: 152 us -> 0.79 us
  Pallas kernels: 0 us -> 69.8 us
  waiting for transfers between devices: 101 us -> 52.6 us
  local copies, waits for them, and re-layouts: 27.6 us -> 2.14 us
  starting transfers between devices: 6.4 us -> 23.7 us
  between operations: 14.5 us -> 0.92 us
    add x3, other arithmetic: 77 us -> 0.14 us  [share(): return mine + lax.ppermute(theirs, 'vel', partner)]
    pallas_call x0 -> x8, Pallas kernels: none -> 69.8 us  [the longest x3 39.7 us: advance(): pl.pallas_call(functools.partial(advance_kernel, tiles, raw_tiles, edges)...]
    reduce_sum x1 -> x0, other arithmetic: 59.8 us -> none  [relax_cells(): term_energy = jnp.sum(flat * (wide_x * wide_x + wide_y * wide_y), 0)]
    psum x1 -> x0, waiting for transfers between devices: 51.4 us -> none  [relax_cells(): lax.psum((term_mass, term_x, term_y, term_energy), 'vel')]
    unnamed x59 -> x28, local copies, waits for them, and re-layouts: 18.7 us -> 1.35 us
    ppermute x2 -> x16, starting transfers between devices: 6.36 us -> 23.7 us  [the longest x3 6.37 us: total(): lax.ppermute(received, 'vel', partner)]
    select_n x2 -> x0, other arithmetic: 12 us -> none  [the longest x1 11.3 us: per_device(): rimmed = jnp.where(outside[None, :, None], inflow[:, None, None], rimmed)]
    add x1 -> x0, local copies, waits for them, and re-layouts: 8.25 us -> none  [relax_cells(): relaxed = flat + approach_weighting[None, :] * (maxwellian_state - flat)]
  transfers between devices with their start and end apart: 3 -> 16, of which waited for: 3 -> 4; matrix products, arithmetic and copies ran while one was open for 0% -> 1% of each run, Pallas kernels for 0% -> 24%
where the time goes in v1:
time: 151 us; the launch traced here: 150 us
  Pallas kernels  69.8 us (46%)
  waiting for transfers between devices  52.6 us (35%)
  starting transfers between devices  23.7 us (16%)
  local copies, waits for them, and re-layouts  2.14 us (1%)
    pallas_call x3, Pallas kernels, advance(): pl.pallas_call(functools.partial(advance_kernel, tiles, raw_tiles, edges)...  39.7 us
    ppermute x1, waiting for transfers between devices, per_device(): from_high = lax.ppermute(edge_sums[:per_tile], 'space', backward)  23.7 us
    ppermute x1, waiting for transfers between devices, per_device(): from_low = lax.ppermute(edge_sums[4 * per_tile:], 'space', forward)  21 us
    pallas_call x1, Pallas kernels, relax_edges(): pl.pallas_call(relax_edges_kernel, out_shape=jax.ShapeDtypeStruct(out.sha...  14.8 us
    pallas_call x2, Pallas kernels, relax(): pl.pallas_call(relax_kernel, grid=(count,), out_shape=out_shape, in_specs...  9.02 us
    ppermute x3, waiting for transfers between devices, total(): received = lax.ppermute(sums, 'vel', across)  7.87 us
    ppermute x3, starting transfers between devices, total(): lax.ppermute(received, 'vel', partner)  6.37 us
    pallas_call x1, Pallas kernels, pack_rows(): pl.pallas_call(functools.partial(pack_kernel, cuts), out_shape=[jax.Shape...  4.33 us
  transfers between devices with their start and end apart: 16, of which 4 were waited for; matrix products, arithmetic and copies ran while one was open for 1% of the time, Pallas kernels for 24%

profile of v1, /device:TPU:9, one launch (start us, length us, event | category | flops | bytes accessed | tf_op | source)
XLA Modules:
  0.0 149.9 jit_solution(10281116259935583474)
XLA Ops:
  0.0 0.7 pad_add_fusion.meta_ref
  0.7 18.3 %advance_edges.1 = (f32[164,8,128]{2,1,0:T(8,128)}, f32[164,8,128]{2,1,0:T(8,128)}) custom-call(s32[4]{0:T(128)} %pad_add_fusion.meta_ref, s32[16]{0:T(128)} %sx_ref.11, s32[16]{0:T(128)} %sy_ref.13, f32[16]{0:T(128)} %fx_ref.11, f32[16]{0:T(128)} %fy_ref.11, f32[16]{0:T(128)} %inflow_ref.7, f32[16]{0:T(128)} %wall_ref.7, s32[16,128]{1,0:T(8,128)} %bitcast.20, ...), custom_call_target="tpu_custom_call" | custom-call | tf_op jit(solution)/shard_map/advance_edges/pallas_call | solution.py:294
  19.0 0.7 collective-permute-start.2
  19.7 9.1 %advance_inside.3 = (f32[16,2,16,8,128]{4,3,2,1,0:T(8,128)}, f32[64,8,128]{2,1,0:T(8,128)}, f32[64,8,128]{2,1,0:T(8,128)}) custom-call(s32[4]{0:T(128)} %pad_add_fusion.meta_ref, s32[16]{0:T(128)} %sx_ref.11, s32[16]{0:T(128)} %sy_ref.13, f32[16]{0:T(128)} %fx_ref.11, f32[16]{0:T(128)} %fy_ref.11, f32[16]{0:T(128)} %inflow_ref.7, f32[16]{0:T(128)} %wall_ref.7, ...), custom_call_target="tpu_custom_call" | custom-call | tf_op jit(solution)/shard_map/advance_inside/pallas_call | solution.py:294
  28.8 0.0 copy-start.11
  28.8 0.0 copy-start.4
  28.8 0.1 collective-permute-start.12
  28.9 12.3 %advance_inside.2 = (f32[16,3,16,8,128]{4,3,2,1,0:T(8,128)}, f32[96,8,128]{2,1,0:T(8,128)}, f32[96,8,128]{2,1,0:T(8,128)}) custom-call(s32[4]{0:T(128)} %pad_add_fusion.meta_ref, s32[16]{0:T(128)} %sx_ref.11, s32[16]{0:T(128)} %sy_ref.13, f32[16]{0:T(128)} %fx_ref.11, f32[16]{0:T(128)} %fy_ref.11, f32[16]{0:T(128)} %inflow_ref.7, f32[16]{0:T(128)} %wall_ref.7, ...), custom_call_target="tpu_custom_call" | custom-call | tf_op jit(solution)/shard_map/advance_inside/pallas_call | solution.py:294
  41.1 0.0 copy-start.6
  41.1 0.4 collective-permute-start.8
  41.5 0.0 collective-permute-done.12
  41.5 0.0 copy-done.11
  41.6 0.0 copy-start.3
  41.6 1.4 collective-permute-start.13
  42.9 4.3 %pack_rows.1 = (f32[16,144,128]{2,1,0:T(8,128)}, f32[16,128,128]{2,1,0:T(8,128)}) custom-call(s32[16]{0:T(128)} %sy_ref.13, f32[16,8,16,8,128]{4,3,2,1,0:T(8,128)} %bitcast.18), custom_call_target="tpu_custom_call" | custom-call | tf_op jit(solution)/shard_map/pack_rows/pallas_call | solution.py:85
  47.3 3.1 %collective-permute-start = (f32[16,144,128]{2,1,0:T(8,128)}, f32[16,144,128]{2,1,0:T(8,128)S(1)}, u32[]{:S(2)}, u32[]{:S(2)}) collective-permute-start(f32[16,144,128]{2,1,0:T(8,128)} %get-tuple-element.15), channel_id=1, source_target_pairs={{0,4},{4,8},{8,12},{12,16},{16,20},{20,24},{24,28},{1,5},{5,9},{9,... | collective-permute-start | bytes 3538952 | tf_op jit(solution)/shard_map/ppermute | solution.py:532
  50.4 0.0 collective-permute-done.2
  50.4 0.0 copy-done.4
  50.4 0.1 add.14
  50.5 3.1 %collective-permute-start.4 = (f32[32,8,128]{2,1,0:T(8,128)S(1)}, f32[32,8,128]{2,1,0:T(8,128)S(1)}, u32[]{:S(2)}, u32[]{:S(2)}) collective-permute-start(f32[32,8,128]{2,1,0:T(8,128)S(1)} %slice.14), channel_id=1, source_target_pairs={{4,0},{8,4},{12,8},{16,12},{20,16},{24,20},{28,24},{5,1},{9,5},{13... | collective-permute-start | bytes 393224 | tf_op jit(solution)/shard_map/ppermute | solution.py:558
  53.6 2.2 %collective-permute-start.1 = (f32[16,128,128]{2,1,0:T(8,128)}, f32[16,128,128]{2,1,0:T(8,128)S(1)}, u32[]{:S(2)}, u32[]{:S(2)}) collective-permute-start(f32[16,128,128]{2,1,0:T(8,128)} %get-tuple-element.16), channel_id=1, source_target_pairs={{4,0},{8,4},{12,8},{16,12},{20,16},{24,20},{28,24},{5,1},{9,5},{13... | collective-permute-start | bytes 3145736 | tf_op jit(solution)/shard_map/ppermute | solution.py:533
  55.8 0.0 collective-permute-done.8
  55.8 1.3 collective-permute-start.14
  57.1 0.0 collective-permute-done.13.s1
  57.1 0.1 collective-permute-start.15
  57.2 23.7 %collective-permute-done.4.high_ref = f32[32,8,128]{2,1,0:T(8,128)S(1)} collective-permute-done((f32[32,8,128]{2,1,0:T(8,128)S(1)}, f32[32,8,128]{2,1,0:T(8,128)S(1)}, u32[]{:S(2)}, u32[]{:S(2)}) %collective-permute-start.4) | collective-permute-done | bytes 131104 | tf_op jit(solution)/shard_map/ppermute | solution.py:558
  81.0 1.9 %collective-permute-start.3 = (f32[36,8,128]{2,1,0:T(8,128)S(1)}, f32[36,8,128]{2,1,0:T(8,128)S(1)}, u32[]{:S(2)}, u32[]{:S(2)}) collective-permute-start(f32[36,8,128]{2,1,0:T(8,128)S(1)} %slice.13), channel_id=1, source_target_pairs={{0,4},{4,8},{8,12},{12,16},{16,20},{20,24},{24,28},{1,5},{5,9},{9,... | collective-permute-start | bytes 442376 | tf_op jit(solution)/shard_map/ppermute | solution.py:559
  82.9 0.0 copy-done.6
  83.0 0.0 copy-start
  83.0 21.0 %collective-permute-done.3.low_ref = f32[36,8,128]{2,1,0:T(8,128)S(1)} collective-permute-done((f32[36,8,128]{2,1,0:T(8,128)S(1)}, f32[36,8,128]{2,1,0:T(8,128)S(1)}, u32[]{:S(2)}, u32[]{:S(2)}) %collective-permute-start.3) | collective-permute-done | bytes 147488 | tf_op jit(solution)/shard_map/ppermute | solution.py:559
  103.9 0.1 collective-permute-start.9
  104.1 0.8 slice.12.edge_ref
  104.8 0.0 copy-done.13
  104.8 0.0 copy-done.12
  104.9 1.9 %join_edges.1.s0 = f32[96,8,128]{2,1,0:T(8,128)} custom-call(f32[96,8,128]{2,1,0:T(8,128)} %slice.12.edge_ref, f32[36,8,128]{2,1,0:T(8,128)} %copy-done.12, f32[32,8,128]{2,1,0:T(8,128)} %copy-done.13), custom_call_target="tpu_custom_call" | custom-call | tf_op jit(solution)/shard_map/join_edges/pallas_call | solution.py:326
  106.8 0.0 collective-permute-done.14.s2
  106.8 1.6 %collective-permute-start.10 = (f32[96,8,128]{2,1,0:T(8,128)S(1)}, f32[96,8,128]{2,1,0:T(8,128)S(1)}, u32[]{:S(2)}, u32[]{:S(2)}) collective-permute-start(f32[96,8,128]{2,1,0:T(8,128)S(1)} %add.15.s0), channel_id=1, source_target_pairs={{0,1},{1,0},{2,3},{3,2},{4,5},{5,4},{6,7},{7,6},{8,9},{9,8},{10,11... | collective-permute-start | bytes 1179656 | tf_op jit(solution)/shard_map/ppermute | solution.py:543
  108.4 0.0 copy-done.9
  108.4 0.0 collective-permute-done.15.s3
  108.4 1.4 collective-permute-start.5
  109.7 3.6 %collective-permute-done.9.s1 = f32[96,8,128]{2,1,0:T(8,128)} collective-permute-done((f32[96,8,128]{2,1,0:T(8,128)S(1)}, f32[96,8,128]{2,1,0:T(8,128)}, u32[]{:S(2)}, u32[]{:S(2)}) %collective-permute-start.9) | collective-permute-done | bytes 393248 | tf_op jit(solution)/shard_map/ppermute | solution.py:539
  113.4 4.0 %collective-permute-start.11 = (f32[96,8,128]{2,1,0:T(8,128)}, f32[96,8,128]{2,1,0:T(8,128)}, u32[]{:S(2)}, u32[]{:S(2)}) collective-permute-start(f32[96,8,128]{2,1,0:T(8,128)} %collective-permute-done.9.s1), channel_id=1, source_target_pairs={{0,1},{1,0},{2,3},{3,2},{4,5},{5,4},{6,7},{7,6},{8,9},{9,8},{10,11... | collective-permute-start | bytes 1179656 | tf_op jit(solution)/shard_map/ppermute | solution.py:544
  117.4 0.0 collective-permute-done.10.s2
  117.4 0.1 collective-permute-start.6
  117.4 4.2 %collective-permute-done.5.s1 = f32[96,8,128]{2,1,0:T(8,128)S(1)} collective-permute-done((f32[96,8,128]{2,1,0:T(8,128)}, f32[96,8,128]{2,1,0:T(8,128)S(1)}, u32[]{:S(2)}, u32[]{:S(2)}) %collective-permute-start.5) | collective-permute-done | bytes 393248 | tf_op jit(solution)/shard_map/ppermute | solution.py:539
  121.7 0.0 copy-done.10
  121.7 0.0 copy-done.7
  121.7 2.3 %collective-permute-start.7 = (f32[96,8,128]{2,1,0:T(8,128)S(1)}, f32[96,8,128]{2,1,0:T(8,128)}, u32[]{:S(2)}, u32[]{:S(2)}) collective-permute-start(f32[96,8,128]{2,1,0:T(8,128)S(1)} %collective-permute-done.5.s1), channel_id=1, source_target_pairs={{0,1},{1,0},{2,3},{3,2},{4,5},{5,4},{6,7},{7,6},{8,9},{9,8},{10,11... | collective-permute-start | bytes 1179656 | tf_op jit(solution)/shard_map/ppermute | solution.py:544
  124.6 0.0 copy-done.3
  124.6 0.0 copy-done.8
  124.6 3.5 %relax_inside.2.refs_0_ = f32[16,8,16,8,128]{4,3,2,1,0:T(8,128)} custom-call(s32[4]{0:T(128)} %pad_add_fusion.meta_ref, s32[16]{0:T(128)} %sx_ref.11, s32[16]{0:T(128)} %sy_ref.13, f32[16]{0:T(128)} %fx_ref.11, f32[16]{0:T(128)} %fy_ref.11, f32[1]{0:T(128)} %bitcast.12.factor_ref, f32[16,2,16,8,128]{4,3,2,1,0:T(8,128)} %get-tuple-element.22.planes_ref, ...), custom_call_target="tpu_custom_call" | custom-call | tf_op jit(solution)/shard_map/relax_inside/pallas_call | solution.py:394
  128.1 0.0 collective-permute-done.11.s3
  128.1 0.0 copy-done
  128.1 5.5 %relax_inside.3.before_ref = f32[16,8,16,8,128]{4,3,2,1,0:T(8,128)} custom-call(s32[4]{0:T(128)} %pad_add_fusion.meta_ref, s32[16]{0:T(128)} %sx_ref.11, s32[16]{0:T(128)} %sy_ref.13, f32[16]{0:T(128)} %fx_ref.11, f32[16]{0:T(128)} %fy_ref.11, f32[1]{0:T(128)} %bitcast.13.factor_ref, ...), custom_call_target="tpu_custom_call", output_to_operand_aliasing={{}: (11, {})} | custom-call | tf_op jit(solution)/shard_map/relax_inside/pallas_call | solution.py:394
  133.7 0.0 copy-done.5
  133.7 0.0 collective-permute-done.1.high_ref
  133.7 0.0 copy-start.2
  133.7 0.0 collective-permute-done.low_ref
  133.7 0.0 copy-start.1
  133.7 0.0 collective-permute-done.6.s2
  133.7 0.0 collective-permute-done.7.s3
  133.7 0.9 copy-done.2
  134.6 0.4 copy-done.1
  135.0 14.8 %relax_edges.1 = f32[16,8,16,8,128]{4,3,2,1,0:T(8,128)} custom-call(s32[4]{0:T(128)} %pad_add_fusion.meta_ref, s32[16]{0:T(128)} %sx_ref.11, s32[16]{0:T(128)} %sy_ref.13, f32[16]{0:T(128)} %fx_ref.11, f32[16]{0:T(128)} %fy_ref.11, f32[16]{0:T(128)} %inflow_ref.7, f32[16]{0:T(128)} %wall_ref.7, ...), custom_call_target="tpu_custom_call", output_to_operand_aliasing={{}: (16, {})} | custom-call | tf_op jit(solution)/shard_map/relax_edges/pallas_call | solution.py:490
  (11 shorter events, 0.1 us)
Async XLA Ops:
  19.0 31.4 %collective-permute-start.2 = (f32[164,8,128]{2,1,0:T(8,128)}, f32[164,8,128]{2,1,0:T(8,128)S(1)}, u32[]{:S(2)}, u32[]{:S(2)}) collective-permute-start(f32[164,8,128]{2,1,0:T(8,128)} %get-tuple-element.18), channel_id=1, source_target_pairs={{0,1},{1,0},{2,3},{3,2},{4,5},{5,4},{6,7},{7,6},{8,9},{9,8},{10,11... | collective-permute-start | bytes 2015240 | tf_op jit(solution)/shard_map/ppermute | solution.py:536
  28.8 12.8 %copy-start.11 = (f32[64,8,128]{2,1,0:T(8,128)S(1)}, f32[64,8,128]{2,1,0:T(8,128)}, u32[]{:S(2)}) copy-start(f32[64,8,128]{2,1,0:T(8,128)} %get-tuple-element.23) | copy-start | bytes 786436
  28.8 21.6 %copy-start.4 = (f32[164,8,128]{2,1,0:T(8,128)S(1)}, f32[164,8,128]{2,1,0:T(8,128)}, u32[]{:S(2)}) copy-start(f32[164,8,128]{2,1,0:T(8,128)} %get-tuple-element.17) | copy-start | bytes 2015236
  28.8 12.7 %collective-permute-start.12 = (f32[64,8,128]{2,1,0:T(8,128)}, f32[64,8,128]{2,1,0:T(8,128)S(1)}, u32[]{:S(2)}, u32[]{:S(2)}) collective-permute-start(f32[64,8,128]{2,1,0:T(8,128)} %get-tuple-element.24), channel_id=1, source_target_pairs={{0,1},{1,0},{2,3},{3,2},{4,5},{5,4},{6,7},{7,6},{8,9},{9,8},{10,11... | collective-permute-start | bytes 786440 | tf_op jit(solution)/shard_map/ppermute | solution.py:536
  41.1 41.8 %copy-start.6 = (f32[96,8,128]{2,1,0:T(8,128)S(1)}, f32[96,8,128]{2,1,0:T(8,128)}, u32[]{:S(2)}) copy-start(f32[96,8,128]{2,1,0:T(8,128)} %get-tuple-element.20) | copy-start | bytes 1179652
  41.1 14.6 %collective-permute-start.8 = (f32[96,8,128]{2,1,0:T(8,128)}, f32[96,8,128]{2,1,0:T(8,128)S(1)}, u32[]{:S(2)}, u32[]{:S(2)}) collective-permute-start(f32[96,8,128]{2,1,0:T(8,128)} %get-tuple-element.21), channel_id=1, source_target_pairs={{0,1},{1,0},{2,3},{3,2},{4,5},{5,4},{6,7},{7,6},{8,9},{9,8},{10,11... | collective-permute-start | bytes 1179656 | tf_op jit(solution)/shard_map/ppermute | solution.py:536
  41.6 83.0 %copy-start.3 = (f32[64,8,128]{2,1,0:T(8,128)}, f32[64,8,128]{2,1,0:T(8,128)S(1)}, u32[]{:S(2)}) copy-start(f32[64,8,128]{2,1,0:T(8,128)S(1)} %add.16.s0) | copy-start | bytes 786436
  41.6 15.5 %collective-permute-start.13 = (f32[64,8,128]{2,1,0:T(8,128)S(1)}, f32[64,8,128]{2,1,0:T(8,128)S(1)}, u32[]{:S(2)}, u32[]{:S(2)}) collective-permute-start(f32[64,8,128]{2,1,0:T(8,128)S(1)} %add.16.s0), channel_id=1, source_target_pairs={{0,2},{1,3},{2,0},{3,1},{4,6},{5,7},{6,4},{7,5},{8,10},{9,11},{10,... | collective-permute-start | bytes 786440 | tf_op jit(solution)/shard_map/ppermute | solution.py:539
  47.3 86.4 %collective-permute-start = (f32[16,144,128]{2,1,0:T(8,128)}, f32[16,144,128]{2,1,0:T(8,128)S(1)}, u32[]{:S(2)}, u32[]{:S(2)}) collective-permute-start(f32[16,144,128]{2,1,0:T(8,128)} %get-tuple-element.15), channel_id=1, source_target_pairs={{0,4},{4,8},{8,12},{12,16},{16,20},{20,24},{24,28},{1,5},{5,9},{9,... | collective-permute-start | bytes 3538952 | tf_op jit(solution)/shard_map/ppermute | solution.py:532
  50.5 30.5 %collective-permute-start.4 = (f32[32,8,128]{2,1,0:T(8,128)S(1)}, f32[32,8,128]{2,1,0:T(8,128)S(1)}, u32[]{:S(2)}, u32[]{:S(2)}) collective-permute-start(f32[32,8,128]{2,1,0:T(8,128)S(1)} %slice.14), channel_id=1, source_target_pairs={{4,0},{8,4},{12,8},{16,12},{20,16},{24,20},{28,24},{5,1},{9,5},{13... | collective-permute-start | bytes 393224 | tf_op jit(solution)/shard_map/ppermute | solution.py:558
  53.6 80.1 %collective-permute-start.1 = (f32[16,128,128]{2,1,0:T(8,128)}, f32[16,128,128]{2,1,0:T(8,128)S(1)}, u32[]{:S(2)}, u32[]{:S(2)}) collective-permute-start(f32[16,128,128]{2,1,0:T(8,128)} %get-tuple-element.16), channel_id=1, source_target_pairs={{4,0},{8,4},{12,8},{16,12},{20,16},{24,20},{28,24},{5,1},{9,5},{13... | collective-permute-start | bytes 3145736 | tf_op jit(solution)/shard_map/ppermute | solution.py:533
  55.8 51.0 %collective-permute-start.14 = (f32[64,8,128]{2,1,0:T(8,128)S(1)}, f32[64,8,128]{2,1,0:T(8,128)S(1)}, u32[]{:S(2)}, u32[]{:S(2)}) collective-permute-start(f32[64,8,128]{2,1,0:T(8,128)S(1)} %add.16.s0), channel_id=1, source_target_pairs={{0,1},{1,0},{2,3},{3,2},{4,5},{5,4},{6,7},{7,6},{8,9},{9,8},{10,11... | collective-permute-start | bytes 786440 | tf_op jit(solution)/shard_map/ppermute | solution.py:543
  57.1 67.5 %copy-start.8 = (f32[64,8,128]{2,1,0:T(8,128)}, f32[64,8,128]{2,1,0:T(8,128)S(1)}, u32[]{:S(2)}) copy-start(f32[64,8,128]{2,1,0:T(8,128)S(1)} %collective-permute-done.13.s1) | copy-start | bytes 786436
  57.1 51.2 %collective-permute-start.15 = (f32[64,8,128]{2,1,0:T(8,128)S(1)}, f32[64,8,128]{2,1,0:T(8,128)S(1)}, u32[]{:S(2)}, u32[]{:S(2)}) collective-permute-start(f32[64,8,128]{2,1,0:T(8,128)S(1)} %collective-permute-done.13.s1), channel_id=1, source_target_pairs={{0,1},{1,0},{2,3},{3,2},{4,5},{5,4},{6,7},{7,6},{8,9},{9,8},{10,11... | collective-permute-start | bytes 786440 | tf_op jit(solution)/shard_map/ppermute | solution.py:544
  81.0 23.9 %copy-start.13 = (f32[32,8,128]{2,1,0:T(8,128)}, f32[32,8,128]{2,1,0:T(8,128)S(1)}, u32[]{:S(2)}) copy-start(f32[32,8,128]{2,1,0:T(8,128)S(1)} %collective-permute-done.4.high_ref) | copy-start | bytes 393220
  81.0 22.9 %collective-permute-start.3 = (f32[36,8,128]{2,1,0:T(8,128)S(1)}, f32[36,8,128]{2,1,0:T(8,128)S(1)}, u32[]{:S(2)}, u32[]{:S(2)}) collective-permute-start(f32[36,8,128]{2,1,0:T(8,128)S(1)} %slice.13), channel_id=1, source_target_pairs={{0,4},{4,8},{8,12},{12,16},{16,20},{20,24},{24,28},{1,5},{5,9},{9,... | collective-permute-start | bytes 442376 | tf_op jit(solution)/shard_map/ppermute | solution.py:559
  83.0 45.2 %copy-start = (f32[96,8,128]{2,1,0:T(8,128)}, f32[96,8,128]{2,1,0:T(8,128)S(1)}, u32[]{:S(2)}) copy-start(f32[96,8,128]{2,1,0:T(8,128)S(1)} %add.15.s0) | copy-start | bytes 1179652
  103.9 0.9 copy-start.12
  103.9 9.4 %collective-permute-start.9 = (f32[96,8,128]{2,1,0:T(8,128)S(1)}, f32[96,8,128]{2,1,0:T(8,128)}, u32[]{:S(2)}, u32[]{:S(2)}) collective-permute-start(f32[96,8,128]{2,1,0:T(8,128)S(1)} %add.15.s0), channel_id=1, source_target_pairs={{0,2},{1,3},{2,0},{3,1},{4,6},{5,7},{6,4},{7,5},{8,10},{9,11},{10,... | collective-permute-start | bytes 1179656 | tf_op jit(solution)/shard_map/ppermute | solution.py:539
  106.8 1.6 %copy-start.9 = (f32[64,8,128]{2,1,0:T(8,128)}, f32[64,8,128]{2,1,0:T(8,128)S(1)}, u32[]{:S(2)}) copy-start(f32[64,8,128]{2,1,0:T(8,128)S(1)} %collective-permute-done.14.s2) | copy-start | bytes 786436
  106.8 10.6 %collective-permute-start.10 = (f32[96,8,128]{2,1,0:T(8,128)S(1)}, f32[96,8,128]{2,1,0:T(8,128)S(1)}, u32[]{:S(2)}, u32[]{:S(2)}) collective-permute-start(f32[96,8,128]{2,1,0:T(8,128)S(1)} %add.15.s0), channel_id=1, source_target_pairs={{0,1},{1,0},{2,3},{3,2},{4,5},{5,4},{6,7},{7,6},{8,9},{9,8},{10,11... | collective-permute-start | bytes 1179656 | tf_op jit(solution)/shard_map/ppermute | solution.py:543
  108.4 13.3 %copy-start.10 = (f32[64,8,128]{2,1,0:T(8,128)}, f32[64,8,128]{2,1,0:T(8,128)S(1)}, u32[]{:S(2)}) copy-start(f32[64,8,128]{2,1,0:T(8,128)S(1)} %collective-permute-done.15.s3) | copy-start | bytes 786436
  108.4 13.3 %collective-permute-start.5 = (f32[96,8,128]{2,1,0:T(8,128)}, f32[96,8,128]{2,1,0:T(8,128)S(1)}, u32[]{:S(2)}, u32[]{:S(2)}) collective-permute-start(f32[96,8,128]{2,1,0:T(8,128)} %join_edges.1.s0), channel_id=1, source_target_pairs={{0,2},{1,3},{2,0},{3,1},{4,6},{5,7},{6,4},{7,5},{8,10},{9,11},{10,... | collective-permute-start | bytes 1179656 | tf_op jit(solution)/shard_map/ppermute | solution.py:539
  113.4 14.7 %collective-permute-start.11 = (f32[96,8,128]{2,1,0:T(8,128)}, f32[96,8,128]{2,1,0:T(8,128)}, u32[]{:S(2)}, u32[]{:S(2)}) collective-permute-start(f32[96,8,128]{2,1,0:T(8,128)} %collective-permute-done.9.s1), channel_id=1, source_target_pairs={{0,1},{1,0},{2,3},{3,2},{4,5},{5,4},{6,7},{7,6},{8,9},{9,8},{10,11... | collective-permute-start | bytes 1179656 | tf_op jit(solution)/shard_map/ppermute | solution.py:544
  117.4 4.3 %copy-start.7 = (f32[96,8,128]{2,1,0:T(8,128)}, f32[96,8,128]{2,1,0:T(8,128)S(1)}, u32[]{:S(2)}) copy-start(f32[96,8,128]{2,1,0:T(8,128)S(1)} %collective-permute-done.10.s2) | copy-start | bytes 1179652
  117.4 16.3 %collective-permute-start.6 = (f32[96,8,128]{2,1,0:T(8,128)}, f32[96,8,128]{2,1,0:T(8,128)}, u32[]{:S(2)}, u32[]{:S(2)}) collective-permute-start(f32[96,8,128]{2,1,0:T(8,128)} %join_edges.1.s0), channel_id=1, source_target_pairs={{0,1},{1,0},{2,3},{3,2},{4,5},{5,4},{6,7},{7,6},{8,9},{9,8},{10,11... | collective-permute-start | bytes 1179656 | tf_op jit(solution)/shard_map/ppermute | solution.py:543
  121.7 12.0 %copy-start.5 = (f32[96,8,128]{2,1,0:T(8,128)}, f32[96,8,128]{2,1,0:T(8,128)S(1)}, u32[]{:S(2)}) copy-start(f32[96,8,128]{2,1,0:T(8,128)S(1)} %collective-permute-done.5.s1) | copy-start | bytes 1179652
  121.7 12.0 %collective-permute-start.7 = (f32[96,8,128]{2,1,0:T(8,128)S(1)}, f32[96,8,128]{2,1,0:T(8,128)}, u32[]{:S(2)}, u32[]{:S(2)}) collective-permute-start(f32[96,8,128]{2,1,0:T(8,128)S(1)} %collective-permute-done.5.s1), channel_id=1, source_target_pairs={{0,1},{1,0},{2,3},{3,2},{4,5},{5,4},{6,7},{7,6},{8,9},{9,8},{10,11... | collective-permute-start | bytes 1179656 | tf_op jit(solution)/shard_map/ppermute | solution.py:544
  133.7 1.0 copy-start.2
  133.7 1.3 copy-start.1

commit v2 on v0

v2 whole, which is shorter than its diff:
```python
import functools
import math

import jax
import jax.numpy as jnp
from jax import lax
from jax.experimental import pallas as pl
from jax.experimental.pallas import tpu as pltpu
from jax.sharding import PartitionSpec as P

SPEED_TALLY = 64
CFL = 8
LOW_ROWS = CFL + 1
HIGH_ROWS = CFL
ROW = 8
LANE = 128
PAD = 24
F32 = jnp.float32
LOW_SENT = 72
HIGH_SENT = 64

SMEM_SPEC = pl.BlockSpec(memory_space=pltpu.SMEM)
ANY_SPEC = pl.BlockSpec(memory_space=pl.ANY)
VMEM_SPEC = pl.BlockSpec(memory_space=pltpu.VMEM)


def params(mebibytes):
    return pltpu.CompilerParams(vmem_limit_bytes=mebibytes * 1024 * 1024)


def cost(us):
    return pl.CostEstimate(flops=0, bytes_accessed=int(us * 3.69e6), transcendentals=0)


def low_need(shift):
    return jnp.where(shift >= 0, shift + 1, 0)


def high_need(shift):
    return jnp.where(shift < 0, -shift, 0)


def fill_rows(padded, v, columns, start, count, value):
    block = jnp.full((ROW, LANE), value, F32)
    for t in columns:
        for r in range(start, start + count, ROW):
            padded[v, t, r : r + ROW, :] = block


def prepare_heights(heights_ref, bars):
    lane_tiles = heights_ref.shape[0]
    sublane = lax.broadcasted_iota(jnp.int32, (ROW, LANE), 0)
    for t in range(lane_tiles):
        bars[t] = jnp.broadcast_to(heights_ref[t : t + 1, :], (ROW, LANE)) - sublane


def advect(padded, v, scalars, tiles):
    sx, sy, fx, fy = scalars
    lane_tiles = padded.shape[1] - 2
    lane = lax.broadcasted_iota(jnp.int32, (ROW, LANE), 1)
    near_roll = jnp.where(sx < 0, sx + LANE, sx)
    far_roll = jnp.where(sx + 1 < 0, sx + 1 + LANE, sx + 1)

    def moved(start, t):
        nearer = padded[v, t + 1, pl.ds(start, ROW), :]
        further = padded[v, t + 1, pl.ds(start - 1, ROW), :]
        line = (1.0 - fy) * nearer + fy * further
        return pltpu.roll(line, near_roll, 1), pltpu.roll(line, far_roll, 1)

    def blend(put, t, near, far):
        put(t, (1.0 - fx) * near + fx * far)

    @pl.when(sx >= 0)
    def _():
        own_near, own_far = lane >= sx, lane >= sx + 1
        for begin, put in tiles:
            before = moved(begin - sy, -1)
            for t in range(lane_tiles):
                here = moved(begin - sy, t)
                near = jnp.where(own_near, here[0], before[0])
                blend(put, t, near, jnp.where(own_far, here[1], before[1]))
                before = here

    @pl.when(sx < 0)
    def _():
        own_near, own_far = lane < sx + LANE, lane < sx + 1 + LANE
        for begin, put in tiles:
            here = moved(begin - sy, 0)
            for t in range(lane_tiles):
                after = moved(begin - sy, t + 1)
                near = jnp.where(own_near, here[0], after[0])
                blend(put, t, near, jnp.where(own_far, here[1], after[1]))
                here = after


def store_masked(target, bars, first_row, solid_value):
    def put(t, value):
        target[t] = jnp.where(first_row < bars[t], solid_value, value)

    return put


def velocity(sx_ref, sy_ref, fx_ref, fy_ref, v):
    return sx_ref[v].astype(F32) + fx_ref[v], sy_ref[v].astype(F32) + fy_ref[v]


def sum_moments(planes_ref, k, weights, lane_tile_range):
    sums = [[None] * 4 for _ in lane_tile_range]
    for v, (along_x, along_y) in enumerate(weights):
        square = along_x * along_x + along_y * along_y
        for n, t in enumerate(lane_tile_range):
            f = planes_ref[v, k, t]
            terms = (f, f * along_x, f * along_y, f * square)
            sums[n] = [b if a is None else a + b for a, b in zip(sums[n], terms)]
    return sums


def tile_loads(pop_ref, padded, raw_tiles, sems, v):
    lane_tiles = pop_ref.shape[2]
    return [
        pltpu.make_async_copy(
            pop_ref.at[v, i],
            padded.at[v, 1 : 1 + lane_tiles, PAD + ROW * i : PAD + ROW * (i + 1), :],
            sems.at[v, n],
        )
        for n, i in enumerate(raw_tiles)
    ]


def start_loads(pop_ref, padded, raw_tiles, sems):
    def one(v, _):
        for load in tile_loads(pop_ref, padded, raw_tiles, sems, v):
            load.start()
        return 0

    lax.fori_loop(0, pop_ref.shape[0], one, 0)


def inside_kernel(tiles, raw_tiles, meta_ref, sx_ref, sy_ref, fx_ref, fy_ref, inflow_ref, wall_ref,
                  heights_ref, pop_ref, _, planes_ref, sums_ref, padded, planes_buf, moments, bars, sem_in,
                  sem_planes, sem_out):
    planes, row_tiles, lane_tiles = pop_ref.shape[:3]
    half = lane_tiles // 2
    count = len(tiles)
    row0 = meta_ref[0]
    start_loads(pop_ref, padded, raw_tiles, sem_in)
    prepare_heights(heights_ref, bars)

    def out_copy(v):
        return pltpu.make_async_copy(planes_buf.at[v], planes_ref.at[v], sem_planes.at[v])

    def one(v, _):
        fill_rows(padded, v, (0, lane_tiles + 1), PAD, row_tiles * ROW, inflow_ref[v])
        for load in tile_loads(pop_ref, padded, raw_tiles, sem_in, v):
            load.wait()
        scalars = sx_ref[v], sy_ref[v], fx_ref[v], fy_ref[v]
        work = [
            (PAD + ROW * j, store_masked(planes_buf.at[v, k], bars, row0 + ROW * j, wall_ref[v]))
            for k, j in enumerate(tiles)
        ]
        advect(padded, v, scalars, work)
        out_copy(v).start()
        return 0

    lax.fori_loop(0, planes, one, 0)
    weights = [velocity(sx_ref, sy_ref, fx_ref, fy_ref, v) for v in range(planes)]

    def step(k, _):
        for h in range(2):
            sums = sum_moments(planes_buf, k, weights, range(h * half, (h + 1) * half))
            for t in range(half):
                for m in range(4):
                    moments[((h * count + k) * 4 + m) * half + t] = sums[t][m]
        return 0

    lax.fori_loop(0, count, step, 0)
    copy = pltpu.make_async_copy(moments, sums_ref, sem_out.at[0])
    copy.start()

    def finish(v, _):
        out_copy(v).wait()
        return 0

    lax.fori_loop(0, planes, finish, 0)
    copy.wait()


def advance_inside(tiles, meta, small, heights, pop, after):
    planes, row_tiles, lane_tiles = pop.shape[:3]
    count = len(tiles)
    raw_tiles = list(range(tiles[0] - 2, tiles[-1] + 2))
    blocks = 4 * lane_tiles * count
    return pl.pallas_call(
        functools.partial(inside_kernel, tiles, raw_tiles),
        out_shape=[
            jax.ShapeDtypeStruct((planes, count, lane_tiles, ROW, LANE), F32),
            jax.ShapeDtypeStruct((blocks, ROW, LANE), F32),
        ],
        in_specs=[SMEM_SPEC] * 7 + [VMEM_SPEC, ANY_SPEC, ANY_SPEC],
        out_specs=[ANY_SPEC] * 2,
        scratch_shapes=[
            pltpu.VMEM((planes, lane_tiles + 2, row_tiles * ROW + 2 * PAD, LANE), F32),
            pltpu.VMEM((planes, count, lane_tiles, ROW, LANE), F32),
            pltpu.VMEM((blocks, ROW, LANE), F32),
            pltpu.VMEM((lane_tiles, ROW, LANE), jnp.int32),
            pltpu.SemaphoreType.DMA((planes, len(raw_tiles))),
            pltpu.SemaphoreType.DMA((planes,)),
            pltpu.SemaphoreType.DMA((1,)),
        ],
        compiler_params=params(58),
        cost_estimate=cost(6),
        name="advance_inside",
    )(meta, *small, heights, pop, after)


def edges_kernel(raw_tiles, cuts, meta_ref, sx_ref, sy_ref, fx_ref, fy_ref, inflow_ref, wall_ref,
                 heights_ref, pop_ref, *refs):
    planes_ref, mine_ref, theirs_ref = refs[:3]
    packs = refs[3 : 3 + len(cuts)]
    (padded, planes_buf, moments, bars, low_pack, high_pack, sem_in, sem_planes, sem_out) = refs[
        3 + len(cuts) :
    ]
    planes, row_tiles, lane_tiles = pop_ref.shape[:3]
    half = lane_tiles // 2
    rows = row_tiles * ROW
    row0, first, last, core = (meta_ref[i] for i in range(4))
    start_loads(pop_ref, padded, raw_tiles, sem_in)
    prepare_heights(heights_ref, bars)
    zero = jnp.zeros((ROW, LANE), F32)

    def out_copy(v):
        return pltpu.make_async_copy(planes_buf.at[v, 1:4], planes_ref.at[v], sem_planes.at[v])

    def one(v, offsets):
        low, high = offsets
        value = inflow_ref[v]
        shift = sy_ref[v]
        columns = range(lane_tiles + 2)
        fill_rows(padded, v, (0, lane_tiles + 1), PAD, rows, value)
        fill_rows(padded, v, columns, 0, PAD, jnp.where(first == 1, value, 0.0))
        fill_rows(padded, v, columns, PAD + rows, PAD, jnp.where(last == 1, value, 0.0))
        up = shift >= 0
        idle_slot = jnp.where(up, 0, 4)
        for t in range(lane_tiles):
            planes_buf[v, idle_slot, t] = zero
            planes_buf[v, 5, t] = zero
        for load in tile_loads(pop_ref, padded, raw_tiles, sem_in, v):
            load.wait()
        scalars = sx_ref[v], shift, fx_ref[v], fy_ref[v]

        def entry(j, slot, solid_value):
            first_row = row0 + ROW * j
            return PAD + ROW * j, store_masked(planes_buf.at[v, slot], bars, first_row, solid_value)

        wall = wall_ref[v]
        work = [
            entry(0, 1, wall),
            entry(1, 2, wall),
            entry(row_tiles - 1, 3, wall),
            entry(jnp.where(up, row_tiles, -1), 4 - idle_slot, 0.0),
        ]
        advect(padded, v, scalars, work)
        out_copy(v).start()

        @pl.when(shift == CFL)
        def _():
            advect(padded, v, scalars, [entry(row_tiles + 1, 5, 0.0)])
            for t in range(lane_tiles):
                low_pack[t, pl.ds(low + 8, 8), :] = padded[v, t + 1, PAD + rows - 1 : PAD + rows + 7, :]

        @pl.when(up)
        def _():
            for t in range(lane_tiles):
                source = pl.ds(PAD + rows - 1 - shift, 8)
                low_pack[t, pl.ds(low, 8), :] = padded[v, t + 1, source, :]

        @pl.when(jnp.logical_not(up))
        def _():
            for t in range(lane_tiles):
                high_pack[t, pl.ds(high, 8), :] = padded[v, t + 1, PAD : PAD + 8, :]

        return low + low_need(shift), high + high_need(shift)

    lax.fori_loop(0, planes, one, (jnp.int32(0), jnp.int32(0)))
    weights = [velocity(sx_ref, sy_ref, fx_ref, fy_ref, v) for v in range(planes)]

    def step(k, _):
        for h in range(2):
            sums = sum_moments(planes_buf, k, weights, range(h * half, (h + 1) * half))
            slot = jnp.bitwise_xor(core, h)
            for t in range(half):
                for m in range(4):
                    moments[slot, (k * 4 + m) * half + t] = sums[t][m]
        return 0

    lax.fori_loop(0, 5, step, 0)
    for h in range(2):
        sums = sum_moments(planes_buf, 5, weights, range(h * half, (h + 1) * half))
        slot = jnp.bitwise_xor(core, h)
        for t in range(half):
            for m in range(4):
                moments[slot, 20 * half + m, t : t + 1, :] = sums[t][m][0:1, :]
    copies = [
        pltpu.make_async_copy(moments.at[1], theirs_ref, sem_out.at[1]),
        pltpu.make_async_copy(moments.at[0], mine_ref, sem_out.at[0]),
    ]
    for n, (pack, begin, end) in enumerate(cuts):
        source = (low_pack, high_pack)[pack].at[:, begin:end, :]
        copies.append(pltpu.make_async_copy(source, packs[n], sem_out.at[2 + n]))
    for copy in copies:
        copy.start()

    def finish(v, _):
        out_copy(v).wait()
        return 0

    lax.fori_loop(0, planes, finish, 0)
    for copy in copies:
        copy.wait()


def advance_edges(meta, small, heights, pop, cuts):
    planes, row_tiles, lane_tiles = pop.shape[:3]
    half = lane_tiles // 2
    raw_tiles = [0, 1, 2, row_tiles - 3, row_tiles - 2, row_tiles - 1]
    blocks = 20 * half + 4
    half_sums = jax.ShapeDtypeStruct((blocks, ROW, LANE), F32)
    return pl.pallas_call(
        functools.partial(edges_kernel, raw_tiles, cuts),
        out_shape=[
            jax.ShapeDtypeStruct((planes, 3, lane_tiles, ROW, LANE), F32),
            half_sums,
            half_sums,
        ]
        + [jax.ShapeDtypeStruct((lane_tiles, end - begin, LANE), F32) for _, begin, end in cuts],
        in_specs=[SMEM_SPEC] * 7 + [VMEM_SPEC, ANY_SPEC],
        out_specs=[ANY_SPEC] * (3 + len(cuts)),
        scratch_shapes=[
            pltpu.VMEM((planes, lane_tiles + 2, row_tiles * ROW + 2 * PAD, LANE), F32),
            pltpu.VMEM((planes, 6, lane_tiles, ROW, LANE), F32),
            pltpu.VMEM((2, blocks, ROW, LANE), F32),
            pltpu.VMEM((lane_tiles, ROW, LANE), jnp.int32),
            pltpu.VMEM((lane_tiles, planes * LOW_ROWS + 16, LANE), F32),
            pltpu.VMEM((lane_tiles, planes * HIGH_ROWS + 16, LANE), F32),
            pltpu.SemaphoreType.DMA((planes, len(raw_tiles))),
            pltpu.SemaphoreType.DMA((planes,)),
            pltpu.SemaphoreType.DMA((2 + len(cuts),)),
        ],
        compiler_params=params(58),
        cost_estimate=cost(6),
        name="advance_edges",
    )(meta, *small, heights, pop)


def split_kernel(mine_ref, received_ref, down_ref, edge_ref, up_ref):
    begin = 0
    for ref in (down_ref, edge_ref, up_ref):
        n = ref.shape[0]
        ref[...] = mine_ref[begin : begin + n] + received_ref[begin : begin + n]
        begin += n


def split(mine, received, per_tile):
    sizes = per_tile, 3 * per_tile, per_tile + 4
    return pl.pallas_call(
        split_kernel,
        out_shape=[jax.ShapeDtypeStruct((n, ROW, LANE), F32) for n in sizes],
        in_specs=[VMEM_SPEC] * 2,
        out_specs=[VMEM_SPEC] * 3,
        compiler_params=params(4),
        cost_estimate=cost(1),
        name="split_edges",
    )(mine, received)


def join_kernel(edge_ref, low_ref, high_ref, out_ref):
    per_tile = high_ref.shape[0]
    half = per_tile // 4
    out_ref[0:per_tile] = edge_ref[0:per_tile] + low_ref[0:per_tile]
    out_ref[2 * per_tile :] = edge_ref[2 * per_tile :] + high_ref[...]
    top = lax.broadcasted_iota(jnp.int32, (ROW, LANE), 0) == 0
    for m in range(4):
        for t in range(half):
            n = per_tile + m * half + t
            row = jnp.broadcast_to(low_ref[per_tile + m, t : t + 1, :], (ROW, LANE))
            out_ref[n] = edge_ref[n] + jnp.where(top, row, 0.0)


def join(edge, from_low, from_high):
    return pl.pallas_call(
        join_kernel,
        out_shape=jax.ShapeDtypeStruct(edge.shape, F32),
        in_specs=[VMEM_SPEC] * 3,
        out_specs=VMEM_SPEC,
        compiler_params=params(4),
        cost_estimate=cost(1),
        name="join_edges",
    )(edge, from_low, from_high)


def profile(density, flux_x, flux_y, energy, factor):
    inverse = 1.0 / density
    mean_x = flux_x * inverse
    mean_y = flux_y * inverse
    temperature = 0.5 * (energy * inverse - mean_x * mean_x - mean_y * mean_y)
    rate = 1.0 - jnp.exp(-factor * density / (SPEED_TALLY * jnp.sqrt(temperature)))
    height = rate * (density / (2.0 * math.pi * temperature))
    return mean_x, mean_y, -0.5 / temperature, height, 1.0 - rate


def relax_cells(get, put, values, factor, weights):
    mean_x, mean_y, scale, height, keep = profile(*values, factor)
    for v, (along_x, along_y) in enumerate(weights):
        gap_x = along_x - mean_x
        gap_y = along_y - mean_y
        state = height * jnp.exp((gap_x * gap_x + gap_y * gap_y) * scale)
        put(v, keep * get(v) + state)


def relax_kernel(meta_ref, sx_ref, sy_ref, fx_ref, fy_ref, factor_ref, planes_ref, own_ref, core_ref,
                 mine_ref, other_ref, out_ref):
    planes, _, half = planes_ref.shape[:3]
    weights = [velocity(sx_ref, sy_ref, fx_ref, fy_ref, v) for v in range(planes)]
    is_mine = meta_ref[3] == pl.program_id(1)
    for t in range(half):
        values = []
        for m in range(4):
            n = m * half + t
            far = jnp.where(is_mine, mine_ref[n], other_ref[n])
            values.append(own_ref[n] + core_ref[n] + far)

        def put(v, value):
            out_ref[v, 0, t] = value

        relax_cells(lambda v: planes_ref[v, 0, t], put, values, factor_ref[0], weights)


def relax_inside(meta, small, factor, after_move, own, from_core, mine, other, out_shape, first_tile):
    planes, count, lane_tiles = after_move.shape[:3]
    half = lane_tiles // 2
    plane_block = (planes, 1, half, ROW, LANE)
    sums_block = (4 * half, ROW, LANE)
    return pl.pallas_call(
        relax_kernel,
        grid=(count, 2),
        out_shape=out_shape,
        in_specs=[SMEM_SPEC] * 6
        + [pl.BlockSpec(plane_block, lambda k, h: (0, k, h, 0, 0))]
        + [pl.BlockSpec(sums_block, lambda k, h: (h * count + k, 0, 0))] * 2
        + [pl.BlockSpec(sums_block, lambda k, h: (k, 0, 0))] * 2,
        out_specs=pl.BlockSpec(plane_block, lambda k, h: (0, first_tile + k, h, 0, 0)),
        compiler_params=params(58),
        cost_estimate=cost(6),
        name="relax_inside",
    )(meta, *small[:4], factor, after_move, own, from_core, mine, other)


def relax_edges_kernel(cuts, meta_ref, sx_ref, sy_ref, fx_ref, fy_ref, inflow_ref, factor_ref,
                       heights_ref, planes_ref, s0, s1, s2, s3, *refs):
    pack_refs = refs[: len(cuts)]
    (_, out_ref, frames, planes_buf, low_buf, high_buf, bars, sem_in, sem_planes, sem_out) = refs[
        len(cuts) :
    ]
    planes, _, lane_tiles = planes_ref.shape[:3]
    row_tiles = out_ref.shape[1]
    half = lane_tiles // 2
    row0, first, last, core = (meta_ref[i] for i in range(4))

    def in_copy(v):
        return pltpu.make_async_copy(planes_ref.at[v], planes_buf.at[v], sem_planes.at[v])

    loads = []
    for n, (pack, begin, end) in enumerate(cuts):
        target = (low_buf, high_buf)[pack].at[:, 16 + begin : 16 + end, :]
        loads.append(pltpu.make_async_copy(pack_refs[n], target, sem_in.at[n]))
        loads[-1].start()

    def begin_load(v, _):
        in_copy(v).start()
        return 0

    lax.fori_loop(0, planes, begin_load, 0)
    prepare_heights(heights_ref, bars)
    for load in loads:
        load.wait()

    def add_masked(target, first_row):
        def put(t, value):
            target[t] = target[t] + jnp.where(first_row < bars[t], 0.0, value)

        return put

    def one(v, offsets):
        low, high = offsets
        value = inflow_ref[v]
        shift = sy_ref[v]
        up = shift >= 0
        in_copy(v).wait()
        scalars = sx_ref[v], shift, fx_ref[v], fy_ref[v]
        borders = (0, lane_tiles + 1)
        columns = range(lane_tiles + 2)

        @pl.when(up & (first == 0))
        def _():
            fill_rows(frames, v, borders, 8, 16, value)
            fill_rows(frames, v, columns, 24, 16, 0.0)
            for t in range(lane_tiles):
                for r in range(0, 16, ROW):
                    piece = low_buf[t, pl.ds(low + shift + 1 + r, ROW), :]
                    frames[v, t + 1, 8 + r : 8 + r + ROW, :] = piece
            advect(frames, v, scalars, [(24, add_masked(planes_buf.at[v, 0], row0))])

            @pl.when(shift == CFL)
            def _():
                advect(frames, v, scalars, [(32, add_masked(planes_buf.at[v, 1], row0 + ROW))])

        @pl.when(jnp.logical_not(up) & (last == 0))
        def _():
            fill_rows(frames, v, borders, 32, 8, value)
            fill_rows(frames, v, columns, 16, 16, 0.0)
            for t in range(lane_tiles):
                frames[v, t + 1, 32:40, :] = high_buf[t, pl.ds(16 + high, ROW), :]
            first_row = row0 + ROW * (row_tiles - 1)
            advect(frames, v, scalars, [(24, add_masked(planes_buf.at[v, 2], first_row))])

        return low + low_need(shift), high + high_need(shift)

    lax.fori_loop(0, planes, one, (jnp.int32(0), jnp.int32(0)))
    weights = [velocity(sx_ref, sy_ref, fx_ref, fy_ref, v) for v in range(planes)]

    def out_copy(k, h):
        j = jnp.where(k < 2, k, row_tiles - 1)
        lanes = pl.ds(h * half, half)
        return pltpu.make_async_copy(
            planes_buf.at[:, k, lanes], out_ref.at[:, j, lanes], sem_out.at[2 * k + h]
        )

    def step(k, _):
        for h in range(2):
            for n in range(half):
                t = h * half + n
                values = []
                for m in range(4):
                    index = (k * 4 + m) * half + n
                    values.append(
                        jnp.where(core == h, s0[index] + s1[index], s2[index] + s3[index])
                    )

                def put(v, value):
                    planes_buf[v, k, t] = value

                relax_cells(lambda v: planes_buf[v, k, t], put, values, factor_ref[0], weights)
            out_copy(k, h).start()
        return 0

    lax.fori_loop(0, 3, step, 0)
    for k in range(3):
        for h in range(2):
            out_copy(k, h).wait()


def relax_edges(meta, small, factor, heights, planes_part, sums, packs, cuts, out):
    planes, _, lane_tiles = planes_part.shape[:3]
    operands = [meta, *small[:5], factor, heights, planes_part, *sums, *packs, out]
    return pl.pallas_call(
        functools.partial(relax_edges_kernel, cuts),
        out_shape=jax.ShapeDtypeStruct(out.shape, F32),
        in_specs=[SMEM_SPEC] * 7
        + [VMEM_SPEC, ANY_SPEC]
        + [VMEM_SPEC] * 4
        + [ANY_SPEC] * (len(cuts) + 1),
        out_specs=ANY_SPEC,
        scratch_shapes=[
            pltpu.VMEM((planes, lane_tiles + 2, 48, LANE), F32),
            pltpu.VMEM((planes, 3, lane_tiles, ROW, LANE), F32),
            pltpu.VMEM((lane_tiles, planes * LOW_ROWS + 32, LANE), F32),
            pltpu.VMEM((lane_tiles, planes * HIGH_ROWS + 32, LANE), F32),
            pltpu.VMEM((lane_tiles, ROW, LANE), jnp.int32),
            pltpu.SemaphoreType.DMA((len(cuts),)),
            pltpu.SemaphoreType.DMA((planes,)),
            pltpu.SemaphoreType.DMA((6,)),
        ],
        input_output_aliases={len(operands) - 1: 0},
        compiler_params=params(58),
        cost_estimate=cost(5),
        name="relax_edges",
    )(*operands)


def per_device(populations, shift_x, shift_y, frac_x, frac_y, inflow, wall_state, heights,
               impact_frequency_factor):
    planes, row_count, col_count = populations.shape
    space_count, vel_count = lax.axis_size("space"), lax.axis_size("vel")
    row_tiles, lane_tiles = row_count // ROW, col_count // LANE
    half = lane_tiles // 2
    space, vel = lax.axis_index("space"), lax.axis_index("vel")
    core = vel % 2
    forward = [(i, i + 1) for i in range(space_count - 1)]
    backward = [(target, source) for source, target in forward]
    partner = [(i, i ^ 1) for i in range(vel_count)]
    across = [(i, i ^ 2) for i in range(vel_count)]

    meta = jnp.stack([space * row_count, space == 0, space == space_count - 1, core]).astype(jnp.int32)
    small = (shift_x, shift_y, frac_x, frac_y, inflow, wall_state)
    factor = impact_frequency_factor.reshape(1)
    bars = heights.reshape(lane_tiles, LANE)
    pop = populations.reshape(planes, row_tiles, ROW, lane_tiles, LANE).transpose(0, 1, 3, 2, 4)
    low_sent, high_sent = min(LOW_SENT, planes * LOW_ROWS), min(HIGH_SENT, planes * HIGH_ROWS)
    cuts = [
        (0, 0, low_sent),
        (1, 0, high_sent),
        (0, low_sent, planes * LOW_ROWS),
        (1, high_sent, planes * HIGH_ROWS),
    ]

    edge_planes, mine, theirs, *packs = advance_edges(meta, small, bars, pop, cuts)
    received = lax.ppermute(theirs, "vel", partner)
    tiles = list(range(2, row_tiles - 1))
    inside_planes, own = advance_inside(tiles, meta, small, bars, pop, mine)
    from_core = lax.ppermute(own, "vel", partner)
    down, edge, up = split(mine, received, 4 * half)
    from_low = lax.ppermute(up, "space", forward)
    from_high = lax.ppermute(down, "space", backward)
    low_first = lax.ppermute(packs[0], "space", forward)
    high_first = lax.ppermute(packs[1], "space", backward)

    length = own.shape[0] // 2
    begin = core * length
    crossing = lax.dynamic_slice_in_dim(own, begin, length) + lax.dynamic_slice_in_dim(
        from_core, begin, length
    )
    inside_mine = lax.ppermute(crossing, "vel", across)
    inside_other = lax.ppermute(inside_mine, "vel", partner)

    edge_sum = join(edge, from_low, from_high)
    edge_mine = lax.ppermute(edge_sum, "vel", across)
    edge_core = lax.ppermute(edge_sum, "vel", partner)
    edge_other = lax.ppermute(edge_mine, "vel", partner)

    def send_more(rows, axis_pairs, needed):
        return lax.cond(needed, lambda x: lax.ppermute(x, "space", axis_pairs), lambda x: x, rows)

    low_more = send_more(packs[2], forward, jnp.sum(low_need(shift_y)) > low_sent)
    high_more = send_more(packs[3], backward, jnp.sum(high_need(shift_y)) > high_sent)

    out_shape = jax.ShapeDtypeStruct(pop.shape, F32)
    out = relax_inside(
        meta, small, factor, inside_planes, own, from_core, inside_mine, inside_other, out_shape, tiles[0]
    )
    edge_sums = edge_sum, edge_mine, edge_core, edge_other
    halo = low_first, high_first, low_more, high_more
    out = relax_edges(meta, small, factor, bars, edge_planes, edge_sums, halo, cuts, out)
    return out.transpose(0, 1, 3, 2, 4).reshape(planes, row_count, col_count)


def solution(mesh):
    return jax.shard_map(
        per_device,
        mesh=mesh,
        in_specs=(
            P("vel", "space", None),
            P("vel"),
            P("vel"),
            P("vel"),
            P("vel"),
            P("vel"),
            P("vel"),
            P(),
            P(),
        ),
        out_specs=P("vel", "space", None),
        check_vma=False,
    )
```

time: 303 us -> 84.1 us (0.28)
  other arithmetic: 152 us -> 2.86 us
  waiting for transfers between devices: 101 us -> 19.7 us
  Pallas kernels: 0 us -> 39.6 us
  local copies, waits for them, and re-layouts: 27.6 us -> 1.67 us
  between operations: 14.5 us -> 2.1 us
  starting transfers between devices: 6.4 us -> 17.7 us
    add x3 -> x1, other arithmetic: 77 us -> 1.6 us  [per_device(): lax.dynamic_slice_in_dim(own, begin, length)]
    reduce_sum x1, other arithmetic: 59.8 us -> 0.7 us  [per_device(): jnp.sum(high_need(shift_y)) > high_sent]
    psum x1 -> x0, waiting for transfers between devices: 51.4 us -> none  [relax_cells(): lax.psum((term_mass, term_x, term_y, term_energy), 'vel')]
    pallas_call x0 -> x6, Pallas kernels: none -> 39.6 us  [the longest x1 11.2 us: advance_edges(): pl.pallas_call(functools.partial(edges_kernel, raw_tiles, cuts), out_shap...]
    ppermute x2 -> x11, waiting for transfers between devices: 49.3 us -> 19.7 us  [the longest x1 8.81 us: per_device(): high_first = lax.ppermute(packs[1], 'space', backward)]
    unnamed x59 -> x18, local copies, waits for them, and re-layouts: 18.7 us -> 1.67 us
    select_n x2 -> x0, other arithmetic: 12 us -> none  [the longest x1 11.3 us: per_device(): rimmed = jnp.where(outside[None, :, None], inflow[:, None, None], rimmed)]
    ppermute x2 -> x11, starting transfers between devices: 6.36 us -> 17.7 us  [the longest x1 3.12 us: per_device(): from_low = lax.ppermute(up, 'space', forward)]
  transfers between devices with their start and end apart: 3 -> 11, of which waited for: 3 -> 4; matrix products, arithmetic and copies ran while one was open for 0% -> 3% of each run, Pallas kernels for 0% -> 12%
where the time goes in v2:
time: 84.1 us; the launch traced here: 83.6 us
  Pallas kernels  39.6 us (47%)
  waiting for transfers between devices  19.7 us (23%)
  starting transfers between devices  17.7 us (21%)
  other arithmetic  2.86 us (3%)
  between operations  2.1 us (2%)
  local copies, waits for them, and re-layouts  1.67 us (2%)
    pallas_call x1, Pallas kernels, advance_edges(): pl.pallas_call(functools.partial(edges_kernel, raw_tiles, cuts), out_shap...  11.2 us
    pallas_call x1, Pallas kernels, relax_inside(): pl.pallas_call(relax_kernel, grid=(count, 2), out_shape=out_shape, in_spe...  10.2 us
    pallas_call x1, Pallas kernels, advance_inside(): pl.pallas_call(functools.partial(inside_kernel, tiles, raw_tiles), out_sh...  10.1 us
    ppermute x1, waiting for transfers between devices, per_device(): high_first = lax.ppermute(packs[1], 'space', backward)  8.81 us
    pallas_call x1, Pallas kernels, relax_edges(): pl.pallas_call(functools.partial(relax_edges_kernel, cuts), out_shape=jax...  7.95 us
    ppermute x1, waiting for transfers between devices, per_device(): from_high = lax.ppermute(down, 'space', backward)  4.75 us
    ppermute x1, waiting for transfers between devices, per_device(): inside_mine = lax.ppermute(crossing, 'vel', across)  3.32 us
    ppermute x1, starting transfers between devices, per_device(): from_low = lax.ppermute(up, 'space', forward)  3.12 us
  transfers between devices with their start and end apart: 11, of which 4 were waited for; matrix products, arithmetic and copies ran while one was open for 3% of the time, Pallas kernels for 12%

profile of v2, /device:TPU:9, one launch (start us, length us, event | category | flops | bytes accessed | tf_op | source)
XLA Modules:
  0.0 83.6 jit_solution(3574279555748731738)
XLA Ops:
  0.0 0.6 pad_add_fusion.meta_ref
  0.6 11.2 %advance_edges.1 = (f32[16,3,16,8,128]{4,3,2,1,0:T(8,128)}, f32[164,8,128]{2,1,0:T(8,128)}, f32[164,8,128]{2,1,0:T(8,128)}, f32[16,72,128]{2,1,0:T(8,128)}, f32[...) custom-call(s32[4]{0:T(128)} %pad_add_fusion.meta_ref, s32[16]{0:T(128)} %sx_ref.7, s32[16]{0:T(128)} %sy_ref.7, ...), custom_call_target="tpu_custom_call" | custom-call | bytes 22140000 | tf_op jit(solution)/shard_map/advance_edges/pallas_call | solution.py:328
  11.8 0.0 copy-start
  11.8 10.1 %advance_inside.1 = (f32[16,5,16,8,128]{4,3,2,1,0:T(8,128)}, f32[320,8,128]{2,1,0:T(8,128)}) custom-call(s32[4]{0:T(128)} %pad_add_fusion.meta_ref, s32[16]{0:T(128)} %sx_ref.7, s32[16]{0:T(128)} %sy_ref.7, f32[16]{0:T(128)} %fx_ref.7, f32[16]{0:T(128)} %fy_ref.7, f32[16]{0:T(128)} %inflow_ref.5, f32[16]{0:T(128)} %wall_ref.3, s32[16,128]{1,0:T(8,128)} %bitcast.17, ...), custom_call_target="tpu_custom_call" | custom-call | bytes 22140000 | tf_op jit(solution)/shard_map/advance_inside/pallas_call | solution.py:193
  21.9 0.0 copy-start.8
  21.9 1.0 %collective-permute-start.10 = (f32[320,8,128]{2,1,0:T(8,128)}, f32[320,8,128]{2,1,0:T(8,128)S(1)}, u32[]{:S(2)}, u32[]{:S(2)}) collective-permute-start(f32[320,8,128]{2,1,0:T(8,128)} %get-tuple-element.38.own_ref), channel_id=1, source_target_pairs={{0,1},{1,0},{2,3},{3,2},{4,5},{5,4},{6,7},{7,6},{8,9},{9,8},{10,11... | collective-permute-start | bytes 3932168 | tf_op jit(solution)/shard_map/ppermute | solution.py:620
  22.9 0.1 collective-permute-start.2
  22.9 2.8 %collective-permute-done.10.core_ref = f32[320,8,128]{2,1,0:T(8,128)S(1)} collective-permute-done((f32[320,8,128]{2,1,0:T(8,128)}, f32[320,8,128]{2,1,0:T(8,128)S(1)}, u32[]{:S(2)}, u32[]{:S(2)}) %collective-permute-start.10) | collective-permute-done | bytes 1310752 | tf_op jit(solution)/shard_map/ppermute | solution.py:620
  25.7 0.0 copy-start.2
  25.7 1.6 %dynamic-slice_add_fusion = f32[160,8,128]{2,1,0:T(8,128)S(1)} fusion(f32[320,8,128]{2,1,0:T(8,128)S(1)} %collective-permute-done.10.core_ref, s32[]{:T(128)S(6)} %select_n.21, f32[320,8,128]{2,1,0:T(8,128)} %get-tuple-element.38.own_ref), kind=kLoop, calls=%fused_computation | loop fusion | flops 163840 | bytes 1966084 | tf_op jit(solution)/shard_map/add | solution.py:629
  27.4 1.1 %collective-permute-start.11 = (f32[160,8,128]{2,1,0:T(8,128)S(1)}, f32[160,8,128]{2,1,0:T(8,128)S(1)}, u32[]{:S(2)}, u32[]{:S(2)}) collective-permute-start(f32[160,8,128]{2,1,0:T(8,128)S(1)} %dynamic-slice_add_fusion), channel_id=1, source_target_pairs={{0,2},{1,3},{2,0},{3,1},{4,6},{5,7},{6,4},{7,5},{8,10},{9,11},{10,... | collective-permute-start | bytes 1966088 | tf_op jit(solution)/shard_map/ppermute | solution.py:632
  28.4 0.0 collective-permute-done.2.received_ref
  28.4 0.0 copy-done
  28.4 0.1 split_edges.1
  28.5 3.1 %collective-permute-start.3 = (f32[36,8,128]{2,1,0:T(8,128)S(1)}, f32[36,8,128]{2,1,0:T(8,128)S(1)}, u32[]{:S(2)}, u32[]{:S(2)}) collective-permute-start(f32[36,8,128]{2,1,0:T(8,128)S(1)} %get-tuple-element.31), channel_id=1, source_target_pairs={{0,4},{4,8},{8,12},{12,16},{16,20},{20,24},{24,28},{1,5},{5,9},{9,... | collective-permute-start | bytes 442376 | tf_op jit(solution)/shard_map/ppermute | solution.py:622
  31.6 3.1 %collective-permute-start.4 = (f32[32,8,128]{2,1,0:T(8,128)S(1)}, f32[32,8,128]{2,1,0:T(8,128)S(1)}, u32[]{:S(2)}, u32[]{:S(2)}) collective-permute-start(f32[32,8,128]{2,1,0:T(8,128)S(1)} %get-tuple-element.32), channel_id=1, source_target_pairs={{4,0},{8,4},{12,8},{16,12},{20,16},{24,20},{28,24},{5,1},{9,5},{13... | collective-permute-start | bytes 393224 | tf_op jit(solution)/shard_map/ppermute | solution.py:623
  34.7 4.8 %collective-permute-done.4.high_ref = f32[32,8,128]{2,1,0:T(8,128)S(1)} collective-permute-done((f32[32,8,128]{2,1,0:T(8,128)S(1)}, f32[32,8,128]{2,1,0:T(8,128)S(1)}, u32[]{:S(2)}, u32[]{:S(2)}) %collective-permute-start.4) | collective-permute-done | bytes 131104 | tf_op jit(solution)/shard_map/ppermute | solution.py:623
  39.5 0.0 collective-permute-done.3.low_ref
  39.5 0.0 copy-start.1
  39.5 0.5 collective-permute-start.5
  40.0 3.3 %collective-permute-done.11.mine_ref = f32[160,8,128]{2,1,0:T(8,128)S(1)} collective-permute-done((f32[160,8,128]{2,1,0:T(8,128)S(1)}, f32[160,8,128]{2,1,0:T(8,128)S(1)}, u32[]{:S(2)}, u32[]{:S(2)}) %collective-permute-start.11) | collective-permute-done | bytes 655392 | tf_op jit(solution)/shard_map/ppermute | solution.py:632
  43.4 0.0 copy-start.3
  43.4 2.0 %collective-permute-start.12 = (f32[160,8,128]{2,1,0:T(8,128)S(1)}, f32[160,8,128]{2,1,0:T(8,128)S(1)}, u32[]{:S(2)}, u32[]{:S(2)}) collective-permute-start(f32[160,8,128]{2,1,0:T(8,128)S(1)} %collective-permute-done.11.mine_ref), channel_id=1, source_target_pairs={{0,1},{1,0},{2,3},{3,2},{4,5},{5,4},{6,7},{7,6},{8,9},{9,8},{10,11... | collective-permute-start | bytes 1966088 | tf_op jit(solution)/shard_map/ppermute | solution.py:633
  45.4 3.1 %collective-permute-start.8 = (f32[16,72,128]{2,1,0:T(8,128)}, f32[16,72,128]{2,1,0:T(8,128)}, u32[]{:S(2)}, u32[]{:S(2)}) collective-permute-start(f32[16,72,128]{2,1,0:T(8,128)} %get-tuple-element.33), channel_id=1, source_target_pairs={{0,4},{4,8},{8,12},{12,16},{16,20},{20,24},{24,28},{1,5},{5,9},{9,... | collective-permute-start | bytes 1769480 | tf_op jit(solution)/shard_map/ppermute | solution.py:624
  48.5 3.1 %collective-permute-start.9 = (f32[16,64,128]{2,1,0:T(8,128)}, f32[16,64,128]{2,1,0:T(8,128)S(1)}, u32[]{:S(2)}, u32[]{:S(2)}) collective-permute-start(f32[16,64,128]{2,1,0:T(8,128)} %get-tuple-element.34), channel_id=1, source_target_pairs={{4,0},{8,4},{12,8},{16,12},{20,16},{24,20},{28,24},{5,1},{9,5},{13... | collective-permute-start | bytes 1572872 | tf_op jit(solution)/shard_map/ppermute | solution.py:625
  51.6 0.0 copy-done.8
  51.6 0.7 fusion.1
  53.6 0.0 copy-done.2
  53.6 0.6 collective-permute-start.6
  54.2 0.0 collective-permute-done.5.s1
  54.2 0.1 collective-permute-start.7
  55.0 0.0 collective-permute-done.12.other_ref
  55.0 0.0 copy-start.4
  55.0 0.0 copy-done.3
  55.0 0.8 %copy-done.4 = f32[160,8,128]{2,1,0:T(8,128)} copy-done((f32[160,8,128]{2,1,0:T(8,128)}, f32[160,8,128]{2,1,0:T(8,128)S(1)}, u32[]{:S(2)}) %copy-start.4) | copy-done | bytes 655384
  55.8 0.0 copy-start.5
  55.8 0.0 copy-start.6
  55.8 10.2 %relax_inside.1.refs_4_ = f32[16,8,16,8,128]{4,3,2,1,0:T(8,128)} custom-call(s32[4]{0:T(128)} %pad_add_fusion.meta_ref, s32[16]{0:T(128)} %sx_ref.7, s32[16]{0:T(128)} %sy_ref.7, f32[16]{0:T(128)} %fx_ref.7, f32[16]{0:T(128)} %fy_ref.7, f32[1]{0:T(128)} %bitcast.12.factor_ref, f32[16,5,16,8,128]{4,3,2,1,0:T(8,128)} %get-tuple-element.37.planes_ref, ...), custom_call_target="tpu_custom_call" | custom-call | bytes 22140000 | tf_op jit(solution)/shard_map/relax_inside/pallas_call | solution.py:443
  66.1 0.0 copy-done.1
  66.1 8.8 %collective-permute-done.9.refs_1_ = f32[16,64,128]{2,1,0:T(8,128)S(1)} collective-permute-done((f32[16,64,128]{2,1,0:T(8,128)}, f32[16,64,128]{2,1,0:T(8,128)S(1)}, u32[]{:S(2)}, u32[]{:S(2)}) %collective-permute-start.9) | collective-permute-done | bytes 524320 | tf_op jit(solution)/shard_map/ppermute | solution.py:625
  74.9 0.0 copy-start.7
  74.9 0.0 collective-permute-done.8.refs_0_
  74.9 0.0 collective-permute-done.6.s2
  74.9 0.0 collective-permute-done.7.s3
  74.9 0.8 copy-done.7
  75.7 0.0 copy-done.5
  75.7 0.0 copy-done.6
  75.7 8.0 %relax_edges.1 = f32[16,8,16,8,128]{4,3,2,1,0:T(8,128)} custom-call(s32[4]{0:T(128)} %pad_add_fusion.meta_ref, s32[16]{0:T(128)} %sx_ref.7, s32[16]{0:T(128)} %sy_ref.7, f32[16]{0:T(128)} %fx_ref.7, f32[16]{0:T(128)} %fy_ref.7, f32[16]{0:T(128)} %inflow_ref.5, f32[1]{0:T(128)} %bitcast.13.factor_ref, ...), custom_call_target="tpu_custom_call", output_to_operand_aliasing={{}: (17, {})} | custom-call | bytes 18450000 | tf_op jit(solution)/shard_map/relax_edges/pallas_call | solution.py:565
  (3 shorter events, 0.1 us)
Async XLA Ops:
  11.8 16.7 %copy-start = (f32[164,8,128]{2,1,0:T(8,128)S(1)}, f32[164,8,128]{2,1,0:T(8,128)}, u32[]{:S(2)}) copy-start(f32[164,8,128]{2,1,0:T(8,128)} %get-tuple-element.28.mine_ref._) | copy-start | bytes 2015236
  21.9 29.7 %copy-start.8 = (s32[16]{0:T(128)S(1)}, s32[16]{0:T(128)}, u32[]{:S(2)}) copy-start(s32[16]{0:T(128)} %sy_ref.7) | copy-start | bytes 196
  21.9 3.8 %collective-permute-start.10 = (f32[320,8,128]{2,1,0:T(8,128)}, f32[320,8,128]{2,1,0:T(8,128)S(1)}, u32[]{:S(2)}, u32[]{:S(2)}) collective-permute-start(f32[320,8,128]{2,1,0:T(8,128)} %get-tuple-element.38.own_ref), channel_id=1, source_target_pairs={{0,1},{1,0},{2,3},{3,2},{4,5},{5,4},{6,7},{7,6},{8,9},{9,8},{10,11... | collective-permute-start | bytes 3932168 | tf_op jit(solution)/shard_map/ppermute | solution.py:620
  22.9 5.6 %collective-permute-start.2 = (f32[164,8,128]{2,1,0:T(8,128)}, f32[164,8,128]{2,1,0:T(8,128)S(1)}, u32[]{:S(2)}, u32[]{:S(2)}) collective-permute-start(f32[164,8,128]{2,1,0:T(8,128)} %get-tuple-element.29), channel_id=1, source_target_pairs={{0,1},{1,0},{2,3},{3,2},{4,5},{5,4},{6,7},{7,6},{8,9},{9,8},{10,11... | collective-permute-start | bytes 2015240 | tf_op jit(solution)/shard_map/ppermute | solution.py:617
  25.7 27.8 %copy-start.2 = (f32[320,8,128]{2,1,0:T(8,128)}, f32[320,8,128]{2,1,0:T(8,128)S(1)}, u32[]{:S(2)}) copy-start(f32[320,8,128]{2,1,0:T(8,128)S(1)} %collective-permute-done.10.core_ref) | copy-start | bytes 3932164
  27.4 16.0 %collective-permute-start.11 = (f32[160,8,128]{2,1,0:T(8,128)S(1)}, f32[160,8,128]{2,1,0:T(8,128)S(1)}, u32[]{:S(2)}, u32[]{:S(2)}) collective-permute-start(f32[160,8,128]{2,1,0:T(8,128)S(1)} %dynamic-slice_add_fusion), channel_id=1, source_target_pairs={{0,2},{1,3},{2,0},{3,1},{4,6},{5,7},{6,4},{7,5},{8,10},{9,11},{10,... | collective-permute-start | bytes 1966088 | tf_op jit(solution)/shard_map/ppermute | solution.py:632
  28.5 11.0 %collective-permute-start.3 = (f32[36,8,128]{2,1,0:T(8,128)S(1)}, f32[36,8,128]{2,1,0:T(8,128)S(1)}, u32[]{:S(2)}, u32[]{:S(2)}) collective-permute-start(f32[36,8,128]{2,1,0:T(8,128)S(1)} %get-tuple-element.31), channel_id=1, source_target_pairs={{0,4},{4,8},{8,12},{12,16},{16,20},{20,24},{24,28},{1,5},{5,9},{9,... | collective-permute-start | bytes 442376 | tf_op jit(solution)/shard_map/ppermute | solution.py:622
  31.6 7.8 %collective-permute-start.4 = (f32[32,8,128]{2,1,0:T(8,128)S(1)}, f32[32,8,128]{2,1,0:T(8,128)S(1)}, u32[]{:S(2)}, u32[]{:S(2)}) collective-permute-start(f32[32,8,128]{2,1,0:T(8,128)S(1)} %get-tuple-element.32), channel_id=1, source_target_pairs={{4,0},{8,4},{12,8},{16,12},{20,16},{24,20},{28,24},{5,1},{9,5},{13... | collective-permute-start | bytes 393224 | tf_op jit(solution)/shard_map/ppermute | solution.py:623
  39.5 26.5 %copy-start.1 = (f32[96,8,128]{2,1,0:T(8,128)}, f32[96,8,128]{2,1,0:T(8,128)S(1)}, u32[]{:S(2)}) copy-start(f32[96,8,128]{2,1,0:T(8,128)S(1)} %join_edges.1.s0) | copy-start | bytes 1179652
  39.5 14.7 %collective-permute-start.5 = (f32[96,8,128]{2,1,0:T(8,128)S(1)}, f32[96,8,128]{2,1,0:T(8,128)}, u32[]{:S(2)}, u32[]{:S(2)}) collective-permute-start(f32[96,8,128]{2,1,0:T(8,128)S(1)} %join_edges.1.s0), channel_id=1, source_target_pairs={{0,2},{1,3},{2,0},{3,1},{4,6},{5,7},{6,4},{7,5},{8,10},{9,11},{10,... | collective-permute-start | bytes 1179656 | tf_op jit(solution)/shard_map/ppermute | solution.py:636
  43.4 11.6 %copy-start.3 = (f32[160,8,128]{2,1,0:T(8,128)}, f32[160,8,128]{2,1,0:T(8,128)S(1)}, u32[]{:S(2)}) copy-start(f32[160,8,128]{2,1,0:T(8,128)S(1)} %collective-permute-done.11.mine_ref) | copy-start | bytes 1966084
  43.4 11.6 %collective-permute-start.12 = (f32[160,8,128]{2,1,0:T(8,128)S(1)}, f32[160,8,128]{2,1,0:T(8,128)S(1)}, u32[]{:S(2)}, u32[]{:S(2)}) collective-permute-start(f32[160,8,128]{2,1,0:T(8,128)S(1)} %collective-permute-done.11.mine_ref), channel_id=1, source_target_pairs={{0,1},{1,0},{2,3},{3,2},{4,5},{5,4},{6,7},{7,6},{8,9},{9,8},{10,11... | collective-permute-start | bytes 1966088 | tf_op jit(solution)/shard_map/ppermute | solution.py:633
  45.4 29.5 %collective-permute-start.8 = (f32[16,72,128]{2,1,0:T(8,128)}, f32[16,72,128]{2,1,0:T(8,128)}, u32[]{:S(2)}, u32[]{:S(2)}) collective-permute-start(f32[16,72,128]{2,1,0:T(8,128)} %get-tuple-element.33), channel_id=1, source_target_pairs={{0,4},{4,8},{8,12},{12,16},{16,20},{20,24},{24,28},{1,5},{5,9},{9,... | collective-permute-start | bytes 1769480 | tf_op jit(solution)/shard_map/ppermute | solution.py:624
  48.5 26.4 %collective-permute-start.9 = (f32[16,64,128]{2,1,0:T(8,128)}, f32[16,64,128]{2,1,0:T(8,128)S(1)}, u32[]{:S(2)}, u32[]{:S(2)}) collective-permute-start(f32[16,64,128]{2,1,0:T(8,128)} %get-tuple-element.34), channel_id=1, source_target_pairs={{4,0},{8,4},{12,8},{16,12},{20,16},{24,20},{28,24},{5,1},{9,5},{13... | collective-permute-start | bytes 1572872 | tf_op jit(solution)/shard_map/ppermute | solution.py:625
  53.6 21.3 %collective-permute-start.6 = (f32[96,8,128]{2,1,0:T(8,128)S(1)}, f32[96,8,128]{2,1,0:T(8,128)}, u32[]{:S(2)}, u32[]{:S(2)}) collective-permute-start(f32[96,8,128]{2,1,0:T(8,128)S(1)} %join_edges.1.s0), channel_id=1, source_target_pairs={{0,1},{1,0},{2,3},{3,2},{4,5},{5,4},{6,7},{7,6},{8,9},{9,8},{10,11... | collective-permute-start | bytes 1179656 | tf_op jit(solution)/shard_map/ppermute | solution.py:637
  54.2 20.7 %collective-permute-start.7 = (f32[96,8,128]{2,1,0:T(8,128)}, f32[96,8,128]{2,1,0:T(8,128)}, u32[]{:S(2)}, u32[]{:S(2)}) collective-permute-start(f32[96,8,128]{2,1,0:T(8,128)} %collective-permute-done.5.s1), channel_id=1, source_target_pairs={{0,1},{1,0},{2,3},{3,2},{4,5},{5,4},{6,7},{7,6},{8,9},{9,8},{10,11... | collective-permute-start | bytes 1179656 | tf_op jit(solution)/shard_map/ppermute | solution.py:638
  55.0 0.9 %copy-start.4 = (f32[160,8,128]{2,1,0:T(8,128)}, f32[160,8,128]{2,1,0:T(8,128)S(1)}, u32[]{:S(2)}) copy-start(f32[160,8,128]{2,1,0:T(8,128)S(1)} %collective-permute-done.12.other_ref) | copy-start | bytes 1966084
  55.8 19.8 %copy-start.5 = (f32[16,72,128]{2,1,0:T(8,128)S(1)}, f32[16,72,128]{2,1,0:T(8,128)}, u32[]{:S(2)}) copy-start(f32[16,72,128]{2,1,0:T(8,128)} %get-tuple-element.41.refs_2_) | copy-start | bytes 1769476
  55.8 19.9 %copy-start.6 = (f32[16,64,128]{2,1,0:T(8,128)S(1)}, f32[16,64,128]{2,1,0:T(8,128)}, u32[]{:S(2)}) copy-start(f32[16,64,128]{2,1,0:T(8,128)} %get-tuple-element.42.refs_3_) | copy-start | bytes 1572868
  74.9 0.8 copy-start.7

commit v3 on v2

v3 whole, which is shorter than its diff:
```python
import functools
import math

import jax
import jax.numpy as jnp
from jax import lax
from jax.experimental import pallas as pl
from jax.experimental.pallas import tpu as pltpu
from jax.sharding import PartitionSpec as P

SPEED_TALLY = 64
CFL = 8
LOW_ROWS = CFL + 1
HIGH_ROWS = CFL
ROW = 8
LANE = 128
PAD = 16
F32 = jnp.float32
LOW_SENT = 72
HIGH_SENT = 64

SMEM_SPEC = pl.BlockSpec(memory_space=pltpu.SMEM)
ANY_SPEC = pl.BlockSpec(memory_space=pl.ANY)
HBM_SPEC = pl.BlockSpec(memory_space=pltpu.HBM)
VMEM_SPEC = pl.BlockSpec(memory_space=pltpu.VMEM)


def params(mebibytes):
    return pltpu.CompilerParams(vmem_limit_bytes=mebibytes * 1024 * 1024)


def low_need(shift):
    return jnp.where(shift >= 0, shift + 1, 0)


def high_need(shift):
    return jnp.where(shift < 0, -shift, 0)


def fill_rows(padded, v, columns, start, count, value):
    block = jnp.full((ROW, LANE), value, F32)
    for t in columns:
        for r in range(start, start + count, ROW):
            padded[v, t, r : r + ROW, :] = block


def prepare_heights(heights_ref, bars):
    lane_tiles = heights_ref.shape[0]
    sublane = lax.broadcasted_iota(jnp.int32, (ROW, LANE), 0)
    for t in range(lane_tiles):
        bars[t] = jnp.broadcast_to(heights_ref[t : t + 1, :], (ROW, LANE)) - sublane


def advect(padded, v, scalars, tiles):
    sx, sy, fx, fy = scalars
    lane_tiles = padded.shape[1] - 2
    lane = lax.broadcasted_iota(jnp.int32, (ROW, LANE), 1)
    near_roll = jnp.where(sx < 0, sx + LANE, sx)
    far_roll = jnp.where(sx + 1 < 0, sx + 1 + LANE, sx + 1)

    def moved(start, t):
        nearer = padded[v, t + 1, pl.ds(start, ROW), :]
        further = padded[v, t + 1, pl.ds(start - 1, ROW), :]
        line = (1.0 - fy) * nearer + fy * further
        return pltpu.roll(line, near_roll, 1), pltpu.roll(line, far_roll, 1)

    def blend(put, t, near, far):
        put(t, (1.0 - fx) * near + fx * far)

    @pl.when(sx >= 0)
    def _():
        own_near, own_far = lane >= sx, lane >= sx + 1
        for begin, put in tiles:
            before = moved(begin - sy, -1)
            for t in range(lane_tiles):
                here = moved(begin - sy, t)
                near = jnp.where(own_near, here[0], before[0])
                blend(put, t, near, jnp.where(own_far, here[1], before[1]))
                before = here

    @pl.when(sx < 0)
    def _():
        own_near, own_far = lane < sx + LANE, lane < sx + 1 + LANE
        for begin, put in tiles:
            here = moved(begin - sy, 0)
            for t in range(lane_tiles):
                after = moved(begin - sy, t + 1)
                near = jnp.where(own_near, here[0], after[0])
                blend(put, t, near, jnp.where(own_far, here[1], after[1]))
                here = after


def store_masked(target, bars, first_row, solid_value):
    def put(t, value):
        target[t] = jnp.where(first_row < bars[t], solid_value, value)

    return put


def velocity(sx_ref, sy_ref, fx_ref, fy_ref, v):
    return sx_ref[v].astype(F32) + fx_ref[v], sy_ref[v].astype(F32) + fy_ref[v]


def sum_moments(planes_ref, k, weights, lane_tile_range):
    sums = [[None] * 4 for _ in lane_tile_range]
    for v, (along_x, along_y) in enumerate(weights):
        square = along_x * along_x + along_y * along_y
        for n, t in enumerate(lane_tile_range):
            f = planes_ref[v, k, t]
            terms = (f, f * along_x, f * along_y, f * square)
            sums[n] = [b if a is None else a + b for a, b in zip(sums[n], terms)]
    return sums


def outer_kernel(cuts, meta_ref, sx_ref, sy_ref, fx_ref, fy_ref, inflow_ref, heights_ref, pop_ref, *refs):
    up_ref, down_ref = refs[:2]
    packs = refs[2 : 2 + len(cuts)]
    frames, outer, up_sums, down_sums, low_pack, high_pack, bars, sem_in, sem_out = refs[2 + len(cuts) :]
    planes, row_tiles, lane_tiles = pop_ref.shape[:3]
    half = lane_tiles // 2
    row0 = meta_ref[0]

    def load(v, i, row, n):
        target = frames.at[v, 1 : 1 + lane_tiles, row : row + ROW, :]
        return pltpu.make_async_copy(pop_ref.at[v, i], target, sem_in.at[v, n])

    def start(v, _):
        up = sy_ref[v] >= 0

        @pl.when(up)
        def _():
            load(v, row_tiles - 2, 8, 0).start()
            load(v, row_tiles - 1, 16, 1).start()

        @pl.when(jnp.logical_not(up))
        def _():
            load(v, 0, 16, 0).start()

        return 0

    lax.fori_loop(0, planes, start, 0)
    prepare_heights(heights_ref, bars)
    row_blocks = 8 * half
    up_sums[row_blocks:] = jnp.zeros((8, ROW, LANE), F32)

    def one(v, offsets):
        low, high = offsets
        value = inflow_ref[v]
        shift = sy_ref[v]
        scalars = sx_ref[v], shift, fx_ref[v], fy_ref[v]
        borders = (0, lane_tiles + 1)
        columns = range(lane_tiles + 2)

        @pl.when(shift >= 0)
        def _():
            fill_rows(frames, v, borders, 8, 16, value)
            fill_rows(frames, v, columns, 24, 8, 0.0)
            load(v, row_tiles - 2, 8, 0).wait()
            load(v, row_tiles - 1, 16, 1).wait()
            for t in range(lane_tiles):
                low_pack[t, pl.ds(low, 8), :] = frames[v, t + 1, pl.ds(23 - shift, 8), :]

        @pl.when(shift < 0)
        def _():
            fill_rows(frames, v, borders, 16, 8, value)
            fill_rows(frames, v, columns, 8, 8, 0.0)
            load(v, 0, 16, 0).wait()
            for t in range(lane_tiles):
                high_pack[t, pl.ds(high, 8), :] = frames[v, t + 1, 16:24, :]

        first_row = row0 + jnp.where(shift >= 0, ROW * row_tiles, -ROW)
        begin = jnp.where(shift >= 0, 24, 8)
        advect(frames, v, scalars, [(begin, store_masked(outer.at[v], bars, first_row, 0.0))])

        @pl.when(shift == CFL)
        def _():
            along_x, along_y = velocity(sx_ref, sy_ref, fx_ref, fy_ref, v)
            factors = 1.0, along_x, along_y, along_x * along_x + along_y * along_y

            def put(t, value):
                row = jnp.where(row0 + ROW * (row_tiles + 1) < bars[t], 0.0, value)
                for m in range(4):
                    n, r = row_blocks + 2 * m + t // ROW, t % ROW
                    up_sums[n, r : r + 1, :] = up_sums[n, r : r + 1, :] + (row * factors[m])[0:1, :]

            advect(frames, v, scalars, [(32, put)])
            for t in range(lane_tiles):
                low_pack[t, pl.ds(low + 8, 1), :] = frames[v, t + 1, 23:24, :]

        return low + low_need(shift), high + high_need(shift)

    lax.fori_loop(0, planes, one, (jnp.int32(0), jnp.int32(0)))

    for h in range(2):
        for rising, sums_ref in ((True, up_sums), (False, down_sums)):
            for part in range(2):
                tiles = range(h * half + part * half // 2, h * half + (part + 1) * half // 2)
                sums = [[None] * 4 for _ in tiles]
                for v in range(planes):
                    along_x, along_y = velocity(sx_ref, sy_ref, fx_ref, fy_ref, v)
                    goes = jnp.where((sy_ref[v] >= 0) == rising, 1.0, 0.0)
                    square = (along_x * along_x + along_y * along_y) * goes
                    factors = goes, along_x * goes, along_y * goes, square
                    for n, t in enumerate(tiles):
                        f = outer[v, t]
                        terms = [f * w for w in factors]
                        sums[n] = [b if a is None else a + b for a, b in zip(sums[n], terms)]
                for n, t in enumerate(tiles):
                    for m in range(4):
                        sums_ref[(h * 4 + m) * half + t - h * half] = sums[n][m]
    copies = [
        pltpu.make_async_copy(up_sums, up_ref, sem_out.at[0]),
        pltpu.make_async_copy(down_sums, down_ref, sem_out.at[1]),
    ]
    for n, (pack, begin, end) in enumerate(cuts):
        source = (low_pack, high_pack)[pack].at[:, begin:end, :]
        copies.append(pltpu.make_async_copy(source, packs[n], sem_out.at[2 + n]))
    for copy in copies:
        copy.start()
    for copy in copies:
        copy.wait()


def outer_rows(meta, small, heights, pop, cuts):
    planes, row_tiles, lane_tiles = pop.shape[:3]
    blocks = 4 * lane_tiles
    return pl.pallas_call(
        functools.partial(outer_kernel, cuts),
        out_shape=[
            jax.ShapeDtypeStruct((blocks + 8, ROW, LANE), F32),
            jax.ShapeDtypeStruct((blocks, ROW, LANE), F32),
        ]
        + [jax.ShapeDtypeStruct((lane_tiles, end - begin, LANE), F32) for _, begin, end in cuts],
        in_specs=[SMEM_SPEC] * 6 + [VMEM_SPEC, HBM_SPEC],
        out_specs=[ANY_SPEC] * (2 + len(cuts)),
        scratch_shapes=[
            pltpu.VMEM((planes, lane_tiles + 2, 40, LANE), F32),
            pltpu.VMEM((planes, lane_tiles, ROW, LANE), F32),
            pltpu.VMEM((blocks + 8, ROW, LANE), F32),
            pltpu.VMEM((blocks, ROW, LANE), F32),
            pltpu.VMEM((lane_tiles, planes * LOW_ROWS + 16, LANE), F32),
            pltpu.VMEM((lane_tiles, planes * HIGH_ROWS + 16, LANE), F32),
            pltpu.VMEM((lane_tiles, ROW, LANE), jnp.int32),
            pltpu.SemaphoreType.DMA((planes, 2)),
            pltpu.SemaphoreType.DMA((2 + len(cuts),)),
        ],
        compiler_params=params(20),
        name="outer_rows",
    )(meta, *small[:5], heights, pop)


def advance_kernel(tiles, raw_tiles, edges, meta_ref, sx_ref, sy_ref, fx_ref, fy_ref, inflow_ref,
                   wall_ref, heights_ref, pop_ref, _, planes_ref, sums_ref, padded, bars, sem_in):
    planes, row_tiles, lane_tiles = pop_ref.shape[:3]
    half = lane_tiles // 2
    count = len(tiles)
    rows = row_tiles * ROW
    row0, first, last = (meta_ref[i] for i in range(3))

    def loads(v):
        return [
            pltpu.make_async_copy(
                pop_ref.at[v, i],
                padded.at[v, 1 : 1 + lane_tiles, PAD + ROW * i : PAD + ROW * (i + 1), :],
                sem_in.at[v, n],
            )
            for n, i in enumerate(raw_tiles)
        ]

    def start(v, _):
        for load in loads(v):
            load.start()
        return 0

    lax.fori_loop(0, planes, start, 0)
    prepare_heights(heights_ref, bars)

    def one(v, _):
        value = inflow_ref[v]
        for i in raw_tiles:
            fill_rows(padded, v, (0, lane_tiles + 1), PAD + ROW * i, ROW, value)
        if edges:
            columns = range(lane_tiles + 2)
            fill_rows(padded, v, columns, 0, PAD, jnp.where(first == 1, value, 0.0))
            fill_rows(padded, v, columns, PAD + rows, ROW, jnp.where(last == 1, value, 0.0))
        for load in loads(v):
            load.wait()
        scalars = sx_ref[v], sy_ref[v], fx_ref[v], fy_ref[v]
        work = [
            (PAD + ROW * j, store_masked(planes_ref.at[v, k], bars, row0 + ROW * j, wall_ref[v]))
            for k, j in enumerate(tiles)
        ]
        advect(padded, v, scalars, work)
        return 0

    lax.fori_loop(0, planes, one, 0)
    weights = [velocity(sx_ref, sy_ref, fx_ref, fy_ref, v) for v in range(planes)]

    def step(k, _):
        for h in range(2):
            sums = sum_moments(planes_ref, k, weights, range(h * half, (h + 1) * half))
            for t in range(half):
                for m in range(4):
                    sums_ref[((h * count + k) * 4 + m) * half + t] = sums[t][m]
        return 0

    lax.fori_loop(0, count, step, 0)


def advance(tiles, edges, meta, small, heights, pop, after):
    planes, row_tiles, lane_tiles = pop.shape[:3]
    count = len(tiles)
    raw_tiles = sorted({i for j in tiles for i in range(j - 2, j + 2) if 0 <= i < row_tiles})
    blocks = 4 * lane_tiles * count
    return pl.pallas_call(
        functools.partial(advance_kernel, tiles, raw_tiles, edges),
        out_shape=[
            pltpu.VMEM((planes, count, lane_tiles, ROW, LANE), F32),
            jax.ShapeDtypeStruct((blocks, ROW, LANE), F32),
        ],
        in_specs=[SMEM_SPEC] * 7 + [VMEM_SPEC, HBM_SPEC, ANY_SPEC],
        out_specs=[VMEM_SPEC] * 2,
        scratch_shapes=[
            pltpu.VMEM((planes, lane_tiles + 2, PAD + row_tiles * ROW + ROW, LANE), F32),
            pltpu.VMEM((lane_tiles, ROW, LANE), jnp.int32),
            pltpu.SemaphoreType.DMA((planes, len(raw_tiles))),
        ],
        compiler_params=params(20),
        name="advance_edges" if edges else "advance_inside",
    )(meta, *small, heights, pop, after)


def join_kernel(own_ref, low_ref, high_ref, out_ref):
    half = high_ref.shape[0] // 8
    size = 4 * half
    top = lax.broadcasted_iota(jnp.int32, (ROW, LANE), 0) == 0
    for h in range(2):
        base = h * 3 * size
        own = slice(base, base + size)
        out_ref[own] = own_ref[own] + low_ref[h * size : (h + 1) * size]
        own = slice(base + 2 * size, base + 3 * size)
        out_ref[own] = own_ref[own] + high_ref[h * size : (h + 1) * size]
        for m in range(4):
            for n in range(half):
                t = h * half + n
                row = low_ref[8 * half + 2 * m + t // ROW, t % ROW : t % ROW + 1, :]
                index = base + size + m * half + n
                part = jnp.where(top, jnp.broadcast_to(row, (ROW, LANE)), 0.0)
                out_ref[index] = own_ref[index] + part


def join(own, from_low, from_high):
    return pl.pallas_call(
        join_kernel,
        out_shape=jax.ShapeDtypeStruct(own.shape, F32),
        in_specs=[VMEM_SPEC] * 3,
        out_specs=VMEM_SPEC,
        compiler_params=params(8),
        name="join_edges",
    )(own, from_low, from_high)


def fold_kernel(meta_ref, own_ref, core_ref, out_ref):
    length = out_ref.shape[0]
    half = pl.ds(meta_ref[3] * length, length)
    out_ref[...] = own_ref[half] + core_ref[half]


def fold(meta, own, from_core):
    return pl.pallas_call(
        fold_kernel,
        out_shape=jax.ShapeDtypeStruct((own.shape[0] // 2, ROW, LANE), F32),
        in_specs=[SMEM_SPEC] + [VMEM_SPEC] * 2,
        out_specs=VMEM_SPEC,
        compiler_params=params(8),
        name="fold_half",
    )(meta, own, from_core)


def overflow_kernel(limits, sy_ref, *refs):
    low, high = low_need(sy_ref[0]), high_need(sy_ref[0])
    for v in range(1, sy_ref.shape[0]):
        low, high = low + low_need(sy_ref[v]), high + high_need(sy_ref[v])
    refs[-1][0] = jnp.where((low > limits[0]) | (high > limits[1]), 1, 0)


def overflow(shift_y, limits, after):
    return pl.pallas_call(
        functools.partial(overflow_kernel, limits),
        out_shape=jax.ShapeDtypeStruct((1,), jnp.int32),
        in_specs=[SMEM_SPEC] + [ANY_SPEC] * len(after),
        out_specs=SMEM_SPEC,
        compiler_params=params(8),
        name="overflow",
    )(shift_y, *after)[0]


def profile(density, flux_x, flux_y, energy, factor):
    inverse = 1.0 / density
    mean_x = flux_x * inverse
    mean_y = flux_y * inverse
    temperature = 0.5 * (energy * inverse - mean_x * mean_x - mean_y * mean_y)
    rate = 1.0 - jnp.exp(-factor * density / (SPEED_TALLY * jnp.sqrt(temperature)))
    height = rate * (density / (2.0 * math.pi * temperature))
    return mean_x, mean_y, -0.5 / temperature, height, 1.0 - rate


def relax_cells(get, put, values, factor, weights):
    mean_x, mean_y, scale, height, keep = profile(*values, factor)
    for v, (along_x, along_y) in enumerate(weights):
        gap_x = along_x - mean_x
        gap_y = along_y - mean_y
        state = height * jnp.exp((gap_x * gap_x + gap_y * gap_y) * scale)
        put(v, keep * get(v) + state)


def relax_tile(planes_ref, out_buf, sums, core, factor, weights, k, h, count):
    own_ref, core_ref, mine_ref, other_ref = sums
    half = planes_ref.shape[2] // 2
    for n in range(half):
        t = h * half + n
        values = []
        for m in range(4):
            near = ((h * count + k) * 4 + m) * half + n
            far = (k * 4 + m) * half + n
            across = jnp.where(core == h, mine_ref[far], other_ref[far])
            values.append(own_ref[near] + core_ref[near] + across)

        def put(v, value):
            out_buf[v, k, t] = value

        relax_cells(lambda v: planes_ref[v, k, t], put, values, factor, weights)


def relax_kernel(first_tile, meta_ref, sx_ref, sy_ref, fx_ref, fy_ref, factor_ref, planes_ref, s0, s1, s2,
                 s3, *refs):
    out_ref, out_buf, sem_out = refs[-3:]
    planes, count, lane_tiles = planes_ref.shape[:3]
    half = lane_tiles // 2
    weights = [velocity(sx_ref, sy_ref, fx_ref, fy_ref, v) for v in range(planes)]

    def out_copy(k, h):
        lanes = pl.ds(h * half, half)
        return pltpu.make_async_copy(
            out_buf.at[:, k, lanes], out_ref.at[:, first_tile + k, lanes], sem_out.at[2 * k + h]
        )

    def step(k, _):
        for h in range(2):
            relax_tile(
                planes_ref, out_buf, (s0, s1, s2, s3), meta_ref[3], factor_ref[0], weights, k, h, count
            )
            out_copy(k, h).start()
        return 0

    lax.fori_loop(0, count, step, 0)
    for k in range(count):
        for h in range(2):
            out_copy(k, h).wait()


def relax_inside(meta, small, factor, planes_part, sums, out, out_shape, first_tile):
    planes, count, lane_tiles = planes_part.shape[:3]
    planes_part = pltpu.with_memory_space_constraint(planes_part, pltpu.VMEM)
    operands = [meta, *small[:4], factor, planes_part, *sums]
    in_specs = [SMEM_SPEC] * 6 + [VMEM_SPEC] * 5
    aliases = {}
    if out is not None:
        aliases = {len(operands): 0}
        operands.append(out)
        in_specs.append(HBM_SPEC)
    return pl.pallas_call(
        functools.partial(relax_kernel, first_tile),
        out_shape=out_shape,
        in_specs=in_specs,
        out_specs=HBM_SPEC,
        scratch_shapes=[
            pltpu.VMEM((planes, count, lane_tiles, ROW, LANE), F32),
            pltpu.SemaphoreType.DMA((2 * count,)),
        ],
        input_output_aliases=aliases,
        compiler_params=params(20),
        name="relax_inside",
    )(*operands)


def relax_edges_kernel(cuts, meta_ref, sx_ref, sy_ref, fx_ref, fy_ref, inflow_ref, factor_ref,
                       heights_ref, planes_ref, s0, s1, s2, s3, *refs):
    pack_refs = refs[: len(cuts)]
    _, out_ref, frames, out_buf, low_buf, high_buf, bars, sem_in, sem_out = refs[len(cuts) :]
    planes, _, lane_tiles = planes_ref.shape[:3]
    row_tiles = out_ref.shape[1]
    half = lane_tiles // 2
    row0, first, last, core = (meta_ref[i] for i in range(4))
    needs = [low_need(sy_ref[0]), high_need(sy_ref[0])]
    for v in range(1, planes):
        needs = [needs[0] + low_need(sy_ref[v]), needs[1] + high_need(sy_ref[v])]

    def pack_copy(n):
        pack, begin, end = cuts[n]
        target = (low_buf, high_buf)[pack].at[:, 16 + begin : 16 + end, :]
        return pltpu.make_async_copy(pack_refs[n], target, sem_in.at[n])

    for n in range(len(cuts)):
        pl.when(needs[cuts[n][0]] > cuts[n][1])(lambda n=n: pack_copy(n).start())
    prepare_heights(heights_ref, bars)
    for n in range(len(cuts)):
        pl.when(needs[cuts[n][0]] > cuts[n][1])(lambda n=n: pack_copy(n).wait())

    def add_masked(v, k, first_row):
        def put(t, value):
            out_buf[v, k, t] = planes_ref[v, k, t] + jnp.where(first_row < bars[t], 0.0, value)

        return put

    def keep(v, k):
        for t in range(lane_tiles):
            out_buf[v, k, t] = planes_ref[v, k, t]

    def one(v, offsets):
        low, high = offsets
        value = inflow_ref[v]
        shift = sy_ref[v]
        up = shift >= 0
        scalars = sx_ref[v], shift, fx_ref[v], fy_ref[v]
        borders = (0, lane_tiles + 1)
        columns = range(lane_tiles + 2)
        from_low = up & (first == 0)
        from_high = jnp.logical_not(up) & (last == 0)
        reaches_second = from_low & (shift == CFL)

        @pl.when(from_low)
        def _():
            fill_rows(frames, v, borders, 8, 16, value)
            fill_rows(frames, v, columns, 24, 16, 0.0)
            for t in range(lane_tiles):
                for r in range(0, 16, ROW):
                    piece = low_buf[t, pl.ds(low + shift + 1 + r, ROW), :]
                    frames[v, t + 1, 8 + r : 8 + r + ROW, :] = piece
            advect(frames, v, scalars, [(24, add_masked(v, 0, row0))])

        @pl.when(from_high)
        def _():
            fill_rows(frames, v, borders, 32, 8, value)
            fill_rows(frames, v, columns, 16, 16, 0.0)
            for t in range(lane_tiles):
                frames[v, t + 1, 32:40, :] = high_buf[t, pl.ds(16 + high, ROW), :]
            first_row = row0 + ROW * (row_tiles - 1)
            advect(frames, v, scalars, [(24, add_masked(v, 2, first_row))])

        @pl.when(reaches_second)
        def _():
            advect(frames, v, scalars, [(32, add_masked(v, 1, row0 + ROW))])

        pl.when(jnp.logical_not(from_low))(lambda: keep(v, 0))
        pl.when(jnp.logical_not(reaches_second))(lambda: keep(v, 1))
        pl.when(jnp.logical_not(from_high))(lambda: keep(v, 2))
        return low + low_need(shift), high + high_need(shift)

    lax.fori_loop(0, planes, one, (jnp.int32(0), jnp.int32(0)))
    weights = [velocity(sx_ref, sy_ref, fx_ref, fy_ref, v) for v in range(planes)]

    def out_copy(k, h):
        j = jnp.where(k < 2, k, row_tiles - 1)
        lanes = pl.ds(h * half, half)
        return pltpu.make_async_copy(
            out_buf.at[:, k, lanes], out_ref.at[:, j, lanes], sem_out.at[2 * k + h]
        )

    def step(k, _):
        for h in range(2):
            relax_tile(out_buf, out_buf, (s0, s1, s2, s3), core, factor_ref[0], weights, k, h, 3)
            out_copy(k, h).start()
        return 0

    lax.fori_loop(0, 3, step, 0)
    for k in range(3):
        for h in range(2):
            out_copy(k, h).wait()


def relax_edges(meta, small, factor, heights, planes_part, sums, packs, cuts, out):
    planes, _, lane_tiles = planes_part.shape[:3]
    planes_part = pltpu.with_memory_space_constraint(planes_part, pltpu.VMEM)
    operands = [meta, *small[:5], factor, heights, planes_part, *sums, *packs, out]
    return pl.pallas_call(
        functools.partial(relax_edges_kernel, cuts),
        out_shape=jax.ShapeDtypeStruct(out.shape, F32),
        in_specs=[SMEM_SPEC] * 7
        + [VMEM_SPEC] * 6
        + [ANY_SPEC] * len(cuts)
        + [HBM_SPEC],
        out_specs=HBM_SPEC,
        scratch_shapes=[
            pltpu.VMEM((planes, lane_tiles + 2, 48, LANE), F32),
            pltpu.VMEM((planes, 3, lane_tiles, ROW, LANE), F32),
            pltpu.VMEM((lane_tiles, planes * LOW_ROWS + 32, LANE), F32),
            pltpu.VMEM((lane_tiles, planes * HIGH_ROWS + 32, LANE), F32),
            pltpu.VMEM((lane_tiles, ROW, LANE), jnp.int32),
            pltpu.SemaphoreType.DMA((len(cuts),)),
            pltpu.SemaphoreType.DMA((6,)),
        ],
        input_output_aliases={len(operands) - 1: 0},
        compiler_params=params(20),
        name="relax_edges",
    )(*operands)


def per_device(populations, shift_x, shift_y, frac_x, frac_y, inflow, wall_state, heights,
               impact_frequency_factor):
    planes, row_count, col_count = populations.shape
    space_count, vel_count = lax.axis_size("space"), lax.axis_size("vel")
    row_tiles, lane_tiles = row_count // ROW, col_count // LANE
    space, vel = lax.axis_index("space"), lax.axis_index("vel")
    forward = [(i, i + 1) for i in range(space_count - 1)]
    backward = [(target, source) for source, target in forward]
    partner = [(i, i ^ 1) for i in range(vel_count)]
    across = [(i, i ^ 2) for i in range(vel_count)]

    meta = jnp.stack([space * row_count, space == 0, space == space_count - 1, vel % 2]).astype(jnp.int32)
    small = (shift_x, shift_y, frac_x, frac_y, inflow, wall_state)
    factor = impact_frequency_factor.reshape(1)
    bars = heights.reshape(lane_tiles, LANE)
    pop = populations.reshape(planes, row_tiles, ROW, lane_tiles, LANE).transpose(0, 1, 3, 2, 4)
    pop = pltpu.with_memory_space_constraint(pop, pltpu.HBM)
    low_sent, high_sent = min(LOW_SENT, planes * LOW_ROWS), min(HIGH_SENT, planes * HIGH_ROWS)
    cuts = [
        (0, 0, low_sent),
        (1, 0, high_sent),
        (0, low_sent, planes * LOW_ROWS),
        (1, high_sent, planes * HIGH_ROWS),
    ]

    up, down, *packs = outer_rows(meta, small, bars, pop, cuts)
    from_low = lax.ppermute(up, "space", forward)
    from_high = lax.ppermute(down, "space", backward)
    low_first = lax.ppermute(packs[0], "space", forward)
    high_first = lax.ppermute(packs[1], "space", backward)

    def total(own):
        from_core = lax.ppermute(own, "vel", partner)
        mine = lax.ppermute(fold(meta, own, from_core), "vel", across)
        return own, from_core, mine, lax.ppermute(mine, "vel", partner)

    middle = row_tiles // 2
    chunks = [list(range(2, middle)), list(range(middle, row_tiles - 1))]
    parts = []
    after = up
    for tiles in chunks:
        planes_part, own = advance(tiles, False, meta, small, bars, pop, after)
        parts.append((tiles[0], planes_part, total(own)))
        after = own
    edge_planes, own = advance([0, 1, row_tiles - 1], True, meta, small, bars, pop, after)
    edge_sums = total(join(own, from_low, from_high))

    out_shape = jax.ShapeDtypeStruct(pop.shape, F32)
    out = None
    for first_tile, planes_part, sums in parts:
        out = relax_inside(meta, small, factor, planes_part, sums, out, out_shape, first_tile)
    needed = overflow(shift_y, (low_sent, high_sent), (low_first, high_first, edge_sums[3]))

    def send_more(low, high):
        return lax.ppermute(low, "space", forward), lax.ppermute(high, "space", backward)

    more = lax.cond(needed > 0, send_more, lambda low, high: (low, high), packs[2], packs[3])
    halo = low_first, high_first, *more
    out = relax_edges(meta, small, factor, bars, edge_planes, edge_sums, halo, cuts, out)
    return out.transpose(0, 1, 3, 2, 4).reshape(planes, row_count, col_count)


def solution(mesh):
    return jax.shard_map(
        per_device,
        mesh=mesh,
        in_specs=(
            P("vel", "space", None),
            P("vel"),
            P("vel"),
            P("vel"),
            P("vel"),
            P("vel"),
            P("vel"),
            P(),
            P(),
        ),
        out_specs=P("vel", "space", None),
        check_vma=False,
    )
```

time: 84.1 us -> 90.8 us (1.080)
  local copies, waits for them, and re-layouts: 1.67 us -> 11.8 us
  waiting for transfers between devices: 19.7 us -> 12.6 us
  starting transfers between devices: 17.7 us -> 20.9 us
  Pallas kernels: 39.6 us -> 42.5 us
  other arithmetic: 2.86 us -> 0.08 us
    unnamed x18 -> x48, local copies, waits for them, and re-layouts: 1.67 us -> 11.8 us
    ppermute x1, waiting for transfers between devices: 8.81 us -> 0.01 us  [per_device(): high_first = lax.ppermute(packs[1], 'space', backward)]
    ppermute x7 -> x9, waiting for transfers between devices: 6.13 us -> 12.6 us  [the longest x3 11.8 us: total(): mine = lax.ppermute(fold(meta, own, from_core), 'vel', across)]
    ppermute x1, waiting for transfers between devices: 4.75 us -> 0.01 us  [per_device(): from_high = lax.ppermute(down, 'space', backward)]
    pallas_call x5 -> x11, Pallas kernels: 31.6 us -> 35 us  [the longest x3 19 us: advance(): pl.pallas_call(functools.partial(advance_kernel, tiles, raw_tiles, edges)...]
    ppermute x7 -> x9, starting transfers between devices: 5.36 us -> 8.52 us  [the longest x3 3.45 us: total(): return (own, from_core, mine, lax.ppermute(mine, 'vel', partner))]
    add x1 -> x0, other arithmetic: 1.6 us -> none  [per_device(): lax.dynamic_slice_in_dim(own, begin, length)]
  transfers between devices with their start and end apart: 11 -> 13, of which waited for: 4 -> 4; matrix products, arithmetic and copies ran while one was open for 3% -> 0% of each run, Pallas kernels for 12% -> 31%
where the time goes in v3:
time: 90.8 us; the launch traced here: 89.5 us
  Pallas kernels  42.5 us (47%)
  starting transfers between devices  20.9 us (23%)
  waiting for transfers between devices  12.6 us (14%)
  local copies, waits for them, and re-layouts  11.8 us (13%)
  between operations  1.59 us (2%)
    pallas_call x3, Pallas kernels, advance(): pl.pallas_call(functools.partial(advance_kernel, tiles, raw_tiles, edges)...  19 us
    unnamed x48, local copies, waits for them, and re-layouts  11.8 us
    ppermute x3, waiting for transfers between devices, total(): mine = lax.ppermute(fold(meta, own, from_core), 'vel', across)  11.8 us
    pallas_call x1, Pallas kernels, relax_edges(): pl.pallas_call(functools.partial(relax_edges_kernel, cuts), out_shape=jax...  7.52 us
    pallas_call x2, Pallas kernels, relax_inside(): pl.pallas_call(functools.partial(relax_kernel, first_tile), out_shape=out...  6.67 us
    pallas_call x1, Pallas kernels, outer_rows(): pl.pallas_call(functools.partial(outer_kernel, cuts), out_shape=[jax.Shap...  6.38 us
    ppermute x1, starting transfers between devices, per_device(): high_first = lax.ppermute(packs[1], 'space', backward)  3.95 us
    ppermute x3, starting transfers between devices, total(): return (own, from_core, mine, lax.ppermute(mine, 'vel', partner))  3.45 us
  transfers between devices with their start and end apart: 13, of which 4 were waited for; matrix products, arithmetic and copies ran while one was open for 0% of the time, Pallas kernels for 31%

profile of v3, /device:TPU:9, one launch (start us, length us, event | category | flops | bytes accessed | tf_op | source)
XLA Modules:
  0.0 89.5 jit_solution(5979189163580506337)
XLA Ops:
  0.0 0.1 pad_add_fusion.meta_ref
  0.1 0.7 copy-done.10
  0.8 0.7 copy-done.12
  1.4 0.7 copy-done.14
  2.1 0.7 copy-done.16
  2.7 0.7 copy-done.18
  3.4 0.7 copy-done.20
  4.1 6.4 %outer_rows.1 = (f32[72,8,128]{2,1,0:T(8,128)S(1)}, f32[64,8,128]{2,1,0:T(8,128)S(1)}, f32[16,72,128]{2,1,0:T(8,128)}, f32[16,64,128]{2,1,0:T(8,128)}, f32[16,72,128]{2,1,0:T(8,128)}, /*index=5*/f32[16,64,128]{2,1,0:T(8,128)}) custom-call(s32[4]{0:T(128)S(1)} %pad_add_fusion.meta_ref, s32[16]{0:T(128)S(1)} %copy-done.14, s32[16]{0:T(128)S(1)} %copy-done.12, ...), custom_call_target="tpu_custom_call" | custom-call | tf_op jit(solution)/shard_map/outer_rows/pallas_call | solution.py:227
  10.4 3.1 %collective-permute-start.2 = (f32[72,8,128]{2,1,0:T(8,128)S(1)}, f32[72,8,128]{2,1,0:T(8,128)S(1)}, u32[]{:S(2)}, u32[]{:S(2)}) collective-permute-start(f32[72,8,128]{2,1,0:T(8,128)S(1)} %get-tuple-element.29._), channel_id=1, source_target_pairs={{0,4},{4,8},{8,12},{12,16},{16,20},{20,24},{24,28},{1,5},{5,9},{9,... | collective-permute-start | bytes 884744 | tf_op jit(solution)/shard_map/ppermute | solution.py:635
  13.6 3.1 %collective-permute-start.3 = (f32[64,8,128]{2,1,0:T(8,128)S(1)}, f32[64,8,128]{2,1,0:T(8,128)S(1)}, u32[]{:S(2)}, u32[]{:S(2)}) collective-permute-start(f32[64,8,128]{2,1,0:T(8,128)S(1)} %get-tuple-element.34), channel_id=1, source_target_pairs={{4,0},{8,4},{12,8},{16,12},{20,16},{24,20},{28,24},{5,1},{9,5},{13... | collective-permute-start | bytes 786440 | tf_op jit(solution)/shard_map/ppermute | solution.py:636
  16.6 0.0 copy-done.22
  16.7 5.6 %advance_inside.2 = (f32[16,2,16,8,128]{4,3,2,1,0:T(8,128)S(1)}, f32[128,8,128]{2,1,0:T(8,128)S(1)}) custom-call(s32[4]{0:T(128)S(1)} %pad_add_fusion.meta_ref, s32[16]{0:T(128)S(1)} %copy-done.14, s32[16]{0:T(128)S(1)} %copy-done.12, f32[16]{0:T(128)S(1)} %copy-done.16, f32[16]{0:T(128)S(1)} %copy-done.18, f32[16]{0:T(128)S(1)} %copy-done.20, ...), custom_call_target="tpu_custom_call" | custom-call | tf_op jit(solution)/shard_map/advance_inside/pallas_call | solution.py:315
  22.3 0.0 copy-start.6
  22.3 1.3 %copy-done.6 = f32[16,2,16,8,128]{4,3,2,1,0:T(8,128)} copy-done((f32[16,2,16,8,128]{4,3,2,1,0:T(8,128)}, f32[16,2,16,8,128]{4,3,2,1,0:T(8,128)S(1)}, u32[]{:S(2)}) %copy-start.6) | copy-done | bytes 2097176
  23.6 6.6 %advance_inside.3 = (f32[16,3,16,8,128]{4,3,2,1,0:T(8,128)S(1)}, f32[192,8,128]{2,1,0:T(8,128)S(1)}) custom-call(s32[4]{0:T(128)S(1)} %pad_add_fusion.meta_ref, s32[16]{0:T(128)S(1)} %copy-done.14, s32[16]{0:T(128)S(1)} %copy-done.12, f32[16]{0:T(128)S(1)} %copy-done.16, f32[16]{0:T(128)S(1)} %copy-done.18, f32[16]{0:T(128)S(1)} %copy-done.20, ...), custom_call_target="tpu_custom_call" | custom-call | tf_op jit(solution)/shard_map/advance_inside/pallas_call | solution.py:315
  30.2 0.0 copy-start.4
  30.2 1.7 %copy-done.4 = f32[16,3,16,8,128]{4,3,2,1,0:T(8,128)} copy-done((f32[16,3,16,8,128]{4,3,2,1,0:T(8,128)}, f32[16,3,16,8,128]{4,3,2,1,0:T(8,128)S(1)}, u32[]{:S(2)}) %copy-start.4) | copy-done | bytes 3145752
  31.9 1.3 %collective-permute-start.9 = (f32[192,8,128]{2,1,0:T(8,128)S(1)}, f32[192,8,128]{2,1,0:T(8,128)S(1)}, u32[]{:S(2)}, u32[]{:S(2)}) collective-permute-start(f32[192,8,128]{2,1,0:T(8,128)S(1)} %get-tuple-element.31._.own_ref.s0), channel_id=1, source_target_pairs={{0,1},{1,0},{2,3},{3,2},{4,5},{5,4},{6,7},{7,6},{8,9},{9,8},{10,11... | collective-permute-start | bytes 2359304 | tf_op jit(solution)/shard_map/ppermute | solution.py:641
  33.2 6.8 %advance_edges.1 = (f32[16,3,16,8,128]{4,3,2,1,0:T(8,128)S(1)}, f32[192,8,128]{2,1,0:T(8,128)S(1)}) custom-call(s32[4]{0:T(128)S(1)} %pad_add_fusion.meta_ref, s32[16]{0:T(128)S(1)} %copy-done.14, s32[16]{0:T(128)S(1)} %copy-done.12, f32[16]{0:T(128)S(1)} %copy-done.16, f32[16]{0:T(128)S(1)} %copy-done.18, f32[16]{0:T(128)S(1)} %copy-done.20, ...), custom_call_target="tpu_custom_call" | custom-call | tf_op jit(solution)/shard_map/advance_edges/pallas_call | solution.py:315
  40.0 0.0 copy-start.2
  40.1 0.0 collective-permute-done.3.high_ref
  40.1 0.0 collective-permute-done.2.low_ref
  40.1 0.1 join_edges.1.own_ref.s0
  40.2 0.1 collective-permute-start.4
  40.3 0.5 collective-permute-start.12
  40.7 0.0 collective-permute-done.9.core_ref.s1
  40.7 0.6 fold_half.4
  41.3 1.6 %collective-permute-start.10 = (f32[96,8,128]{2,1,0:T(8,128)S(1)}, f32[96,8,128]{2,1,0:T(8,128)}, u32[]{:S(2)}, u32[]{:S(2)}) collective-permute-start(f32[96,8,128]{2,1,0:T(8,128)S(1)} %fold_half.4), channel_id=1, source_target_pairs={{0,2},{1,3},{2,0},{3,1},{4,6},{5,7},{6,4},{7,5},{8,10},{9,11},{10,... | collective-permute-start | bytes 1179656 | tf_op jit(solution)/shard_map/ppermute | solution.py:642
  42.9 0.0 collective-permute-done.4.core_ref.s1
  42.9 0.6 fold_half.3
  43.5 1.2 %collective-permute-start.5 = (f32[96,8,128]{2,1,0:T(8,128)S(1)}, f32[96,8,128]{2,1,0:T(8,128)}, u32[]{:S(2)}, u32[]{:S(2)}) collective-permute-start(f32[96,8,128]{2,1,0:T(8,128)S(1)} %fold_half.3), channel_id=1, source_target_pairs={{0,2},{1,3},{2,0},{3,1},{4,6},{5,7},{6,4},{7,5},{8,10},{9,11},{10,... | collective-permute-start | bytes 1179656 | tf_op jit(solution)/shard_map/ppermute | solution.py:642
  44.6 2.2 %collective-permute-start.7 = (f32[16,72,128]{2,1,0:T(8,128)}, f32[16,72,128]{2,1,0:T(8,128)S(1)}, u32[]{:S(2)}, u32[]{:S(2)}) collective-permute-start(f32[16,72,128]{2,1,0:T(8,128)} %get-tuple-element.35), channel_id=1, source_target_pairs={{0,4},{4,8},{8,12},{12,16},{16,20},{20,24},{24,28},{1,5},{5,9},{9,... | collective-permute-start | bytes 1769480 | tf_op jit(solution)/shard_map/ppermute | solution.py:637
  46.9 0.0 collective-permute-done.12.core_ref.s1
  46.9 0.0 copy-done
  46.9 0.0 copy-start.8
  46.9 0.6 fold_half.5
  47.5 0.4 collective-permute-start.13
  47.9 0.0 copy-done.8
  47.9 4.0 %collective-permute-start.8 = (f32[16,64,128]{2,1,0:T(8,128)}, f32[16,64,128]{2,1,0:T(8,128)}, u32[]{:S(2)}, u32[]{:S(2)}) collective-permute-start(f32[16,64,128]{2,1,0:T(8,128)} %get-tuple-element.36), channel_id=1, source_target_pairs={{4,0},{8,4},{12,8},{16,12},{20,16},{24,20},{28,24},{5,1},{9,5},{13... | collective-permute-start | bytes 1572872 | tf_op jit(solution)/shard_map/ppermute | solution.py:638
  51.9 0.3 collective-permute-done.10.s2
  52.2 1.3 %collective-permute-start.11 = (f32[96,8,128]{2,1,0:T(8,128)}, f32[96,8,128]{2,1,0:T(8,128)}, u32[]{:S(2)}, u32[]{:S(2)}) collective-permute-start(f32[96,8,128]{2,1,0:T(8,128)} %collective-permute-done.10.s2), channel_id=1, source_target_pairs={{0,1},{1,0},{2,3},{3,2},{4,5},{5,4},{6,7},{7,6},{8,9},{9,8},{10,11... | collective-permute-start | bytes 1179656 | tf_op jit(solution)/shard_map/ppermute | solution.py:643
  53.5 7.1 %collective-permute-done.5.s2 = f32[96,8,128]{2,1,0:T(8,128)} collective-permute-done((f32[96,8,128]{2,1,0:T(8,128)S(1)}, f32[96,8,128]{2,1,0:T(8,128)}, u32[]{:S(2)}, u32[]{:S(2)}) %collective-permute-start.5) | collective-permute-done | bytes 393248 | tf_op jit(solution)/shard_map/ppermute | solution.py:642
  60.6 1.3 %collective-permute-start.6 = (f32[96,8,128]{2,1,0:T(8,128)}, f32[96,8,128]{2,1,0:T(8,128)}, u32[]{:S(2)}, u32[]{:S(2)}) collective-permute-start(f32[96,8,128]{2,1,0:T(8,128)} %collective-permute-done.5.s2), channel_id=1, source_target_pairs={{0,1},{1,0},{2,3},{3,2},{4,5},{5,4},{6,7},{7,6},{8,9},{9,8},{10,11... | collective-permute-start | bytes 1179656 | tf_op jit(solution)/shard_map/ppermute | solution.py:643
  61.9 4.3 %collective-permute-done.13.s2 = f32[64,8,128]{2,1,0:T(8,128)} collective-permute-done((f32[64,8,128]{2,1,0:T(8,128)S(1)}, f32[64,8,128]{2,1,0:T(8,128)}, u32[]{:S(2)}, u32[]{:S(2)}) %collective-permute-start.13) | collective-permute-done | bytes 262176 | tf_op jit(solution)/shard_map/ppermute | solution.py:642
  66.3 0.8 collective-permute-start.14
  67.8 0.0 copy-start.1
  67.8 0.0 copy-start.5
  67.8 0.8 collective-permute-done.14.s3
  68.6 0.0 copy-done.13
  68.6 0.0 copy-start.7
  68.6 1.9 %copy-done.7 = f32[16,2,16,8,128]{4,3,2,1,0:T(8,128)S(1)} copy-done((f32[16,2,16,8,128]{4,3,2,1,0:T(8,128)S(1)}, f32[16,2,16,8,128]{4,3,2,1,0:T(8,128)}, u32[]{:S(2)}) %copy-start.7) | copy-done | bytes 2097176
  70.5 1.0 %copy-done.9 = f32[128,8,128]{2,1,0:T(8,128)S(1)} copy-done((f32[128,8,128]{2,1,0:T(8,128)S(1)}, f32[128,8,128]{2,1,0:T(8,128)}, u32[]{:S(2)}) %copy-start.9) | copy-done | bytes 524312
  71.6 3.0 %relax_inside.2.refs_0_ = f32[16,8,16,8,128]{4,3,2,1,0:T(8,128)} custom-call(s32[4]{0:T(128)S(1)} %pad_add_fusion.meta_ref, s32[16]{0:T(128)S(1)} %copy-done.15, s32[16]{0:T(128)S(1)} %copy-done.13, f32[16]{0:T(128)S(1)} %copy-done.17, f32[16]{0:T(128)S(1)} %copy-done.19, f32[1]{0:T(128)} %bitcast.13.factor_ref, f32[16,2,16,8,128]{4,3,2,1,0:T(8,128)S(1)} %copy-done.7, ...), custom_call_target="tpu_custom_call" | custom-call | tf_op jit(solution)/shard_map/relax_inside/pallas_call | solution.py:472
  74.6 0.0 collective-permute-done.11.s3
  74.6 0.0 copy-start.11
  74.6 0.0 copy-start.21
  74.6 3.7 %relax_inside.3.refs_4_ = f32[16,8,16,8,128]{4,3,2,1,0:T(8,128)} custom-call(s32[4]{0:T(128)S(1)} %pad_add_fusion.meta_ref, s32[16]{0:T(128)S(1)} %copy-done.15, s32[16]{0:T(128)S(1)} %copy-done.13, f32[16]{0:T(128)S(1)} %copy-done.17, f32[16]{0:T(128)S(1)} %copy-done.19, f32[1]{0:T(128)} %bitcast.14.factor_ref, ...), custom_call_target="tpu_custom_call", output_to_operand_aliasing={{}: (11, {})} | custom-call | tf_op jit(solution)/shard_map/relax_inside/pallas_call | solution.py:472
  78.3 0.0 collective-permute-done.8.refs_1_
  78.3 0.0 collective-permute-done.7.refs_0_
  78.3 0.0 collective-permute-done.6.refs_2_.s3
  78.4 1.1 %overflow.1 = s32[1]{0:T(128)} custom-call(s32[16]{0:T(128)S(1)} %copy-done.13, f32[16,72,128]{2,1,0:T(8,128)S(1)} %collective-permute-done.7.refs_0_, f32[16,64,128]{2,1,0:T(8,128)} %collective-permute-done.8.refs_1_, f32[96,8,128]{2,1,0:T(8,128)} %collective-permute-done.6.refs_2_.s3), custom_call_target="tpu_custom_call" | custom-call | tf_op jit(solution)/shard_map/overflow/pallas_call | solution.py:388
  80.0 0.0 copy-done.23
  80.1 1.9 %copy-done.3 = f32[16,3,16,8,128]{4,3,2,1,0:T(8,128)S(1)} copy-done((f32[16,3,16,8,128]{4,3,2,1,0:T(8,128)S(1)}, f32[16,3,16,8,128]{4,3,2,1,0:T(8,128)}, u32[]{:S(2)}) %copy-start.3) | copy-done | bytes 3145752
  82.0 7.5 %relax_edges.1 = f32[16,8,16,8,128]{4,3,2,1,0:T(8,128)} custom-call(s32[4]{0:T(128)S(1)} %pad_add_fusion.meta_ref, s32[16]{0:T(128)S(1)} %copy-done.15, s32[16]{0:T(128)S(1)} %copy-done.13, f32[16]{0:T(128)S(1)} %copy-done.17, f32[16]{0:T(128)S(1)} %copy-done.19, f32[16]{0:T(128)S(1)} %copy-done.21, ...), custom_call_target="tpu_custom_call", output_to_operand_aliasing={{}: (17, {})} | custom-call | tf_op jit(solution)/shard_map/relax_edges/pallas_call | solution.py:586
  (24 shorter events, 0.0 us)
Async XLA Ops:
  0.0 16.6 %copy-start.22 = (f32[16]{0:T(128)S(1)}, f32[16]{0:T(128)}, u32[]{:S(2)}) copy-start(f32[16]{0:T(128)} %wall_ref.5) | copy-start | bytes 196
  0.1 0.7 copy-start.10
  0.8 0.7 copy-start.12
  1.4 0.7 copy-start.14
  2.1 0.7 copy-start.16
  2.7 0.7 copy-start.18
  3.4 0.7 copy-start.20
  10.4 29.6 %collective-permute-start.2 = (f32[72,8,128]{2,1,0:T(8,128)S(1)}, f32[72,8,128]{2,1,0:T(8,128)S(1)}, u32[]{:S(2)}, u32[]{:S(2)}) collective-permute-start(f32[72,8,128]{2,1,0:T(8,128)S(1)} %get-tuple-element.29._), channel_id=1, source_target_pairs={{0,4},{4,8},{8,12},{12,16},{16,20},{20,24},{24,28},{1,5},{5,9},{9,... | collective-permute-start | bytes 884744 | tf_op jit(solution)/shard_map/ppermute | solution.py:635
  13.6 26.5 %collective-permute-start.3 = (f32[64,8,128]{2,1,0:T(8,128)S(1)}, f32[64,8,128]{2,1,0:T(8,128)S(1)}, u32[]{:S(2)}, u32[]{:S(2)}) collective-permute-start(f32[64,8,128]{2,1,0:T(8,128)S(1)} %get-tuple-element.34), channel_id=1, source_target_pairs={{4,0},{8,4},{12,8},{16,12},{20,16},{24,20},{28,24},{5,1},{9,5},{13... | collective-permute-start | bytes 786440 | tf_op jit(solution)/shard_map/ppermute | solution.py:636
  22.3 1.3 %copy-start.6 = (f32[16,2,16,8,128]{4,3,2,1,0:T(8,128)}, f32[16,2,16,8,128]{4,3,2,1,0:T(8,128)S(1)}, u32[]{:S(2)}) copy-start(f32[16,2,16,8,128]{4,3,2,1,0:T(8,128)S(1)} %get-tuple-element.42.planes_ref) | copy-start | bytes 6291460
  30.2 1.7 %copy-start.4 = (f32[16,3,16,8,128]{4,3,2,1,0:T(8,128)}, f32[16,3,16,8,128]{4,3,2,1,0:T(8,128)S(1)}, u32[]{:S(2)}) copy-start(f32[16,3,16,8,128]{4,3,2,1,0:T(8,128)S(1)} %get-tuple-element.41.planes_ref) | copy-start | bytes 9437188
  31.9 36.7 %copy-start.13 = (s32[16]{0:T(128)S(1)}, s32[16]{0:T(128)}, u32[]{:S(2)}) copy-start(s32[16]{0:T(128)} %sy_ref.15) | copy-start | bytes 196
  31.9 36.7 %copy-start.15 = (s32[16]{0:T(128)S(1)}, s32[16]{0:T(128)}, u32[]{:S(2)}) copy-start(s32[16]{0:T(128)} %sx_ref.13) | copy-start | bytes 196
  31.9 36.7 %copy-start.17 = (f32[16]{0:T(128)S(1)}, f32[16]{0:T(128)}, u32[]{:S(2)}) copy-start(f32[16]{0:T(128)} %fx_ref.13) | copy-start | bytes 196
  31.9 36.7 %copy-start.19 = (f32[16]{0:T(128)S(1)}, f32[16]{0:T(128)}, u32[]{:S(2)}) copy-start(f32[16]{0:T(128)} %fy_ref.13) | copy-start | bytes 196
  31.9 8.9 %collective-permute-start.9 = (f32[192,8,128]{2,1,0:T(8,128)S(1)}, f32[192,8,128]{2,1,0:T(8,128)S(1)}, u32[]{:S(2)}, u32[]{:S(2)}) collective-permute-start(f32[192,8,128]{2,1,0:T(8,128)S(1)} %get-tuple-element.31._.own_ref.s0), channel_id=1, source_target_pairs={{0,1},{1,0},{2,3},{3,2},{4,5},{5,4},{6,7},{7,6},{8,9},{9,8},{10,11... | collective-permute-start | bytes 2359304 | tf_op jit(solution)/shard_map/ppermute | solution.py:641
  40.0 7.4 %copy-start.2 = (f32[16,3,16,8,128]{4,3,2,1,0:T(8,128)}, f32[16,3,16,8,128]{4,3,2,1,0:T(8,128)S(1)}, u32[]{:S(2)}) copy-start(f32[16,3,16,8,128]{4,3,2,1,0:T(8,128)S(1)} %get-tuple-element.32.planes_ref) | copy-start | bytes 9437188
  40.2 2.7 %collective-permute-start.4 = (f32[192,8,128]{2,1,0:T(8,128)S(1)}, f32[192,8,128]{2,1,0:T(8,128)S(1)}, u32[]{:S(2)}, u32[]{:S(2)}) collective-permute-start(f32[192,8,128]{2,1,0:T(8,128)S(1)} %join_edges.1.own_ref.s0), channel_id=1, source_target_pairs={{0,1},{1,0},{2,3},{3,2},{4,5},{5,4},{6,7},{7,6},{8,9},{9,8},{10,11... | collective-permute-start | bytes 2359304 | tf_op jit(solution)/shard_map/ppermute | solution.py:641
  40.3 6.6 %collective-permute-start.12 = (f32[128,8,128]{2,1,0:T(8,128)S(1)}, f32[128,8,128]{2,1,0:T(8,128)S(1)}, u32[]{:S(2)}, u32[]{:S(2)}) collective-permute-start(f32[128,8,128]{2,1,0:T(8,128)S(1)} %get-tuple-element.30._.own_ref.s0), channel_id=1, source_target_pairs={{0,1},{1,0},{2,3},{3,2},{4,5},{5,4},{6,7},{7,6},{8,9},{9,8},{10,11... | collective-permute-start | bytes 1572872 | tf_op jit(solution)/shard_map/ppermute | solution.py:641
  40.7 6.1 %copy-start = (f32[192,8,128]{2,1,0:T(8,128)}, f32[192,8,128]{2,1,0:T(8,128)S(1)}, u32[]{:S(2)}) copy-start(f32[192,8,128]{2,1,0:T(8,128)S(1)} %collective-permute-done.9.core_ref.s1) | copy-start | bytes 2359300
  41.3 10.9 %collective-permute-start.10 = (f32[96,8,128]{2,1,0:T(8,128)S(1)}, f32[96,8,128]{2,1,0:T(8,128)}, u32[]{:S(2)}, u32[]{:S(2)}) collective-permute-start(f32[96,8,128]{2,1,0:T(8,128)S(1)} %fold_half.4), channel_id=1, source_target_pairs={{0,2},{1,3},{2,0},{3,1},{4,6},{5,7},{6,4},{7,5},{8,10},{9,11},{10,... | collective-permute-start | bytes 1179656 | tf_op jit(solution)/shard_map/ppermute | solution.py:642
  43.5 17.1 %collective-permute-start.5 = (f32[96,8,128]{2,1,0:T(8,128)S(1)}, f32[96,8,128]{2,1,0:T(8,128)}, u32[]{:S(2)}, u32[]{:S(2)}) collective-permute-start(f32[96,8,128]{2,1,0:T(8,128)S(1)} %fold_half.3), channel_id=1, source_target_pairs={{0,2},{1,3},{2,0},{3,1},{4,6},{5,7},{6,4},{7,5},{8,10},{9,11},{10,... | collective-permute-start | bytes 1179656 | tf_op jit(solution)/shard_map/ppermute | solution.py:642
  44.6 33.7 %collective-permute-start.7 = (f32[16,72,128]{2,1,0:T(8,128)}, f32[16,72,128]{2,1,0:T(8,128)S(1)}, u32[]{:S(2)}, u32[]{:S(2)}) collective-permute-start(f32[16,72,128]{2,1,0:T(8,128)} %get-tuple-element.35), channel_id=1, source_target_pairs={{0,4},{4,8},{8,12},{12,16},{16,20},{20,24},{24,28},{1,5},{5,9},{9,... | collective-permute-start | bytes 1769480 | tf_op jit(solution)/shard_map/ppermute | solution.py:637
  46.9 1.0 %copy-start.8 = (f32[128,8,128]{2,1,0:T(8,128)}, f32[128,8,128]{2,1,0:T(8,128)S(1)}, u32[]{:S(2)}) copy-start(f32[128,8,128]{2,1,0:T(8,128)S(1)} %collective-permute-done.12.core_ref.s1) | copy-start | bytes 1572868
  47.5 18.8 %collective-permute-start.13 = (f32[64,8,128]{2,1,0:T(8,128)S(1)}, f32[64,8,128]{2,1,0:T(8,128)}, u32[]{:S(2)}, u32[]{:S(2)}) collective-permute-start(f32[64,8,128]{2,1,0:T(8,128)S(1)} %fold_half.5), channel_id=1, source_target_pairs={{0,2},{1,3},{2,0},{3,1},{4,6},{5,7},{6,4},{7,5},{8,10},{9,11},{10,... | collective-permute-start | bytes 786440 | tf_op jit(solution)/shard_map/ppermute | solution.py:642
  47.9 30.4 %collective-permute-start.8 = (f32[16,64,128]{2,1,0:T(8,128)}, f32[16,64,128]{2,1,0:T(8,128)}, u32[]{:S(2)}, u32[]{:S(2)}) collective-permute-start(f32[16,64,128]{2,1,0:T(8,128)} %get-tuple-element.36), channel_id=1, source_target_pairs={{4,0},{8,4},{12,8},{16,12},{20,16},{24,20},{28,24},{5,1},{9,5},{13... | collective-permute-start | bytes 1572872 | tf_op jit(solution)/shard_map/ppermute | solution.py:638
  52.2 22.4 %collective-permute-start.11 = (f32[96,8,128]{2,1,0:T(8,128)}, f32[96,8,128]{2,1,0:T(8,128)}, u32[]{:S(2)}, u32[]{:S(2)}) collective-permute-start(f32[96,8,128]{2,1,0:T(8,128)} %collective-permute-done.10.s2), channel_id=1, source_target_pairs={{0,1},{1,0},{2,3},{3,2},{4,5},{5,4},{6,7},{7,6},{8,9},{9,8},{10,11... | collective-permute-start | bytes 1179656 | tf_op jit(solution)/shard_map/ppermute | solution.py:643
  60.6 17.7 %collective-permute-start.6 = (f32[96,8,128]{2,1,0:T(8,128)}, f32[96,8,128]{2,1,0:T(8,128)}, u32[]{:S(2)}, u32[]{:S(2)}) collective-permute-start(f32[96,8,128]{2,1,0:T(8,128)} %collective-permute-done.5.s2), channel_id=1, source_target_pairs={{0,1},{1,0},{2,3},{3,2},{4,5},{5,4},{6,7},{7,6},{8,9},{9,8},{10,11... | collective-permute-start | bytes 1179656 | tf_op jit(solution)/shard_map/ppermute | solution.py:643
  66.3 2.4 %collective-permute-start.14 = (f32[64,8,128]{2,1,0:T(8,128)}, f32[64,8,128]{2,1,0:T(8,128)}, u32[]{:S(2)}, u32[]{:S(2)}) collective-permute-start(f32[64,8,128]{2,1,0:T(8,128)} %collective-permute-done.13.s2), channel_id=1, source_target_pairs={{0,1},{1,0},{2,3},{3,2},{4,5},{5,4},{6,7},{7,6},{8,9},{9,8},{10,11... | collective-permute-start | bytes 786440 | tf_op jit(solution)/shard_map/ppermute | solution.py:643
  67.8 6.8 %copy-start.1 = (f32[192,8,128]{2,1,0:T(8,128)S(1)}, f32[192,8,128]{2,1,0:T(8,128)}, u32[]{:S(2)}) copy-start(f32[192,8,128]{2,1,0:T(8,128)} %copy-done) | copy-start | bytes 2359300
  67.8 6.8 %copy-start.5 = (f32[16,3,16,8,128]{4,3,2,1,0:T(8,128)S(1)}, f32[16,3,16,8,128]{4,3,2,1,0:T(8,128)}, u32[]{:S(2)}) copy-start(f32[16,3,16,8,128]{4,3,2,1,0:T(8,128)} %copy-done.4) | copy-start | bytes 9437188
  68.6 1.9 %copy-start.7 = (f32[16,2,16,8,128]{4,3,2,1,0:T(8,128)S(1)}, f32[16,2,16,8,128]{4,3,2,1,0:T(8,128)}, u32[]{:S(2)}) copy-start(f32[16,2,16,8,128]{4,3,2,1,0:T(8,128)} %copy-done.6) | copy-start | bytes 6291460
  70.5 1.0 %copy-start.9 = (f32[128,8,128]{2,1,0:T(8,128)S(1)}, f32[128,8,128]{2,1,0:T(8,128)}, u32[]{:S(2)}) copy-start(f32[128,8,128]{2,1,0:T(8,128)} %copy-done.8) | copy-start | bytes 1572868
  74.6 5.4 %copy-start.23 = (f32[16,64,128]{2,1,0:T(8,128)S(1)}, f32[16,64,128]{2,1,0:T(8,128)}, u32[]{:S(2)}) copy-start(f32[16,64,128]{2,1,0:T(8,128)} %get-tuple-element.38) | copy-start | bytes 1572868
  74.6 5.5 %copy-start.11 = (s32[2048]{0:T(1024)S(1)}, s32[2048]{0:T(1024)}, u32[]{:S(2)}) copy-start(s32[2048]{0:T(1024)} %param.18) | copy-start | bytes 24580
  74.6 5.5 %copy-start.21 = (f32[16]{0:T(128)S(1)}, f32[16]{0:T(128)}, u32[]{:S(2)}) copy-start(f32[16]{0:T(128)} %inflow_ref.9) | copy-start | bytes 196
  80.1 1.9 %copy-start.3 = (f32[16,3,16,8,128]{4,3,2,1,0:T(8,128)S(1)}, f32[16,3,16,8,128]{4,3,2,1,0:T(8,128)}, u32[]{:S(2)}) copy-start(f32[16,3,16,8,128]{4,3,2,1,0:T(8,128)} %copy-done.2) | copy-start | bytes 9437188

commit v4 on v3

v4 whole, which is shorter than its diff:
```python
import functools
import math

import jax
import jax.numpy as jnp
from jax import lax
from jax.experimental import pallas as pl
from jax.experimental.pallas import tpu as pltpu
from jax.sharding import PartitionSpec as P

SPEED_TALLY = 64
CFL = 8
LOW_ROWS = CFL + 1
HIGH_ROWS = CFL
ROW = 8
LANE = 128
PAD = 16
F32 = jnp.float32
LOW_SENT = 72
HIGH_SENT = 72

SMEM_SPEC = pl.BlockSpec(memory_space=pltpu.SMEM)
ANY_SPEC = pl.BlockSpec(memory_space=pl.ANY)
HBM_SPEC = pl.BlockSpec(memory_space=pltpu.HBM)
VMEM_SPEC = pl.BlockSpec(memory_space=pltpu.VMEM)


def params(mebibytes):
    return pltpu.CompilerParams(vmem_limit_bytes=mebibytes * 1024 * 1024)


def low_need(shift):
    return jnp.where(shift >= 0, shift + 1, 0)


def high_need(shift):
    return jnp.where(shift < 0, -shift, 0)


def fill_rows(padded, v, columns, start, count, value):
    block = jnp.full((ROW, LANE), value, F32)
    for t in columns:
        for r in range(start, start + count, ROW):
            padded[v, t, r : r + ROW, :] = block


def prepare_heights(heights_ref, bars):
    lane_tiles = heights_ref.shape[0]
    sublane = lax.broadcasted_iota(jnp.int32, (ROW, LANE), 0)
    for t in range(lane_tiles):
        bars[t] = jnp.broadcast_to(heights_ref[t : t + 1, :], (ROW, LANE)) - sublane


def advect(padded, v, scalars, tiles):
    sx, sy, fx, fy = scalars
    lane_tiles = padded.shape[1] - 2
    lane = lax.broadcasted_iota(jnp.int32, (ROW, LANE), 1)
    near_roll = jnp.where(sx < 0, sx + LANE, sx)
    far_roll = jnp.where(sx + 1 < 0, sx + 1 + LANE, sx + 1)

    def moved(start, t):
        nearer = padded[v, t + 1, pl.ds(start, ROW), :]
        further = padded[v, t + 1, pl.ds(start - 1, ROW), :]
        line = (1.0 - fy) * nearer + fy * further
        return pltpu.roll(line, near_roll, 1), pltpu.roll(line, far_roll, 1)

    def blend(put, t, near, far):
        put(t, (1.0 - fx) * near + fx * far)

    @pl.when(sx >= 0)
    def _():
        own_near, own_far = lane >= sx, lane >= sx + 1
        for begin, put in tiles:
            before = moved(begin - sy, -1)
            for t in range(lane_tiles):
                here = moved(begin - sy, t)
                near = jnp.where(own_near, here[0], before[0])
                blend(put, t, near, jnp.where(own_far, here[1], before[1]))
                before = here

    @pl.when(sx < 0)
    def _():
        own_near, own_far = lane < sx + LANE, lane < sx + 1 + LANE
        for begin, put in tiles:
            here = moved(begin - sy, 0)
            for t in range(lane_tiles):
                after = moved(begin - sy, t + 1)
                near = jnp.where(own_near, here[0], after[0])
                blend(put, t, near, jnp.where(own_far, here[1], after[1]))
                here = after


def store_masked(target, bars, first_row, solid_value):
    def put(t, value):
        target[t] = jnp.where(first_row < bars[t], solid_value, value)

    return put


def velocity(sx_ref, sy_ref, fx_ref, fy_ref, v):
    return sx_ref[v].astype(F32) + fx_ref[v], sy_ref[v].astype(F32) + fy_ref[v]


def sum_moments(planes_ref, k, weights, lane_tile_range):
    sums = [[None] * 4 for _ in lane_tile_range]
    for v, (along_x, along_y) in enumerate(weights):
        square = along_x * along_x + along_y * along_y
        for n, t in enumerate(lane_tile_range):
            f = planes_ref[v, k, t]
            terms = (f, f * along_x, f * along_y, f * square)
            sums[n] = [b if a is None else a + b for a, b in zip(sums[n], terms)]
    return sums


class Plan:
    def __init__(self, row_tiles, half):
        self.tile = 4 * half
        self.inside = list(range(2, row_tiles - 2))
        self.sizes = [self.tile + 4, self.tile, len(self.inside) * self.tile, 2 * self.tile, 2 * self.tile]
        self.starts = [sum(self.sizes[:n]) for n in range(len(self.sizes) + 1)]
        self.row_tiles = row_tiles

    def start(self, j):
        low = self.starts[3] + self.tile * j
        high = self.starts[4] + self.tile * (j - self.row_tiles + 2)
        inside = self.starts[2] + self.tile * (j - 2)
        return jnp.where(j < 2, low, jnp.where(j >= self.row_tiles - 2, high, inside))


def advance_kernel(plan, cuts, group, meta_ref, sx_ref, sy_ref, fx_ref, fy_ref, inflow_ref, wall_ref,
                   heights_ref, pop_ref, *refs):
    planes_ref, mine_ref, theirs_ref = refs[:3]
    packs = refs[3 : 3 + len(cuts)]
    (padded, planes_buf, outer, moments, low_pack, high_pack, bars, sem_in, sem_planes, sem_out) = refs[
        3 + len(cuts) :
    ]
    planes, row_tiles, lane_tiles = pop_ref.shape[:3]
    half = lane_tiles // 2
    rows = row_tiles * ROW
    row0, first, last, core = (meta_ref[i] for i in range(4))

    def loads(g):
        members = pl.ds(g * group, group)
        return [
            pltpu.make_async_copy(
                pop_ref.at[members, i],
                padded.at[members, 1 : 1 + lane_tiles, PAD + ROW * i : PAD + ROW * (i + 1), :],
                sem_in.at[g, i],
            )
            for i in range(row_tiles)
        ]

    def start(g, _):
        for load in loads(g):
            load.start()
        return 0

    lax.fori_loop(0, planes // group, start, 0)
    prepare_heights(heights_ref, bars)
    for slot in range(2):
        moments[slot, plan.tile : plan.tile + 4] = jnp.zeros((4, ROW, LANE), F32)

    def out_copy(v):
        return pltpu.make_async_copy(planes_buf.at[v], planes_ref.at[v], sem_planes.at[v])

    def one(v, offsets):
        low, high = offsets
        value = inflow_ref[v]
        shift = sy_ref[v]
        up = shift >= 0
        columns = range(lane_tiles + 2)
        fill_rows(padded, v, (0, lane_tiles + 1), PAD, rows, value)
        fill_rows(padded, v, columns, 0, PAD, jnp.where(first == 1, value, 0.0))
        fill_rows(padded, v, columns, PAD + rows, ROW, jnp.where(last == 1, value, 0.0))

        @pl.when(v % group == 0)
        def _():
            for load in loads(v // group):
                load.wait()

        scalars = sx_ref[v], shift, fx_ref[v], fy_ref[v]
        work = [
            (PAD + ROW * j, store_masked(planes_buf.at[v, j], bars, row0 + ROW * j, wall_ref[v]))
            for j in range(row_tiles)
        ]
        beyond = jnp.where(up, rows, -ROW)
        work.append((PAD + beyond, store_masked(outer.at[v], bars, row0 + beyond, 0.0)))
        advect(padded, v, scalars, work)
        out_copy(v).start()

        @pl.when(shift == CFL)
        def _():
            along_x, along_y = velocity(sx_ref, sy_ref, fx_ref, fy_ref, v)
            factors = 1.0, along_x, along_y, along_x * along_x + along_y * along_y

            def put(t, value):
                row = jnp.where(row0 + rows + ROW < bars[t], 0.0, value)
                slot, r = jnp.bitwise_xor(core, t // half), t % half
                for m in range(4):
                    n = plan.tile + m
                    total = moments[slot, n, r : r + 1, :] + (row * factors[m])[0:1, :]
                    moments[slot, n, r : r + 1, :] = total

            advect(padded, v, scalars, [(PAD + rows + ROW, put)])
            for t in range(lane_tiles):
                low_pack[t, pl.ds(low + 8, 1), :] = padded[v, t + 1, PAD + rows - 1 : PAD + rows, :]

        @pl.when(up)
        def _():
            for t in range(lane_tiles):
                source = pl.ds(PAD + rows - 1 - shift, 8)
                low_pack[t, pl.ds(low, 8), :] = padded[v, t + 1, source, :]

        @pl.when(shift == CFL)
        def _():
            for t in range(lane_tiles):
                low_pack[t, pl.ds(low + 8, 1), :] = padded[v, t + 1, PAD + rows - 1 : PAD + rows, :]

        @pl.when(jnp.logical_not(up))
        def _():
            for t in range(lane_tiles):
                high_pack[t, pl.ds(high, 8), :] = padded[v, t + 1, PAD : PAD + 8, :]

        return low + low_need(shift), high + high_need(shift)

    lax.fori_loop(0, planes, one, (jnp.int32(0), jnp.int32(0)))
    packing = []
    for n, (pack, begin, end) in enumerate(cuts):
        source = (low_pack, high_pack)[pack].at[:, begin:end, :]
        packing.append(pltpu.make_async_copy(source, packs[n], sem_out.at[2 + n]))
        packing[-1].start()

    for h in range(2):
        slot = jnp.bitwise_xor(core, h)
        for rising in (True, False):
            for part in range(2):
                tiles = range(h * half + part * half // 2, h * half + (part + 1) * half // 2)
                sums = [[None] * 4 for _ in tiles]
                for v in range(planes):
                    along_x, along_y = velocity(sx_ref, sy_ref, fx_ref, fy_ref, v)
                    goes = jnp.where((sy_ref[v] >= 0) == rising, 1.0, 0.0)
                    square = (along_x * along_x + along_y * along_y) * goes
                    factors = goes, along_x * goes, along_y * goes, square
                    for n, t in enumerate(tiles):
                        f = outer[v, t]
                        terms = [f * w for w in factors]
                        sums[n] = [b if a is None else a + b for a, b in zip(sums[n], terms)]
                begin = plan.starts[0 if rising else 1]
                for n, t in enumerate(tiles):
                    for m in range(4):
                        moments[slot, begin + m * half + t - h * half] = sums[n][m]
    weights = [velocity(sx_ref, sy_ref, fx_ref, fy_ref, v) for v in range(planes)]

    def step(j, _):
        begin = plan.start(j)
        for h in range(2):
            sums = sum_moments(planes_buf, j, weights, range(h * half, (h + 1) * half))
            slot = jnp.bitwise_xor(core, h)
            for t in range(half):
                for m in range(4):
                    moments[slot, begin + m * half + t] = sums[t][m]
        return 0

    lax.fori_loop(0, row_tiles, step, 0)
    copies = [
        pltpu.make_async_copy(moments.at[1], theirs_ref, sem_out.at[1]),
        pltpu.make_async_copy(moments.at[0], mine_ref, sem_out.at[0]),
    ]
    for copy in copies:
        copy.start()

    def finish(v, _):
        out_copy(v).wait()
        return 0

    lax.fori_loop(0, planes, finish, 0)
    for copy in packing + copies:
        copy.wait()


def advance(plan, meta, small, heights, pop, cuts):
    planes, row_tiles, lane_tiles = pop.shape[:3]
    group = math.gcd(planes, 4)
    blocks = plan.starts[-1]
    half_sums = jax.ShapeDtypeStruct((blocks, ROW, LANE), F32)
    return pl.pallas_call(
        functools.partial(advance_kernel, plan, cuts, group),
        out_shape=[jax.ShapeDtypeStruct(pop.shape, F32), half_sums, half_sums]
        + [jax.ShapeDtypeStruct((lane_tiles, end - begin, LANE), F32) for _, begin, end in cuts],
        in_specs=[SMEM_SPEC] * 7 + [VMEM_SPEC, ANY_SPEC],
        out_specs=[ANY_SPEC] * (3 + len(cuts)),
        scratch_shapes=[
            pltpu.VMEM((planes, lane_tiles + 2, PAD + row_tiles * ROW + ROW, LANE), F32),
            pltpu.VMEM((planes, row_tiles, lane_tiles, ROW, LANE), F32),
            pltpu.VMEM((planes, lane_tiles, ROW, LANE), F32),
            pltpu.VMEM((2, blocks, ROW, LANE), F32),
            pltpu.VMEM((lane_tiles, planes * LOW_ROWS + 16, LANE), F32),
            pltpu.VMEM((lane_tiles, planes * HIGH_ROWS + 16, LANE), F32),
            pltpu.VMEM((lane_tiles, ROW, LANE), jnp.int32),
            pltpu.SemaphoreType.DMA((planes // group, row_tiles)),
            pltpu.SemaphoreType.DMA((planes,)),
            pltpu.SemaphoreType.DMA((2 + len(cuts),)),
        ],
        compiler_params=params(58),
        name="advance",
    )(meta, *small, heights, pop)


def fold_kernel(mine_ref, received_ref, *out_refs):
    begin = 0
    for ref in out_refs:
        n = ref.shape[0]
        ref[...] = mine_ref[begin : begin + n] + received_ref[begin : begin + n]
        begin += n


def fold(mine, received, sizes):
    return pl.pallas_call(
        fold_kernel,
        out_shape=[jax.ShapeDtypeStruct((n, ROW, LANE), F32) for n in sizes],
        in_specs=[VMEM_SPEC] * 2,
        out_specs=[VMEM_SPEC] * len(sizes),
        compiler_params=params(8),
        name="fold",
    )(mine, received)


def join_low_kernel(own_ref, low_ref, out_ref):
    tile = own_ref.shape[0] // 2
    half = tile // 4
    out_ref[:tile] = own_ref[:tile] + low_ref[:tile]
    top = lax.broadcasted_iota(jnp.int32, (ROW, LANE), 0) == 0
    for m in range(4):
        for n in range(half):
            row = jnp.broadcast_to(low_ref[tile + m, n : n + 1, :], (ROW, LANE))
            index = tile + m * half + n
            out_ref[index] = own_ref[index] + jnp.where(top, row, 0.0)


def add_kernel(a_ref, b_ref, out_ref):
    out_ref[...] = a_ref[...] + b_ref[...]


def join_high_kernel(own_ref, high_ref, out_ref):
    tile = high_ref.shape[0]
    out_ref[:tile] = own_ref[:tile]
    out_ref[tile:] = own_ref[tile:] + high_ref[...]


def small_call(kernel, name, *operands):
    return pl.pallas_call(
        kernel,
        out_shape=jax.ShapeDtypeStruct(operands[0].shape, F32),
        in_specs=[VMEM_SPEC] * len(operands),
        out_specs=VMEM_SPEC,
        compiler_params=params(8),
        name=name,
    )(*operands)


def overflow_kernel(limits, sy_ref, *refs):
    low, high = low_need(sy_ref[0]), high_need(sy_ref[0])
    for v in range(1, sy_ref.shape[0]):
        low, high = low + low_need(sy_ref[v]), high + high_need(sy_ref[v])
    refs[-1][0] = jnp.where((low > limits[0]) | (high > limits[1]), 1, 0)


def overflow(shift_y, limits, after):
    return pl.pallas_call(
        functools.partial(overflow_kernel, limits),
        out_shape=jax.ShapeDtypeStruct((1,), jnp.int32),
        in_specs=[SMEM_SPEC] + [ANY_SPEC] * len(after),
        out_specs=SMEM_SPEC,
        compiler_params=params(8),
        name="overflow",
    )(shift_y, *after)[0]


def profile(density, flux_x, flux_y, energy, factor):
    inverse = 1.0 / density
    mean_x = flux_x * inverse
    mean_y = flux_y * inverse
    temperature = 0.5 * (energy * inverse - mean_x * mean_x - mean_y * mean_y)
    rate = 1.0 - jnp.exp(-factor * density / (SPEED_TALLY * jnp.sqrt(temperature)))
    height = rate * (density / (2.0 * math.pi * temperature))
    return mean_x, mean_y, -0.5 / temperature, height, 1.0 - rate


def relax_cells(get, put, values, factor, weights):
    mean_x, mean_y, scale, height, keep = profile(*values, factor)
    for v, (along_x, along_y) in enumerate(weights):
        gap_x = along_x - mean_x
        gap_y = along_y - mean_y
        state = height * jnp.exp((gap_x * gap_x + gap_y * gap_y) * scale)
        put(v, keep * get(v) + state)


def relax_tile(buf, sums, base, core, factor, weights, k, h):
    mine_ref, other_ref = sums
    half = buf.shape[2] // 2
    for n in range(half):
        t = h * half + n
        values = []
        for m in range(4):
            index = base + m * half + n
            values.append(jnp.where(core == h, mine_ref[index], other_ref[index]))

        def put(v, value):
            buf[v, k, t] = value

        relax_cells(lambda v: buf[v, k, t], put, values, factor, weights)


def relax_kernel(tiles, meta_ref, sx_ref, sy_ref, fx_ref, fy_ref, factor_ref, mine_ref, other_ref,
                 planes_ref, out_ref, done_ref, buf, sem_in, sem_out):
    planes, _, lane_tiles = planes_ref.shape[:3]
    half = lane_tiles // 2
    done_ref[0] = 1
    first_tile, count = tiles[0], len(tiles)

    def copy(k, h, out):
        lanes = pl.ds(h * half, half)
        here = buf.at[:, k, lanes]
        if out:
            return pltpu.make_async_copy(here, out_ref.at[:, first_tile + k, lanes], sem_out.at[2 * k + h])
        return pltpu.make_async_copy(planes_ref.at[:, first_tile + k, lanes], here, sem_in.at[2 * k + h])

    for k in range(count):
        for h in range(2):
            copy(k, h, False).start()
    weights = [velocity(sx_ref, sy_ref, fx_ref, fy_ref, v) for v in range(planes)]

    def step(k, _):
        for h in range(2):
            copy(k, h, False).wait()
            sums = mine_ref, other_ref
            relax_tile(buf, sums, k * 4 * half, meta_ref[3], factor_ref[0], weights, k, h)
            copy(k, h, True).start()
        return 0

    lax.fori_loop(0, count, step, 0)
    for k in range(count):
        for h in range(2):
            copy(k, h, True).wait()


def relax_inside(tiles, meta, small, factor, sums, moved):
    planes, _, lane_tiles = moved.shape[:3]
    count = len(tiles)
    return pl.pallas_call(
        functools.partial(relax_kernel, tiles),
        out_shape=[jax.ShapeDtypeStruct(moved.shape, F32), jax.ShapeDtypeStruct((1,), jnp.int32)],
        in_specs=[SMEM_SPEC] * 6 + [VMEM_SPEC] * 2 + [ANY_SPEC],
        out_specs=[ANY_SPEC, SMEM_SPEC],
        scratch_shapes=[
            pltpu.VMEM((planes, count, lane_tiles, ROW, LANE), F32),
            pltpu.SemaphoreType.DMA((2 * count,)),
            pltpu.SemaphoreType.DMA((2 * count,)),
        ],
        compiler_params=params(58),
        name="relax_inside",
    )(meta, *small[:4], factor, *sums, moved)


def relax_edges_kernel(cuts, meta_ref, sx_ref, sy_ref, fx_ref, fy_ref, inflow_ref, factor_ref,
                       heights_ref, m_low, o_low, m_high, o_high, planes_ref, *refs):
    pack_refs = refs[: len(cuts)]
    _, out_ref, frames, buf, low_buf, high_buf, bars, sem_in, sem_planes, sem_out = refs[len(cuts) :]
    planes, row_tiles, lane_tiles = planes_ref.shape[:3]
    half = lane_tiles // 2
    row0, first, last, core = (meta_ref[i] for i in range(4))
    places = 0, 1, row_tiles - 2, row_tiles - 1
    needs = [low_need(sy_ref[0]), high_need(sy_ref[0])]
    for v in range(1, planes):
        needs = [needs[0] + low_need(sy_ref[v]), needs[1] + high_need(sy_ref[v])]

    def pack_copy(n):
        pack, begin, end = cuts[n]
        target = (low_buf, high_buf)[pack].at[:, 16 + begin : 16 + end, :]
        return pltpu.make_async_copy(pack_refs[n], target, sem_in.at[n])

    def in_copy(k):
        return pltpu.make_async_copy(planes_ref.at[:, places[k]], buf.at[:, k], sem_planes.at[k])

    for n in range(len(cuts)):
        pl.when(needs[cuts[n][0]] > cuts[n][1])(lambda n=n: pack_copy(n).start())
    for k in range(4):
        in_copy(k).start()
    prepare_heights(heights_ref, bars)
    for n in range(len(cuts)):
        pl.when(needs[cuts[n][0]] > cuts[n][1])(lambda n=n: pack_copy(n).wait())
    for k in range(4):
        in_copy(k).wait()

    def add_masked(v, k, first_row):
        def put(t, value):
            buf[v, k, t] = buf[v, k, t] + jnp.where(first_row < bars[t], 0.0, value)

        return put

    def one(v, offsets):
        low, high = offsets
        value = inflow_ref[v]
        shift = sy_ref[v]
        up = shift >= 0
        scalars = sx_ref[v], shift, fx_ref[v], fy_ref[v]
        borders = (0, lane_tiles + 1)
        columns = range(lane_tiles + 2)

        @pl.when(up & (first == 0))
        def _():
            fill_rows(frames, v, borders, 8, 16, value)
            fill_rows(frames, v, columns, 24, 16, 0.0)
            for t in range(lane_tiles):
                for r in range(0, 16, ROW):
                    piece = low_buf[t, pl.ds(low + shift + 1 + r, ROW), :]
                    frames[v, t + 1, 8 + r : 8 + r + ROW, :] = piece
            advect(frames, v, scalars, [(24, add_masked(v, 0, row0))])

            @pl.when(shift == CFL)
            def _():
                advect(frames, v, scalars, [(32, add_masked(v, 1, row0 + ROW))])

        @pl.when(jnp.logical_not(up) & (last == 0))
        def _():
            fill_rows(frames, v, borders, 32, 8, value)
            fill_rows(frames, v, columns, 16, 16, 0.0)
            for t in range(lane_tiles):
                frames[v, t + 1, 32:40, :] = high_buf[t, pl.ds(16 + high, ROW), :]
            advect(frames, v, scalars, [(24, add_masked(v, 3, row0 + ROW * (row_tiles - 1)))])

        return low + low_need(shift), high + high_need(shift)

    lax.fori_loop(0, planes, one, (jnp.int32(0), jnp.int32(0)))
    weights = [velocity(sx_ref, sy_ref, fx_ref, fy_ref, v) for v in range(planes)]

    def out_copy(k, h):
        j = jnp.where(k < 2, k, row_tiles - 4 + k)
        lanes = pl.ds(h * half, half)
        return pltpu.make_async_copy(buf.at[:, k, lanes], out_ref.at[:, j, lanes], sem_out.at[2 * k + h])

    for sums, begin in (((m_low, o_low), 0), ((m_high, o_high), 2)):

        def step(k, _, sums=sums, begin=begin):
            for h in range(2):
                relax_tile(buf, sums, (k - begin) * 4 * half, core, factor_ref[0], weights, k, h)
                out_copy(k, h).start()
            return 0

        lax.fori_loop(begin, begin + 2, step, 0)
    for k in range(4):
        for h in range(2):
            out_copy(k, h).wait()


def relax_edges(meta, small, factor, heights, sums, moved, packs, cuts, out):
    planes, _, lane_tiles = moved.shape[:3]
    operands = [meta, *small[:5], factor, heights, *sums, moved, *packs, out]
    return pl.pallas_call(
        functools.partial(relax_edges_kernel, cuts),
        out_shape=jax.ShapeDtypeStruct(out.shape, F32),
        in_specs=[SMEM_SPEC] * 7 + [VMEM_SPEC] * 5 + [ANY_SPEC] * (len(cuts) + 2),
        out_specs=ANY_SPEC,
        scratch_shapes=[
            pltpu.VMEM((planes, lane_tiles + 2, 48, LANE), F32),
            pltpu.VMEM((planes, 4, lane_tiles, ROW, LANE), F32),
            pltpu.VMEM((lane_tiles, planes * LOW_ROWS + 32, LANE), F32),
            pltpu.VMEM((lane_tiles, planes * HIGH_ROWS + 32, LANE), F32),
            pltpu.VMEM((lane_tiles, ROW, LANE), jnp.int32),
            pltpu.SemaphoreType.DMA((len(cuts),)),
            pltpu.SemaphoreType.DMA((4,)),
            pltpu.SemaphoreType.DMA((8,)),
        ],
        input_output_aliases={len(operands) - 1: 0},
        compiler_params=params(58),
        name="relax_edges",
    )(*operands)


def per_device(populations, shift_x, shift_y, frac_x, frac_y, inflow, wall_state, heights,
               impact_frequency_factor):
    planes, row_count, col_count = populations.shape
    space_count, vel_count = lax.axis_size("space"), lax.axis_size("vel")
    row_tiles, lane_tiles = row_count // ROW, col_count // LANE
    space, vel = lax.axis_index("space"), lax.axis_index("vel")
    forward = [(i, i + 1) for i in range(space_count - 1)]
    backward = [(target, source) for source, target in forward]
    partner = [(i, i ^ 1) for i in range(vel_count)]
    across = [(i, i ^ 2) for i in range(vel_count)]

    meta = jnp.stack([space * row_count, space == 0, space == space_count - 1, vel % 2]).astype(jnp.int32)
    small = (shift_x, shift_y, frac_x, frac_y, inflow, wall_state)
    factor = impact_frequency_factor.reshape(1)
    bars = heights.reshape(lane_tiles, LANE)
    pop = populations.reshape(planes, row_tiles, ROW, lane_tiles, LANE).transpose(0, 1, 3, 2, 4)
    low_sent, high_sent = min(LOW_SENT, planes * LOW_ROWS), min(HIGH_SENT, planes * HIGH_ROWS)
    cuts = [
        (0, 0, low_sent),
        (1, 0, high_sent),
        (0, low_sent, planes * LOW_ROWS),
        (1, high_sent, planes * HIGH_ROWS),
    ]
    plan = Plan(row_tiles, lane_tiles // 2)

    moved, mine, theirs, *packs = advance(plan, meta, small, bars, pop, cuts)
    received = lax.ppermute(theirs, "vel", partner)
    up, down, inside, edge_low, edge_high = fold(mine, received, plan.sizes)
    from_low = lax.ppermute(up, "space", forward)
    from_high = lax.ppermute(down, "space", backward)
    low_first = lax.ppermute(packs[0], "space", forward)
    high_first = lax.ppermute(packs[1], "space", backward)

    def total(sums):
        whole = small_call(add_kernel, "add", sums, lax.ppermute(sums, "vel", across))
        return whole, lax.ppermute(whole, "vel", partner)

    sums_inside = total(inside)
    sums_low = total(small_call(join_low_kernel, "join_low", edge_low, from_low))
    sums_high = total(small_call(join_high_kernel, "join_high", edge_high, from_high))

    out, done = relax_inside(plan.inside, meta, small, factor, sums_inside, moved)
    after = low_first, high_first, sums_low[1], sums_high[1], done
    needed = overflow(shift_y, (low_sent, high_sent), after)

    def send_more(low, high):
        return lax.ppermute(low, "space", forward), lax.ppermute(high, "space", backward)

    more = lax.cond(needed > 0, send_more, lambda low, high: (low, high), packs[2], packs[3])
    halo = low_first, high_first, *more
    out = relax_edges(meta, small, factor, bars, sums_low + sums_high, moved, halo, cuts, out)
    return out.transpose(0, 1, 3, 2, 4).reshape(planes, row_count, col_count)


def solution(mesh):
    return jax.shard_map(
        per_device,
        mesh=mesh,
        in_specs=(
            P("vel", "space", None),
            P("vel"),
            P("vel"),
            P("vel"),
            P("vel"),
            P("vel"),
            P("vel"),
            P(),
            P(),
        ),
        out_specs=P("vel", "space", None),
        check_vma=False,
    )
```

time: 90.8 us -> 71.4 us (0.79); the launches traced: 89.5 us -> 71.2 us
  local copies, waits for them, and re-layouts: 11.8 us -> 1.36 us
  Pallas kernels: 42.5 us -> 32.4 us
  waiting for transfers between devices: 12.6 us -> 15.1 us
    pallas_call x10 -> x8, Pallas kernels: 33.9 us -> 21.1 us  [the longest x1 14.9 us: advance(): pl.pallas_call(functools.partial(advance_kernel, plan, cuts, group), out_...]
    unnamed x48 -> x18, local copies, waits for them, and re-layouts: 11.8 us -> 1.36 us
    pallas_call x1, Pallas kernels: 7.52 us -> 9.55 us  [relax_edges(): pl.pallas_call(functools.partial(relax_edges_kernel, cuts), out_shape=jax...]
    ppermute x1, waiting for transfers between devices: 0.01 us -> 1.49 us  [per_device(): high_first = lax.ppermute(packs[1], 'space', backward)]
    ppermute x9 -> x7, waiting for transfers between devices: 12.6 us -> 13.4 us  [the longest x3 10.5 us: total(): lax.ppermute(sums, 'vel', across)]
    ppermute x9 -> x7, starting transfers between devices: 8.52 us -> 7.71 us  [the longest x3 4.12 us: total(): return (whole, lax.ppermute(whole, 'vel', partner))]
  transfers between devices with their start and end apart: 13 -> 11, of which waited for: 4 -> 5; matrix products, arithmetic and copies ran while one was open for 0% -> 0% of each run, Pallas kernels for 31% -> 9%
where the time goes in v4:
time: 71.4 us; the launch traced here: 71.2 us
  Pallas kernels  32.4 us (45%)
  starting transfers between devices  20.1 us (28%)
  waiting for transfers between devices  15.1 us (21%)
  between operations  1.52 us (2%)
  local copies, waits for them, and re-layouts  1.36 us (2%)
    pallas_call x1, Pallas kernels, advance(): pl.pallas_call(functools.partial(advance_kernel, plan, cuts, group), out_...  14.9 us
    ppermute x3, waiting for transfers between devices, total(): lax.ppermute(sums, 'vel', across)  10.5 us
    pallas_call x1, Pallas kernels, relax_edges(): pl.pallas_call(functools.partial(relax_edges_kernel, cuts), out_shape=jax...  9.55 us
    pallas_call x1, Pallas kernels, relax_inside(): pl.pallas_call(functools.partial(relax_kernel, tiles), out_shape=[jax.Sha...  5.88 us
    ppermute x3, starting transfers between devices, total(): return (whole, lax.ppermute(whole, 'vel', partner))  4.12 us
    ppermute x1, starting transfers between devices, per_device(): high_first = lax.ppermute(packs[1], 'space', backward)  3.96 us
    ppermute x1, starting transfers between devices, per_device(): from_low = lax.ppermute(up, 'space', forward)  3.11 us
    ppermute x3, starting transfers between devices, total(): lax.ppermute(sums, 'vel', across)  3.1 us
  transfers between devices with their start and end apart: 11, of which 5 were waited for; matrix products, arithmetic and copies ran while one was open for 0% of the time, Pallas kernels for 9%

profile of v4, /device:TPU:9, one launch (start us, length us, event | category | flops | bytes accessed | tf_op | source)
XLA Modules:
  0.0 71.2 jit_solution(4161586188748526933)
XLA Ops:
  0.0 0.7 pad_add_fusion.meta_ref
  0.7 14.9 %advance.1 = (f32[16,8,16,8,128]{4,3,2,1,0:T(8,128)}, f32[324,8,128]{2,1,0:T(8,128)}, f32[324,8,128]{2,1,0:T(8,128)}, f32[16,72,128]{2,1,0:T(8,128)}, f32[16,72,...) custom-call(s32[4]{0:T(128)} %pad_add_fusion.meta_ref, s32[16]{0:T(128)} %sx_ref.5, s32[16]{0:T(128)} %sy_ref.7, ...), custom_call_target="tpu_custom_call" | custom-call | tf_op jit(solution)/shard_map/advance/pallas_call | solution.py:286
  15.6 0.0 copy-start.8
  15.6 0.5 collective-permute-start.2
  16.1 2.9 %collective-permute-done.2.received_ref = f32[324,8,128]{2,1,0:T(8,128)S(1)} collective-permute-done((f32[324,8,128]{2,1,0:T(8,128)}, f32[324,8,128]{2,1,0:T(8,128)S(1)}, u32[]{:S(2)}, u32[]{:S(2)}) %collective-permute-start.2) | collective-permute-done | bytes 1327136 | tf_op jit(solution)/shard_map/ppermute | solution.py:606
  19.0 0.0 copy-start.3
  19.0 1.3 %copy-done.3 = f32[324,8,128]{2,1,0:T(8,128)S(1)} copy-done((f32[324,8,128]{2,1,0:T(8,128)S(1)}, f32[324,8,128]{2,1,0:T(8,128)}, u32[]{:S(2)}) %copy-start.3) | copy-done | bytes 1327128
  20.3 0.1 fold.1
  20.4 1.6 %collective-permute-start.11 = (f32[128,8,128]{2,1,0:T(8,128)S(1)}, f32[128,8,128]{2,1,0:T(8,128)S(1)}, u32[]{:S(2)}, u32[]{:S(2)}) collective-permute-start(f32[128,8,128]{2,1,0:T(8,128)S(1)} %get-tuple-element.40.a_ref), channel_id=1, source_target_pairs={{0,2},{1,3},{2,0},{3,1},{4,6},{5,7},{6,4},{7,5},{8,10},{9,11},{10,... | collective-permute-start | bytes 1572872 | tf_op jit(solution)/shard_map/ppermute | solution.py:614
  22.0 3.1 %collective-permute-start.3 = (f32[36,8,128]{2,1,0:T(8,128)S(1)}, f32[36,8,128]{2,1,0:T(8,128)S(1)}, u32[]{:S(2)}, u32[]{:S(2)}) collective-permute-start(f32[36,8,128]{2,1,0:T(8,128)S(1)} %get-tuple-element.34), channel_id=1, source_target_pairs={{0,4},{4,8},{8,12},{12,16},{16,20},{20,24},{24,28},{1,5},{5,9},{9,... | collective-permute-start | bytes 442376 | tf_op jit(solution)/shard_map/ppermute | solution.py:608
  25.1 3.1 %collective-permute-start.6 = (f32[32,8,128]{2,1,0:T(8,128)S(1)}, f32[32,8,128]{2,1,0:T(8,128)S(1)}, u32[]{:S(2)}, u32[]{:S(2)}) collective-permute-start(f32[32,8,128]{2,1,0:T(8,128)S(1)} %get-tuple-element.36), channel_id=1, source_target_pairs={{4,0},{8,4},{12,8},{16,12},{20,16},{24,20},{28,24},{5,1},{9,5},{13... | collective-permute-start | bytes 393224 | tf_op jit(solution)/shard_map/ppermute | solution.py:609
  28.2 2.2 %collective-permute-start.9 = (f32[16,72,128]{2,1,0:T(8,128)}, f32[16,72,128]{2,1,0:T(8,128)S(1)}, u32[]{:S(2)}, u32[]{:S(2)}) collective-permute-start(f32[16,72,128]{2,1,0:T(8,128)} %get-tuple-element.38), channel_id=1, source_target_pairs={{0,4},{4,8},{8,12},{12,16},{16,20},{20,24},{24,28},{1,5},{5,9},{9,... | collective-permute-start | bytes 1769480 | tf_op jit(solution)/shard_map/ppermute | solution.py:610
  30.4 4.0 %collective-permute-start.10 = (f32[16,72,128]{2,1,0:T(8,128)}, f32[16,72,128]{2,1,0:T(8,128)S(1)}, u32[]{:S(2)}, u32[]{:S(2)}) collective-permute-start(f32[16,72,128]{2,1,0:T(8,128)} %get-tuple-element.39), channel_id=1, source_target_pairs={{4,0},{8,4},{12,8},{16,12},{20,16},{24,20},{28,24},{5,1},{9,5},{13... | collective-permute-start | bytes 1769480 | tf_op jit(solution)/shard_map/ppermute | solution.py:611
  34.4 0.0 collective-permute-done.6.high_ref
  34.4 0.0 collective-permute-done.11.b_ref
  34.4 0.1 add.16.mine_ref
  34.5 0.0 copy-start.2
  34.5 1.8 %collective-permute-start.12 = (f32[128,8,128]{2,1,0:T(8,128)S(1)}, f32[128,8,128]{2,1,0:T(8,128)}, u32[]{:S(2)}, u32[]{:S(2)}) collective-permute-start(f32[128,8,128]{2,1,0:T(8,128)S(1)} %add.16.mine_ref), channel_id=1, source_target_pairs={{0,1},{1,0},{2,3},{3,2},{4,5},{5,4},{6,7},{7,6},{8,9},{9,8},{10,11... | collective-permute-start | bytes 1572872 | tf_op jit(solution)/shard_map/ppermute | solution.py:615
  36.4 0.1 collective-permute-start.7
  36.5 0.0 collective-permute-done.3.low_ref
  36.5 1.4 %collective-permute-start.4 = (f32[64,8,128]{2,1,0:T(8,128)S(1)}, f32[64,8,128]{2,1,0:T(8,128)S(1)}, u32[]{:S(2)}, u32[]{:S(2)}) collective-permute-start(f32[64,8,128]{2,1,0:T(8,128)S(1)} %join_low.1.a_ref), channel_id=1, source_target_pairs={{0,2},{1,3},{2,0},{3,1},{4,6},{5,7},{6,4},{7,5},{8,10},{9,11},{10,... | collective-permute-start | bytes 786440 | tf_op jit(solution)/shard_map/ppermute | solution.py:614
  37.9 6.3 %collective-permute-done.7.b_ref = f32[64,8,128]{2,1,0:T(8,128)S(1)} collective-permute-done((f32[64,8,128]{2,1,0:T(8,128)S(1)}, f32[64,8,128]{2,1,0:T(8,128)S(1)}, u32[]{:S(2)}, u32[]{:S(2)}) %collective-permute-start.7) | collective-permute-done | bytes 262176 | tf_op jit(solution)/shard_map/ppermute | solution.py:614
  44.3 0.0 copy-start.4
  44.3 1.4 %collective-permute-start.8 = (f32[64,8,128]{2,1,0:T(8,128)S(1)}, f32[64,8,128]{2,1,0:T(8,128)S(1)}, u32[]{:S(2)}, u32[]{:S(2)}) collective-permute-start(f32[64,8,128]{2,1,0:T(8,128)S(1)} %add.15.m_high), channel_id=1, source_target_pairs={{0,1},{1,0},{2,3},{3,2},{4,5},{5,4},{6,7},{7,6},{8,9},{9,8},{10,11... | collective-permute-start | bytes 786440 | tf_op jit(solution)/shard_map/ppermute | solution.py:615
  45.6 4.2 %collective-permute-done.4.b_ref = f32[64,8,128]{2,1,0:T(8,128)S(1)} collective-permute-done((f32[64,8,128]{2,1,0:T(8,128)S(1)}, f32[64,8,128]{2,1,0:T(8,128)S(1)}, u32[]{:S(2)}, u32[]{:S(2)}) %collective-permute-start.4) | collective-permute-done | bytes 262176 | tf_op jit(solution)/shard_map/ppermute | solution.py:614
  49.9 0.0 copy-start.5
  49.9 0.9 %collective-permute-start.5 = (f32[64,8,128]{2,1,0:T(8,128)S(1)}, f32[64,8,128]{2,1,0:T(8,128)S(1)}, u32[]{:S(2)}, u32[]{:S(2)}) collective-permute-start(f32[64,8,128]{2,1,0:T(8,128)S(1)} %add.14.m_low), channel_id=1, source_target_pairs={{0,1},{1,0},{2,3},{3,2},{4,5},{5,4},{6,7},{7,6},{8,9},{9,8},{10,11... | collective-permute-start | bytes 786440 | tf_op jit(solution)/shard_map/ppermute | solution.py:615
  51.5 0.0 collective-permute-done.12.other_ref
  51.5 0.0 copy-done.2
  51.5 5.9 %relax_inside.1 = (f32[16,8,16,8,128]{4,3,2,1,0:T(8,128)}, s32[1]{0:T(128)}) custom-call(s32[4]{0:T(128)} %pad_add_fusion.meta_ref, s32[16]{0:T(128)} %sx_ref.5, s32[16]{0:T(128)} %sy_ref.7, f32[16]{0:T(128)} %fx_ref.5, f32[16]{0:T(128)} %fy_ref.5, f32[1]{0:T(128)} %bitcast.13.factor_ref, f32[128,8,128]{2,1,0:T(8,128)} %copy-done.2, ...), custom_call_target="tpu_custom_call" | custom-call | tf_op jit(solution)/shard_map/relax_inside/pallas_call | solution.py:450
  57.4 0.2 collective-permute-done.9.refs_0_
  57.6 0.0 copy-start
  57.6 1.5 %collective-permute-done.10.refs_1_ = f32[16,72,128]{2,1,0:T(8,128)S(1)} collective-permute-done((f32[16,72,128]{2,1,0:T(8,128)}, f32[16,72,128]{2,1,0:T(8,128)S(1)}, u32[]{:S(2)}, u32[]{:S(2)}) %collective-permute-start.10) | collective-permute-done | bytes 589856 | tf_op jit(solution)/shard_map/ppermute | solution.py:611
  59.1 0.0 copy-start.1
  59.1 0.0 collective-permute-done.8.refs_3_.o_high
  59.1 0.0 copy-start.6
  59.1 0.0 collective-permute-done.5.refs_2_.o_low
  59.1 0.0 copy-start.7
  59.1 0.0 copy-done.8
  59.1 1.8 %overflow.1 = s32[1]{0:T(128)} custom-call(s32[16]{0:T(128)S(1)} %copy-done.8, f32[16,72,128]{2,1,0:T(8,128)S(1)} %collective-permute-done.9.refs_0_, f32[16,72,128]{2,1,0:T(8,128)S(1)} %collective-permute-done.10.refs_1_, f32[64,8,128]{2,1,0:T(8,128)S(1)} %collective-permute-done.5.refs_2_.o_low, f32[64,8,128]{2,1,0:T(8,128)S(1)} %collective-permute-done.8.refs_3_.o_high, ...), custom_call_target="tpu_custom_call" | custom-call | tf_op jit(solution)/shard_map/overflow/pallas_call | solution.py:369
  61.6 0.0 copy-done.4
  61.6 0.0 copy-done.5
  61.6 0.0 copy-done
  61.6 0.0 copy-done.1
  61.6 0.0 copy-done.6
  61.6 0.0 copy-done.7
  61.6 9.5 %relax_edges.1 = f32[16,8,16,8,128]{4,3,2,1,0:T(8,128)} custom-call(s32[4]{0:T(128)} %pad_add_fusion.meta_ref, s32[16]{0:T(128)} %sx_ref.5, s32[16]{0:T(128)} %sy_ref.7, f32[16]{0:T(128)} %fx_ref.5, f32[16]{0:T(128)} %fy_ref.5, f32[16]{0:T(128)} %inflow_ref.3, f32[1]{0:T(128)} %bitcast.14.factor_ref, ...), custom_call_target="tpu_custom_call", output_to_operand_aliasing={{}: (17, {})} | custom-call | tf_op jit(solution)/shard_map/relax_edges/pallas_call | solution.py:559
  (5 shorter events, 0.1 us)
Async XLA Ops:
  15.6 43.5 %copy-start.8 = (s32[16]{0:T(128)S(1)}, s32[16]{0:T(128)}, u32[]{:S(2)}) copy-start(s32[16]{0:T(128)} %sy_ref.7) | copy-start | bytes 196
  15.6 3.4 %collective-permute-start.2 = (f32[324,8,128]{2,1,0:T(8,128)}, f32[324,8,128]{2,1,0:T(8,128)S(1)}, u32[]{:S(2)}, u32[]{:S(2)}) collective-permute-start(f32[324,8,128]{2,1,0:T(8,128)} %get-tuple-element.32), channel_id=1, source_target_pairs={{0,1},{1,0},{2,3},{3,2},{4,5},{5,4},{6,7},{7,6},{8,9},{9,8},{10,11... | collective-permute-start | bytes 3981320 | tf_op jit(solution)/shard_map/ppermute | solution.py:606
  19.0 1.3 %copy-start.3 = (f32[324,8,128]{2,1,0:T(8,128)S(1)}, f32[324,8,128]{2,1,0:T(8,128)}, u32[]{:S(2)}) copy-start(f32[324,8,128]{2,1,0:T(8,128)} %get-tuple-element.31.mine_ref) | copy-start | bytes 3981316
  20.4 14.0 %collective-permute-start.11 = (f32[128,8,128]{2,1,0:T(8,128)S(1)}, f32[128,8,128]{2,1,0:T(8,128)S(1)}, u32[]{:S(2)}, u32[]{:S(2)}) collective-permute-start(f32[128,8,128]{2,1,0:T(8,128)S(1)} %get-tuple-element.40.a_ref), channel_id=1, source_target_pairs={{0,2},{1,3},{2,0},{3,1},{4,6},{5,7},{6,4},{7,5},{8,10},{9,11},{10,... | collective-permute-start | bytes 1572872 | tf_op jit(solution)/shard_map/ppermute | solution.py:614
  22.0 14.5 %collective-permute-start.3 = (f32[36,8,128]{2,1,0:T(8,128)S(1)}, f32[36,8,128]{2,1,0:T(8,128)S(1)}, u32[]{:S(2)}, u32[]{:S(2)}) collective-permute-start(f32[36,8,128]{2,1,0:T(8,128)S(1)} %get-tuple-element.34), channel_id=1, source_target_pairs={{0,4},{4,8},{8,12},{12,16},{16,20},{20,24},{24,28},{1,5},{5,9},{9,... | collective-permute-start | bytes 442376 | tf_op jit(solution)/shard_map/ppermute | solution.py:608
  25.1 9.3 %collective-permute-start.6 = (f32[32,8,128]{2,1,0:T(8,128)S(1)}, f32[32,8,128]{2,1,0:T(8,128)S(1)}, u32[]{:S(2)}, u32[]{:S(2)}) collective-permute-start(f32[32,8,128]{2,1,0:T(8,128)S(1)} %get-tuple-element.36), channel_id=1, source_target_pairs={{4,0},{8,4},{12,8},{16,12},{20,16},{24,20},{28,24},{5,1},{9,5},{13... | collective-permute-start | bytes 393224 | tf_op jit(solution)/shard_map/ppermute | solution.py:609
  28.2 29.4 %collective-permute-start.9 = (f32[16,72,128]{2,1,0:T(8,128)}, f32[16,72,128]{2,1,0:T(8,128)S(1)}, u32[]{:S(2)}, u32[]{:S(2)}) collective-permute-start(f32[16,72,128]{2,1,0:T(8,128)} %get-tuple-element.38), channel_id=1, source_target_pairs={{0,4},{4,8},{8,12},{12,16},{16,20},{20,24},{24,28},{1,5},{5,9},{9,... | collective-permute-start | bytes 1769480 | tf_op jit(solution)/shard_map/ppermute | solution.py:610
  30.4 28.7 %collective-permute-start.10 = (f32[16,72,128]{2,1,0:T(8,128)}, f32[16,72,128]{2,1,0:T(8,128)S(1)}, u32[]{:S(2)}, u32[]{:S(2)}) collective-permute-start(f32[16,72,128]{2,1,0:T(8,128)} %get-tuple-element.39), channel_id=1, source_target_pairs={{4,0},{8,4},{12,8},{16,12},{20,16},{24,20},{28,24},{5,1},{9,5},{13... | collective-permute-start | bytes 1769480 | tf_op jit(solution)/shard_map/ppermute | solution.py:611
  34.5 17.0 %copy-start.2 = (f32[128,8,128]{2,1,0:T(8,128)}, f32[128,8,128]{2,1,0:T(8,128)S(1)}, u32[]{:S(2)}) copy-start(f32[128,8,128]{2,1,0:T(8,128)S(1)} %add.16.mine_ref) | copy-start | bytes 1572868
  34.5 17.0 %collective-permute-start.12 = (f32[128,8,128]{2,1,0:T(8,128)S(1)}, f32[128,8,128]{2,1,0:T(8,128)}, u32[]{:S(2)}, u32[]{:S(2)}) collective-permute-start(f32[128,8,128]{2,1,0:T(8,128)S(1)} %add.16.mine_ref), channel_id=1, source_target_pairs={{0,1},{1,0},{2,3},{3,2},{4,5},{5,4},{6,7},{7,6},{8,9},{9,8},{10,11... | collective-permute-start | bytes 1572872 | tf_op jit(solution)/shard_map/ppermute | solution.py:615
  36.4 7.9 %collective-permute-start.7 = (f32[64,8,128]{2,1,0:T(8,128)S(1)}, f32[64,8,128]{2,1,0:T(8,128)S(1)}, u32[]{:S(2)}, u32[]{:S(2)}) collective-permute-start(f32[64,8,128]{2,1,0:T(8,128)S(1)} %join_high.1.a_ref), channel_id=1, source_target_pairs={{0,2},{1,3},{2,0},{3,1},{4,6},{5,7},{6,4},{7,5},{8,10},{9,11},{10,... | collective-permute-start | bytes 786440 | tf_op jit(solution)/shard_map/ppermute | solution.py:614
  36.5 13.3 %collective-permute-start.4 = (f32[64,8,128]{2,1,0:T(8,128)S(1)}, f32[64,8,128]{2,1,0:T(8,128)S(1)}, u32[]{:S(2)}, u32[]{:S(2)}) collective-permute-start(f32[64,8,128]{2,1,0:T(8,128)S(1)} %join_low.1.a_ref), channel_id=1, source_target_pairs={{0,2},{1,3},{2,0},{3,1},{4,6},{5,7},{6,4},{7,5},{8,10},{9,11},{10,... | collective-permute-start | bytes 786440 | tf_op jit(solution)/shard_map/ppermute | solution.py:614
  44.3 17.3 %copy-start.4 = (f32[64,8,128]{2,1,0:T(8,128)}, f32[64,8,128]{2,1,0:T(8,128)S(1)}, u32[]{:S(2)}) copy-start(f32[64,8,128]{2,1,0:T(8,128)S(1)} %add.15.m_high) | copy-start | bytes 786436
  44.3 14.8 %collective-permute-start.8 = (f32[64,8,128]{2,1,0:T(8,128)S(1)}, f32[64,8,128]{2,1,0:T(8,128)S(1)}, u32[]{:S(2)}, u32[]{:S(2)}) collective-permute-start(f32[64,8,128]{2,1,0:T(8,128)S(1)} %add.15.m_high), channel_id=1, source_target_pairs={{0,1},{1,0},{2,3},{3,2},{4,5},{5,4},{6,7},{7,6},{8,9},{9,8},{10,11... | collective-permute-start | bytes 786440 | tf_op jit(solution)/shard_map/ppermute | solution.py:615
  49.9 11.7 %copy-start.5 = (f32[64,8,128]{2,1,0:T(8,128)}, f32[64,8,128]{2,1,0:T(8,128)S(1)}, u32[]{:S(2)}) copy-start(f32[64,8,128]{2,1,0:T(8,128)S(1)} %add.14.m_low) | copy-start | bytes 786436
  49.9 9.2 %collective-permute-start.5 = (f32[64,8,128]{2,1,0:T(8,128)S(1)}, f32[64,8,128]{2,1,0:T(8,128)S(1)}, u32[]{:S(2)}, u32[]{:S(2)}) collective-permute-start(f32[64,8,128]{2,1,0:T(8,128)S(1)} %add.14.m_low), channel_id=1, source_target_pairs={{0,1},{1,0},{2,3},{3,2},{4,5},{5,4},{6,7},{7,6},{8,9},{9,8},{10,11... | collective-permute-start | bytes 786440 | tf_op jit(solution)/shard_map/ppermute | solution.py:615
  57.6 4.0 %copy-start = (f32[16,72,128]{2,1,0:T(8,128)}, f32[16,72,128]{2,1,0:T(8,128)S(1)}, u32[]{:S(2)}) copy-start(f32[16,72,128]{2,1,0:T(8,128)S(1)} %collective-permute-done.9.refs_0_) | copy-start | bytes 1769476
  59.1 2.5 %copy-start.1 = (f32[16,72,128]{2,1,0:T(8,128)}, f32[16,72,128]{2,1,0:T(8,128)S(1)}, u32[]{:S(2)}) copy-start(f32[16,72,128]{2,1,0:T(8,128)S(1)} %collective-permute-done.10.refs_1_) | copy-start | bytes 1769476
  59.1 2.5 %copy-start.6 = (f32[64,8,128]{2,1,0:T(8,128)}, f32[64,8,128]{2,1,0:T(8,128)S(1)}, u32[]{:S(2)}) copy-start(f32[64,8,128]{2,1,0:T(8,128)S(1)} %collective-permute-done.8.refs_3_.o_high) | copy-start | bytes 786436
  59.1 2.5 %copy-start.7 = (f32[64,8,128]{2,1,0:T(8,128)}, f32[64,8,128]{2,1,0:T(8,128)S(1)}, u32[]{:S(2)}) copy-start(f32[64,8,128]{2,1,0:T(8,128)S(1)} %collective-permute-done.5.refs_2_.o_low) | copy-start | bytes 786436

commit v5 on v4

--- a/solution.py
+++ b/solution.py
@@ -129,10 +129,10 @@
 
 def advance_kernel(plan, cuts, group, meta_ref, sx_ref, sy_ref, fx_ref, fy_ref, inflow_ref, wall_ref,
                    heights_ref, pop_ref, *refs):
-    planes_ref, mine_ref, theirs_ref = refs[:3]
-    packs = refs[3 : 3 + len(cuts)]
-    (padded, planes_buf, outer, moments, low_pack, high_pack, bars, sem_in, sem_planes, sem_out) = refs[
-        3 + len(cuts) :
+    planes_ref, mine_ref, theirs_ref, more_ref = refs[:4]
+    packs = refs[4 : 4 + len(cuts)]
+    (padded, planes_buf, outer, last_row, low_pack, high_pack, bars, sem_in, sem_planes, sem_out) = refs[
+        4 + len(cuts) :
     ]
     planes, row_tiles, lane_tiles = pop_ref.shape[:3]
     half = lane_tiles // 2
@@ -157,8 +157,16 @@
 
     lax.fori_loop(0, planes // group, start, 0)
     prepare_heights(heights_ref, bars)
-    for slot in range(2):
-        moments[slot, plan.tile : plan.tile + 4] = jnp.zeros((4, ROW, LANE), F32)
+    last_row[...] = jnp.zeros_like(last_row)
+
+    def put_sums(h, first_block, sums):
+        for is_mine, ref in ((True, mine_ref), (False, theirs_ref)):
+
+            @pl.when((core == h) == is_mine)
+            def _():
+                for n, value in enumerate(sums):
+                    ref[first_block + n] = value
+
 
     def out_copy(v):
         return pltpu.make_async_copy(planes_buf.at[v], planes_ref.at[v], sem_planes.at[v])
@@ -195,15 +203,12 @@
 
             def put(t, value):
                 row = jnp.where(row0 + rows + ROW < bars[t], 0.0, value)
-                slot, r = jnp.bitwise_xor(core, t // half), t % half
+                h, r = divmod(t, half)
                 for m in range(4):
-                    n = plan.tile + m
-                    total = moments[slot, n, r : r + 1, :] + (row * factors[m])[0:1, :]
-                    moments[slot, n, r : r + 1, :] = total
+                    total = last_row[h, m, r : r + 1, :] + (row * factors[m])[0:1, :]
+                    last_row[h, m, r : r + 1, :] = total
 
             advect(padded, v, scalars, [(PAD + rows + ROW, put)])
-            for t in range(lane_tiles):
-                low_pack[t, pl.ds(low + 8, 1), :] = padded[v, t + 1, PAD + rows - 1 : PAD + rows, :]
 
         @pl.when(up)
         def _():
@@ -223,15 +228,26 @@
 
         return low + low_need(shift), high + high_need(shift)
 
-    lax.fori_loop(0, planes, one, (jnp.int32(0), jnp.int32(0)))
-    packing = []
-    for n, (pack, begin, end) in enumerate(cuts):
+    needs = lax.fori_loop(0, planes, one, (jnp.int32(0), jnp.int32(0)))
+    sent = [end for _, begin, end in cuts if begin == 0]
+    overflows = (needs[0] > sent[0]) | (needs[1] > sent[1])
+    more_ref[0] = jnp.where(overflows, 1, 0)
+
+    def pack_copy(n):
+        pack, begin, end = cuts[n]
         source = (low_pack, high_pack)[pack].at[:, begin:end, :]
-        packing.append(pltpu.make_async_copy(source, packs[n], sem_out.at[2 + n]))
-        packing[-1].start()
-
+        return pltpu.make_async_copy(source, packs[n], sem_out.at[n])
+
+    def each_pack(act):
+        for n, (_, begin, _) in enumerate(cuts):
+            if begin == 0:
+                act(pack_copy(n))
+            else:
+                pl.when(overflows)(lambda n=n: act(pack_copy(n)))
+
+    each_pack(lambda copy: copy.start())
     for h in range(2):
-        slot = jnp.bitwise_xor(core, h)
+        put_sums(h, plan.tile, [last_row[h, m] for m in range(4)])
         for rising in (True, False):
             for part in range(2):
                 tiles = range(h * half + part * half // 2, h * half + (part + 1) * half // 2)
@@ -245,37 +261,26 @@
                         f = outer[v, t]
                         terms = [f * w for w in factors]
                         sums[n] = [b if a is None else a + b for a, b in zip(sums[n], terms)]
-                begin = plan.starts[0 if rising else 1]
-                for n, t in enumerate(tiles):
-                    for m in range(4):
-                        moments[slot, begin + m * half + t - h * half] = sums[n][m]
+                begin = plan.starts[0 if rising else 1] + part * half // 2
+                for m in range(4):
+                    put_sums(h, begin + m * half, [sums[n][m] for n in range(len(tiles))])
     weights = [velocity(sx_ref, sy_ref, fx_ref, fy_ref, v) for v in range(planes)]
 
     def step(j, _):
         begin = plan.start(j)
         for h in range(2):
             sums = sum_moments(planes_buf, j, weights, range(h * half, (h + 1) * half))
-            slot = jnp.bitwise_xor(core, h)
-            for t in range(half):
-                for m in range(4):
-                    moments[slot, begin + m * half + t] = sums[t][m]
+            put_sums(h, begin, [sums[t][m] for m in range(4) for t in range(half)])
         return 0
 
     lax.fori_loop(0, row_tiles, step, 0)
-    copies = [
-        pltpu.make_async_copy(moments.at[1], theirs_ref, sem_out.at[1]),
-        pltpu.make_async_copy(moments.at[0], mine_ref, sem_out.at[0]),
-    ]
-    for copy in copies:
-        copy.start()
 
     def finish(v, _):
         out_copy(v).wait()
         return 0
 
     lax.fori_loop(0, planes, finish, 0)
-    for copy in packing + copies:
-        copy.wait()
+    each_pack(lambda copy: copy.wait())
 
 
 def advance(plan, meta, small, heights, pop, cuts):
@@ -285,21 +290,21 @@
     half_sums = jax.ShapeDtypeStruct((blocks, ROW, LANE), F32)
     return pl.pallas_call(
         functools.partial(advance_kernel, plan, cuts, group),
-        out_shape=[jax.ShapeDtypeStruct(pop.shape, F32), half_sums, half_sums]
-        + [jax.ShapeDtypeStruct((lane_tiles, end - begin, LANE), F32) for _, begin, end in cuts],
-        in_specs=[SMEM_SPEC] * 7 + [VMEM_SPEC, ANY_SPEC],
-        out_specs=[ANY_SPEC] * (3 + len(cuts)),
+        out_shape=[pltpu.HBM(pop.shape, F32), half_sums, half_sums, jax.ShapeDtypeStruct((1,), jnp.int32)]
+        + [pltpu.HBM((lane_tiles, end - begin, LANE), F32) for _, begin, end in cuts],
+        in_specs=[SMEM_SPEC] * 7 + [VMEM_SPEC, HBM_SPEC],
+        out_specs=[HBM_SPEC, VMEM_SPEC, VMEM_SPEC, SMEM_SPEC] + [HBM_SPEC] * len(cuts),
         scratch_shapes=[
             pltpu.VMEM((planes, lane_tiles + 2, PAD + row_tiles * ROW + ROW, LANE), F32),
             pltpu.VMEM((planes, row_tiles, lane_tiles, ROW, LANE), F32),
             pltpu.VMEM((planes, lane_tiles, ROW, LANE), F32),
-            pltpu.VMEM((2, blocks, ROW, LANE), F32),
+            pltpu.VMEM((2, 4, ROW, LANE), F32),
             pltpu.VMEM((lane_tiles, planes * LOW_ROWS + 16, LANE), F32),
             pltpu.VMEM((lane_tiles, planes * HIGH_ROWS + 16, LANE), F32),
             pltpu.VMEM((lane_tiles, ROW, LANE), jnp.int32),
             pltpu.SemaphoreType.DMA((planes // group, row_tiles)),
             pltpu.SemaphoreType.DMA((planes,)),
-            pltpu.SemaphoreType.DMA((2 + len(cuts),)),
+            pltpu.SemaphoreType.DMA((len(cuts),)),
         ],
         compiler_params=params(58),
         name="advance",
@@ -325,9 +330,11 @@
     )(mine, received)
 
 
-def join_low_kernel(own_ref, low_ref, out_ref):
+def join_low_kernel(own_ref, low_ref, *refs):
+    out_ref = refs[-1]
     tile = own_ref.shape[0] // 2
     half = tile // 4
+    out_ref[2 * tile :] = jnp.zeros((out_ref.shape[0] - 2 * tile, ROW, LANE), F32)
     out_ref[:tile] = own_ref[:tile] + low_ref[:tile]
     top = lax.broadcasted_iota(jnp.int32, (ROW, LANE), 0) == 0
     for m in range(4):
@@ -337,43 +344,29 @@
             out_ref[index] = own_ref[index] + jnp.where(top, row, 0.0)
 
 
-def add_kernel(a_ref, b_ref, out_ref):
-    out_ref[...] = a_ref[...] + b_ref[...]
-
-
-def join_high_kernel(own_ref, high_ref, out_ref):
+def add_kernel(a_ref, b_ref, *refs):
+    refs[-1][...] = a_ref[...] + b_ref[...]
+
+
+def join_high_kernel(own_ref, high_ref, *refs):
+    out_ref = refs[-1]
     tile = high_ref.shape[0]
+    out_ref[2 * tile :] = jnp.zeros((out_ref.shape[0] - 2 * tile, ROW, LANE), F32)
     out_ref[:tile] = own_ref[:tile]
-    out_ref[tile:] = own_ref[tile:] + high_ref[...]
-
-
-def small_call(kernel, name, *operands):
+    out_ref[tile : 2 * tile] = own_ref[tile:] + high_ref[...]
+
+
+def small_call(kernel, name, a, b, after=(), extra=0):
+    operands = a, b, *after
+    shape = (a.shape[0] + extra, *a.shape[1:])
     return pl.pallas_call(
         kernel,
-        out_shape=jax.ShapeDtypeStruct(operands[0].shape, F32),
-        in_specs=[VMEM_SPEC] * len(operands),
+        out_shape=jax.ShapeDtypeStruct(shape, F32),
+        in_specs=[VMEM_SPEC] * 2 + [ANY_SPEC] * len(after),
         out_specs=VMEM_SPEC,
         compiler_params=params(8),
         name=name,
     )(*operands)
-
-
-def overflow_kernel(limits, sy_ref, *refs):
-    low, high = low_need(sy_ref[0]), high_need(sy_ref[0])
-    for v in range(1, sy_ref.shape[0]):
-        low, high = low + low_need(sy_ref[v]), high + high_need(sy_ref[v])
-    refs[-1][0] = jnp.where((low > limits[0]) | (high > limits[1]), 1, 0)
-
-
-def overflow(shift_y, limits, after):
-    return pl.pallas_call(
-        functools.partial(overflow_kernel, limits),
-        out_shape=jax.ShapeDtypeStruct((1,), jnp.int32),
-        in_specs=[SMEM_SPEC] + [ANY_SPEC] * len(after),
-        out_specs=SMEM_SPEC,
-        compiler_params=params(8),
-        name="overflow",
-    )(shift_y, *after)[0]
 
 
 def profile(density, flux_x, flux_y, energy, factor):
@@ -593,6 +586,7 @@
     factor = impact_frequency_factor.reshape(1)
     bars = heights.reshape(lane_tiles, LANE)
     pop = populations.reshape(planes, row_tiles, ROW, lane_tiles, LANE).transpose(0, 1, 3, 2, 4)
+    pop = pltpu.with_memory_space_constraint(pop, pltpu.HBM)
     low_sent, high_sent = min(LOW_SENT, planes * LOW_ROWS), min(HIGH_SENT, planes * HIGH_ROWS)
     cuts = [
         (0, 0, low_sent),
@@ -602,7 +596,7 @@
     ]
     plan = Plan(row_tiles, lane_tiles // 2)
 
-    moved, mine, theirs, *packs = advance(plan, meta, small, bars, pop, cuts)
+    moved, mine, theirs, more_needed, *packs = advance(plan, meta, small, bars, pop, cuts)
     received = lax.ppermute(theirs, "vel", partner)
     up, down, inside, edge_low, edge_high = fold(mine, received, plan.sizes)
     from_low = lax.ppermute(up, "space", forward)
@@ -610,22 +604,19 @@
     low_first = lax.ppermute(packs[0], "space", forward)
     high_first = lax.ppermute(packs[1], "space", backward)
 
-    def total(sums):
-        whole = small_call(add_kernel, "add", sums, lax.ppermute(sums, "vel", across))
+    def total(sums, after=()):
+        whole = small_call(add_kernel, "add", sums, lax.ppermute(sums, "vel", across), after)
         return whole, lax.ppermute(whole, "vel", partner)
-
-    sums_inside = total(inside)
-    sums_low = total(small_call(join_low_kernel, "join_low", edge_low, from_low))
-    sums_high = total(small_call(join_high_kernel, "join_high", edge_high, from_high))
-
-    out, done = relax_inside(plan.inside, meta, small, factor, sums_inside, moved)
-    after = low_first, high_first, sums_low[1], sums_high[1], done
-    needed = overflow(shift_y, (low_sent, high_sent), after)
 
     def send_more(low, high):
         return lax.ppermute(low, "space", forward), lax.ppermute(high, "space", backward)
 
-    more = lax.cond(needed > 0, send_more, lambda low, high: (low, high), packs[2], packs[3])
+    more = lax.cond(more_needed[0] > 0, send_more, lambda low, high: (low, high), packs[2], packs[3])
+    sums_inside = total(inside)
+    out, done = relax_inside(plan.inside, meta, small, factor, sums_inside, moved)
+    sums_low = total(small_call(join_low_kernel, "join_low", edge_low, from_low, (), 1))
+    sums_high = total(small_call(join_high_kernel, "join_high", edge_high, from_high, (), 1))
+
     halo = low_first, high_first, *more
     out = relax_edges(meta, small, factor, bars, sums_low + sums_high, moved, halo, cuts, out)
     return out.transpose(0, 1, 3, 2, 4).reshape(planes, row_count, col_count)

time: 71.4 us -> 70.6 us (0.989)
  waiting for transfers between devices: 15.1 us -> 8.95 us
  starting transfers between devices: 20.1 us -> 26.2 us
  Pallas kernels: 32.4 us -> 30.7 us
  local copies, waits for them, and re-layouts: 1.36 us -> 2.12 us
    ppermute x3, waiting for transfers between devices: 10.5 us -> 2.65 us  [total(): lax.ppermute(sums, 'vel', across)]
    ppermute x3, starting transfers between devices: 4.12 us -> 10.2 us  [total(): return (whole, lax.ppermute(whole, 'vel', partner))]
    pallas_call x6 -> x5, Pallas kernels: 1.95 us -> 0.17 us  [small_call(): pl.pallas_call(kernel, out_shape=jax.ShapeDtypeStruct(shape, F32), in_spe...]
    ppermute x1, waiting for transfers between devices: 1.49 us -> 2.83 us  [per_device(): high_first = lax.ppermute(packs[1], 'space', backward)]
    unnamed x18 -> x16, local copies, waits for them, and re-layouts: 1.36 us -> 2.12 us
where the time goes in v5:
time: 70.6 us; the launch traced here: 70.1 us
  Pallas kernels  30.7 us (43%)
  starting transfers between devices  26.2 us (37%)
  waiting for transfers between devices  8.95 us (13%)
  local copies, waits for them, and re-layouts  2.12 us (3%)
  between operations  1.46 us (2%)
    pallas_call x1, Pallas kernels, advance(): pl.pallas_call(functools.partial(advance_kernel, plan, cuts, group), out_...  15 us
    ppermute x3, starting transfers between devices, total(): return (whole, lax.ppermute(whole, 'vel', partner))  10.2 us
    pallas_call x1, Pallas kernels, relax_edges(): pl.pallas_call(functools.partial(relax_edges_kernel, cuts), out_shape=jax...  9.5 us
    pallas_call x1, Pallas kernels, relax_inside(): pl.pallas_call(functools.partial(relax_kernel, tiles), out_shape=[jax.Sha...  5.88 us
    ppermute x1, starting transfers between devices, per_device(): high_first = lax.ppermute(packs[1], 'space', backward)  3.96 us
    ppermute x1, starting transfers between devices, per_device(): from_low = lax.ppermute(up, 'space', forward)  3.11 us
    ppermute x1, starting transfers between devices, per_device(): from_high = lax.ppermute(down, 'space', backward)  3.06 us
    ppermute x1, waiting for transfers between devices, per_device(): received = lax.ppermute(theirs, 'vel', partner)  2.9 us
  transfers between devices with their start and end apart: 11, of which 5 were waited for; matrix products, arithmetic and copies ran while one was open for 0% of the time, Pallas kernels for 9%

profile of v5, /device:TPU:9, one launch (start us, length us, event | category | flops | bytes accessed | tf_op | source)
XLA Modules:
  0.0 70.1 jit_solution(4476322998118144848)
XLA Ops:
  0.0 0.7 pad_add_fusion.meta_ref
  0.7 15.0 %advance.1 = (f32[16,8,16,8,128]{4,3,2,1,0:T(8,128)}, f32[324,8,128]{2,1,0:T(8,128)}, f32[324,8,128]{2,1,0:T(8,128)}, s32[1]{0:T(128)}, f32[16,72,128]{2,1,0:T(8...) custom-call(s32[4]{0:T(128)} %pad_add_fusion.meta_ref, s32[16]{0:T(128)} %sx_ref.5, ...), custom_call_target="tpu_custom_call" | custom-call | tf_op jit(solution)/shard_map/advance/pallas_call | solution.py:291
  15.7 0.8 %collective-permute-start.2 = (f32[324,8,128]{2,1,0:T(8,128)}, f32[324,8,128]{2,1,0:T(8,128)S(1)}, u32[]{:S(2)}, u32[]{:S(2)}) collective-permute-start(f32[324,8,128]{2,1,0:T(8,128)} %get-tuple-element.32), channel_id=1, source_target_pairs={{0,1},{1,0},{2,3},{3,2},{4,5},{5,4},{6,7},{7,6},{8,9},{9,8},{10,11... | collective-permute-start | bytes 3981320 | tf_op jit(solution)/shard_map/ppermute | solution.py:600
  16.5 2.9 %collective-permute-done.2.received_ref = f32[324,8,128]{2,1,0:T(8,128)S(1)} collective-permute-done((f32[324,8,128]{2,1,0:T(8,128)}, f32[324,8,128]{2,1,0:T(8,128)S(1)}, u32[]{:S(2)}, u32[]{:S(2)}) %collective-permute-start.2) | collective-permute-done | bytes 1327136 | tf_op jit(solution)/shard_map/ppermute | solution.py:600
  19.4 0.0 copy-start.1
  19.4 1.3 %copy-done.1 = f32[324,8,128]{2,1,0:T(8,128)S(1)} copy-done((f32[324,8,128]{2,1,0:T(8,128)S(1)}, f32[324,8,128]{2,1,0:T(8,128)}, u32[]{:S(2)}) %copy-start.1) | copy-done | bytes 1327128
  20.8 0.1 fold.1
  20.9 1.2 %collective-permute-start.11 = (f32[128,8,128]{2,1,0:T(8,128)S(1)}, f32[128,8,128]{2,1,0:T(8,128)S(1)}, u32[]{:S(2)}, u32[]{:S(2)}) collective-permute-start(f32[128,8,128]{2,1,0:T(8,128)S(1)} %get-tuple-element.45.a_ref), channel_id=1, source_target_pairs={{0,2},{1,3},{2,0},{3,1},{4,6},{5,7},{6,4},{7,5},{8,10},{9,11},{10,... | collective-permute-start | bytes 1572872 | tf_op jit(solution)/shard_map/ppermute | solution.py:608
  22.1 3.1 %collective-permute-start.3 = (f32[36,8,128]{2,1,0:T(8,128)S(1)}, f32[36,8,128]{2,1,0:T(8,128)S(1)}, u32[]{:S(2)}, u32[]{:S(2)}) collective-permute-start(f32[36,8,128]{2,1,0:T(8,128)S(1)} %get-tuple-element.34), channel_id=1, source_target_pairs={{0,4},{4,8},{8,12},{12,16},{16,20},{20,24},{24,28},{1,5},{5,9},{9,... | collective-permute-start | bytes 442376 | tf_op jit(solution)/shard_map/ppermute | solution.py:602
  25.2 3.1 %collective-permute-start.6 = (f32[32,8,128]{2,1,0:T(8,128)S(1)}, f32[32,8,128]{2,1,0:T(8,128)S(1)}, u32[]{:S(2)}, u32[]{:S(2)}) collective-permute-start(f32[32,8,128]{2,1,0:T(8,128)S(1)} %get-tuple-element.36), channel_id=1, source_target_pairs={{4,0},{8,4},{12,8},{16,12},{20,16},{24,20},{28,24},{5,1},{9,5},{13... | collective-permute-start | bytes 393224 | tf_op jit(solution)/shard_map/ppermute | solution.py:603
  28.9 2.2 %collective-permute-start.9 = (f32[16,72,128]{2,1,0:T(8,128)}, f32[16,72,128]{2,1,0:T(8,128)S(1)}, u32[]{:S(2)}, u32[]{:S(2)}) collective-permute-start(f32[16,72,128]{2,1,0:T(8,128)} %get-tuple-element.38), channel_id=1, source_target_pairs={{0,4},{4,8},{8,12},{12,16},{16,20},{20,24},{24,28},{1,5},{5,9},{9,... | collective-permute-start | bytes 1769480 | tf_op jit(solution)/shard_map/ppermute | solution.py:604
  31.1 4.0 %collective-permute-start.10 = (f32[16,72,128]{2,1,0:T(8,128)}, f32[16,72,128]{2,1,0:T(8,128)S(1)}, u32[]{:S(2)}, u32[]{:S(2)}) collective-permute-start(f32[16,72,128]{2,1,0:T(8,128)} %get-tuple-element.39), channel_id=1, source_target_pairs={{4,0},{8,4},{12,8},{16,12},{20,16},{24,20},{28,24},{5,1},{9,5},{13... | collective-permute-start | bytes 1769480 | tf_op jit(solution)/shard_map/ppermute | solution.py:605
  35.1 0.0 collective-permute-done.6.high_ref
  35.1 0.4 collective-permute-start.7
  35.6 0.0 collective-permute-done.3.low_ref
  35.6 0.0 copy-start.7
  35.6 1.2 %collective-permute-start.4 = (f32[65,8,128]{2,1,0:T(8,128)S(1)}, f32[65,8,128]{2,1,0:T(8,128)S(1)}, u32[]{:S(2)}, u32[]{:S(2)}) collective-permute-start(f32[65,8,128]{2,1,0:T(8,128)S(1)} %join_low.1.a_ref), channel_id=1, source_target_pairs={{0,2},{1,3},{2,0},{3,1},{4,6},{5,7},{6,4},{7,5},{8,10},{9,11},{10,... | collective-permute-start | bytes 798728 | tf_op jit(solution)/shard_map/ppermute | solution.py:608
  36.8 0.0 collective-permute-done.11.b_ref
  36.8 0.1 add.16.mine_ref
  36.9 0.0 copy-start
  36.9 0.0 copy-start.6
  36.9 2.4 %collective-permute-start.12 = (f32[128,8,128]{2,1,0:T(8,128)S(1)}, f32[128,8,128]{2,1,0:T(8,128)}, u32[]{:S(2)}, u32[]{:S(2)}) collective-permute-start(f32[128,8,128]{2,1,0:T(8,128)S(1)} %add.16.mine_ref), channel_id=1, source_target_pairs={{0,1},{1,0},{2,3},{3,2},{4,5},{5,4},{6,7},{7,6},{8,9},{9,8},{10,11... | collective-permute-start | bytes 1572872 | tf_op jit(solution)/shard_map/ppermute | solution.py:609
  39.3 2.0 %collective-permute-done.7.b_ref = f32[65,8,128]{2,1,0:T(8,128)S(1)} collective-permute-done((f32[65,8,128]{2,1,0:T(8,128)S(1)}, f32[65,8,128]{2,1,0:T(8,128)S(1)}, u32[]{:S(2)}, u32[]{:S(2)}) %collective-permute-start.7) | collective-permute-done | bytes 266272 | tf_op jit(solution)/shard_map/ppermute | solution.py:608
  41.4 0.0 copy-start.2
  41.4 5.1 %collective-permute-start.8 = (f32[65,8,128]{2,1,0:T(8,128)S(1)}, f32[65,8,128]{2,1,0:T(8,128)}, u32[]{:S(2)}, u32[]{:S(2)}) collective-permute-start(f32[65,8,128]{2,1,0:T(8,128)S(1)} %add.15.m_high), channel_id=1, source_target_pairs={{0,1},{1,0},{2,3},{3,2},{4,5},{5,4},{6,7},{7,6},{8,9},{9,8},{10,11... | collective-permute-start | bytes 798728 | tf_op jit(solution)/shard_map/ppermute | solution.py:609
  46.4 0.6 collective-permute-done.4.b_ref
  47.1 0.0 copy-start.3
  47.1 2.8 %collective-permute-start.5 = (f32[65,8,128]{2,1,0:T(8,128)S(1)}, f32[65,8,128]{2,1,0:T(8,128)}, u32[]{:S(2)}, u32[]{:S(2)}) collective-permute-start(f32[65,8,128]{2,1,0:T(8,128)S(1)} %add.14.m_low), channel_id=1, source_target_pairs={{0,1},{1,0},{2,3},{3,2},{4,5},{5,4},{6,7},{7,6},{8,9},{9,8},{10,11... | collective-permute-start | bytes 798728 | tf_op jit(solution)/shard_map/ppermute | solution.py:609
  50.5 0.0 collective-permute-done.12.other_ref
  50.5 0.0 copy-done
  50.5 5.9 %relax_inside.1 = (f32[16,8,16,8,128]{4,3,2,1,0:T(8,128)}, s32[1]{0:T(128)}) custom-call(s32[4]{0:T(128)} %pad_add_fusion.meta_ref, s32[16]{0:T(128)} %sx_ref.5, s32[16]{0:T(128)} %sy_ref.5, f32[16]{0:T(128)} %fx_ref.5, f32[16]{0:T(128)} %fy_ref.5, f32[1]{0:T(128)} %bitcast.13.factor_ref, f32[128,8,128]{2,1,0:T(8,128)} %copy-done, ...), custom_call_target="tpu_custom_call" | custom-call | tf_op jit(solution)/shard_map/relax_inside/pallas_call | solution.py:443
  56.4 0.6 collective-permute-done.9.refs_0_
  57.0 0.0 copy-start.4
  57.0 2.8 %collective-permute-done.10.refs_1_ = f32[16,72,128]{2,1,0:T(8,128)S(1)} collective-permute-done((f32[16,72,128]{2,1,0:T(8,128)}, f32[16,72,128]{2,1,0:T(8,128)S(1)}, u32[]{:S(2)}, u32[]{:S(2)}) %collective-permute-start.10) | collective-permute-done | bytes 589856 | tf_op jit(solution)/shard_map/ppermute | solution.py:605
  59.8 0.0 copy-start.5
  59.8 0.0 collective-permute-done.8.o_high
  59.8 0.0 collective-permute-done.5.o_low
  59.8 0.0 copy-done.2
  59.8 0.0 copy-done.3
  59.8 0.0 copy-done.4
  59.8 0.8 %copy-done.5 = f32[16,72,128]{2,1,0:T(8,128)} copy-done((f32[16,72,128]{2,1,0:T(8,128)}, f32[16,72,128]{2,1,0:T(8,128)S(1)}, u32[]{:S(2)}) %copy-start.5) | copy-done | bytes 589848
  60.6 0.0 copy-done.7
  60.6 0.0 copy-done.6
  60.6 9.5 %relax_edges.1 = f32[16,8,16,8,128]{4,3,2,1,0:T(8,128)} custom-call(s32[4]{0:T(128)} %pad_add_fusion.meta_ref, s32[16]{0:T(128)} %sx_ref.5, s32[16]{0:T(128)} %sy_ref.5, f32[16]{0:T(128)} %fx_ref.5, f32[16]{0:T(128)} %fy_ref.5, f32[16]{0:T(128)} %inflow_ref.3, f32[1]{0:T(128)} %bitcast.14.factor_ref, ...), custom_call_target="tpu_custom_call", output_to_operand_aliasing={{}: (17, {})} | custom-call | tf_op jit(solution)/shard_map/relax_edges/pallas_call | solution.py:552
  (5 shorter events, 0.1 us)
Async XLA Ops:
  15.7 3.7 %collective-permute-start.2 = (f32[324,8,128]{2,1,0:T(8,128)}, f32[324,8,128]{2,1,0:T(8,128)S(1)}, u32[]{:S(2)}, u32[]{:S(2)}) collective-permute-start(f32[324,8,128]{2,1,0:T(8,128)} %get-tuple-element.32), channel_id=1, source_target_pairs={{0,1},{1,0},{2,3},{3,2},{4,5},{5,4},{6,7},{7,6},{8,9},{9,8},{10,11... | collective-permute-start | bytes 3981320 | tf_op jit(solution)/shard_map/ppermute | solution.py:600
  19.4 1.3 %copy-start.1 = (f32[324,8,128]{2,1,0:T(8,128)S(1)}, f32[324,8,128]{2,1,0:T(8,128)}, u32[]{:S(2)}) copy-start(f32[324,8,128]{2,1,0:T(8,128)} %get-tuple-element.31.mine_ref) | copy-start | bytes 3981316
  20.9 15.9 %collective-permute-start.11 = (f32[128,8,128]{2,1,0:T(8,128)S(1)}, f32[128,8,128]{2,1,0:T(8,128)S(1)}, u32[]{:S(2)}, u32[]{:S(2)}) collective-permute-start(f32[128,8,128]{2,1,0:T(8,128)S(1)} %get-tuple-element.45.a_ref), channel_id=1, source_target_pairs={{0,2},{1,3},{2,0},{3,1},{4,6},{5,7},{6,4},{7,5},{8,10},{9,11},{10,... | collective-permute-start | bytes 1572872 | tf_op jit(solution)/shard_map/ppermute | solution.py:608
  22.1 13.5 %collective-permute-start.3 = (f32[36,8,128]{2,1,0:T(8,128)S(1)}, f32[36,8,128]{2,1,0:T(8,128)S(1)}, u32[]{:S(2)}, u32[]{:S(2)}) collective-permute-start(f32[36,8,128]{2,1,0:T(8,128)S(1)} %get-tuple-element.34), channel_id=1, source_target_pairs={{0,4},{4,8},{8,12},{12,16},{16,20},{20,24},{24,28},{1,5},{5,9},{9,... | collective-permute-start | bytes 442376 | tf_op jit(solution)/shard_map/ppermute | solution.py:602
  25.2 9.9 %collective-permute-start.6 = (f32[32,8,128]{2,1,0:T(8,128)S(1)}, f32[32,8,128]{2,1,0:T(8,128)S(1)}, u32[]{:S(2)}, u32[]{:S(2)}) collective-permute-start(f32[32,8,128]{2,1,0:T(8,128)S(1)} %get-tuple-element.36), channel_id=1, source_target_pairs={{4,0},{8,4},{12,8},{16,12},{20,16},{24,20},{28,24},{5,1},{9,5},{13... | collective-permute-start | bytes 393224 | tf_op jit(solution)/shard_map/ppermute | solution.py:603
  28.9 28.1 %collective-permute-start.9 = (f32[16,72,128]{2,1,0:T(8,128)}, f32[16,72,128]{2,1,0:T(8,128)S(1)}, u32[]{:S(2)}, u32[]{:S(2)}) collective-permute-start(f32[16,72,128]{2,1,0:T(8,128)} %get-tuple-element.38), channel_id=1, source_target_pairs={{0,4},{4,8},{8,12},{12,16},{16,20},{20,24},{24,28},{1,5},{5,9},{9,... | collective-permute-start | bytes 1769480 | tf_op jit(solution)/shard_map/ppermute | solution.py:604
  31.1 28.7 %collective-permute-start.10 = (f32[16,72,128]{2,1,0:T(8,128)}, f32[16,72,128]{2,1,0:T(8,128)S(1)}, u32[]{:S(2)}, u32[]{:S(2)}) collective-permute-start(f32[16,72,128]{2,1,0:T(8,128)} %get-tuple-element.39), channel_id=1, source_target_pairs={{4,0},{8,4},{12,8},{16,12},{20,16},{24,20},{28,24},{5,1},{9,5},{13... | collective-permute-start | bytes 1769480 | tf_op jit(solution)/shard_map/ppermute | solution.py:605
  35.1 6.2 %collective-permute-start.7 = (f32[65,8,128]{2,1,0:T(8,128)S(1)}, f32[65,8,128]{2,1,0:T(8,128)S(1)}, u32[]{:S(2)}, u32[]{:S(2)}) collective-permute-start(f32[65,8,128]{2,1,0:T(8,128)S(1)} %join_high.1.a_ref), channel_id=1, source_target_pairs={{0,2},{1,3},{2,0},{3,1},{4,6},{5,7},{6,4},{7,5},{8,10},{9,11},{10,... | collective-permute-start | bytes 798728 | tf_op jit(solution)/shard_map/ppermute | solution.py:608
  35.6 25.0 %copy-start.7 = (f32[16,56,128]{2,1,0:T(8,128)S(1)}, f32[16,56,128]{2,1,0:T(8,128)}, u32[]{:S(2)}) copy-start(f32[16,56,128]{2,1,0:T(8,128)} %get-tuple-element.44.refs_3_) | copy-start | bytes 1376260
  35.6 11.4 %collective-permute-start.4 = (f32[65,8,128]{2,1,0:T(8,128)S(1)}, f32[65,8,128]{2,1,0:T(8,128)S(1)}, u32[]{:S(2)}, u32[]{:S(2)}) collective-permute-start(f32[65,8,128]{2,1,0:T(8,128)S(1)} %join_low.1.a_ref), channel_id=1, source_target_pairs={{0,2},{1,3},{2,0},{3,1},{4,6},{5,7},{6,4},{7,5},{8,10},{9,11},{10,... | collective-permute-start | bytes 798728 | tf_op jit(solution)/shard_map/ppermute | solution.py:608
  36.9 13.6 %copy-start = (f32[128,8,128]{2,1,0:T(8,128)}, f32[128,8,128]{2,1,0:T(8,128)S(1)}, u32[]{:S(2)}) copy-start(f32[128,8,128]{2,1,0:T(8,128)S(1)} %add.16.mine_ref) | copy-start | bytes 1572868
  36.9 23.8 %copy-start.6 = (f32[16,72,128]{2,1,0:T(8,128)S(1)}, f32[16,72,128]{2,1,0:T(8,128)}, u32[]{:S(2)}) copy-start(f32[16,72,128]{2,1,0:T(8,128)} %get-tuple-element.43.refs_2_) | copy-start | bytes 1769476
  36.9 13.6 %collective-permute-start.12 = (f32[128,8,128]{2,1,0:T(8,128)S(1)}, f32[128,8,128]{2,1,0:T(8,128)}, u32[]{:S(2)}, u32[]{:S(2)}) collective-permute-start(f32[128,8,128]{2,1,0:T(8,128)S(1)} %add.16.mine_ref), channel_id=1, source_target_pairs={{0,1},{1,0},{2,3},{3,2},{4,5},{5,4},{6,7},{7,6},{8,9},{9,8},{10,11... | collective-permute-start | bytes 1572872 | tf_op jit(solution)/shard_map/ppermute | solution.py:609
  41.4 18.5 %copy-start.2 = (f32[65,8,128]{2,1,0:T(8,128)}, f32[65,8,128]{2,1,0:T(8,128)S(1)}, u32[]{:S(2)}) copy-start(f32[65,8,128]{2,1,0:T(8,128)S(1)} %add.15.m_high) | copy-start | bytes 798724
  41.4 18.4 %collective-permute-start.8 = (f32[65,8,128]{2,1,0:T(8,128)S(1)}, f32[65,8,128]{2,1,0:T(8,128)}, u32[]{:S(2)}, u32[]{:S(2)}) collective-permute-start(f32[65,8,128]{2,1,0:T(8,128)S(1)} %add.15.m_high), channel_id=1, source_target_pairs={{0,1},{1,0},{2,3},{3,2},{4,5},{5,4},{6,7},{7,6},{8,9},{9,8},{10,11... | collective-permute-start | bytes 798728 | tf_op jit(solution)/shard_map/ppermute | solution.py:609
  47.1 12.8 %copy-start.3 = (f32[65,8,128]{2,1,0:T(8,128)}, f32[65,8,128]{2,1,0:T(8,128)S(1)}, u32[]{:S(2)}) copy-start(f32[65,8,128]{2,1,0:T(8,128)S(1)} %add.14.m_low) | copy-start | bytes 798724
  47.1 12.7 %collective-permute-start.5 = (f32[65,8,128]{2,1,0:T(8,128)S(1)}, f32[65,8,128]{2,1,0:T(8,128)}, u32[]{:S(2)}, u32[]{:S(2)}) collective-permute-start(f32[65,8,128]{2,1,0:T(8,128)S(1)} %add.14.m_low), channel_id=1, source_target_pairs={{0,1},{1,0},{2,3},{3,2},{4,5},{5,4},{6,7},{7,6},{8,9},{9,8},{10,11... | collective-permute-start | bytes 798728 | tf_op jit(solution)/shard_map/ppermute | solution.py:609
  57.0 2.9 %copy-start.4 = (f32[16,72,128]{2,1,0:T(8,128)}, f32[16,72,128]{2,1,0:T(8,128)S(1)}, u32[]{:S(2)}) copy-start(f32[16,72,128]{2,1,0:T(8,128)S(1)} %collective-permute-done.9.refs_0_) | copy-start | bytes 1769476
  59.8 0.8 %copy-start.5 = (f32[16,72,128]{2,1,0:T(8,128)}, f32[16,72,128]{2,1,0:T(8,128)S(1)}, u32[]{:S(2)}) copy-start(f32[16,72,128]{2,1,0:T(8,128)S(1)} %collective-permute-done.10.refs_1_) | copy-start | bytes 1769476

commit v6 on v5

--- a/solution.py
+++ b/solution.py
@@ -27,6 +27,10 @@
 
 def params(mebibytes):
     return pltpu.CompilerParams(vmem_limit_bytes=mebibytes * 1024 * 1024)
+
+
+def in_hbm(*arrays):
+    return [pltpu.with_memory_space_constraint(x, pltpu.HBM) for x in arrays]
 
 
 def low_need(shift):
@@ -306,9 +310,9 @@
             pltpu.SemaphoreType.DMA((planes,)),
             pltpu.SemaphoreType.DMA((len(cuts),)),
         ],
-        compiler_params=params(58),
+        compiler_params=params(36),
         name="advance",
-    )(meta, *small, heights, pop)
+    )(*in_hbm(meta, *small, heights, pop))
 
 
 def fold_kernel(mine_ref, received_ref, *out_refs):
@@ -405,10 +409,10 @@
 
 
 def relax_kernel(tiles, meta_ref, sx_ref, sy_ref, fx_ref, fy_ref, factor_ref, mine_ref, other_ref,
-                 planes_ref, out_ref, done_ref, buf, sem_in, sem_out):
+                 planes_ref, *refs):
+    out_ref, buf, sem_in, sem_out = refs[-4:]
     planes, _, lane_tiles = planes_ref.shape[:3]
     half = lane_tiles // 2
-    done_ref[0] = 1
     first_tile, count = tiles[0], len(tiles)
 
     def copy(k, h, out):
@@ -437,22 +441,30 @@
             copy(k, h, True).wait()
 
 
-def relax_inside(tiles, meta, small, factor, sums, moved):
+def relax_tiles(tiles, meta, small, factor, sums, moved, out=None):
     planes, _, lane_tiles = moved.shape[:3]
     count = len(tiles)
+    operands = [*in_hbm(meta, *small[:4]), factor, *sums, *in_hbm(moved)]
+    in_specs = [SMEM_SPEC] * 6 + [VMEM_SPEC] * 2 + [HBM_SPEC]
+    aliases = {}
+    if out is not None:
+        aliases = {len(operands): 0}
+        operands.extend(in_hbm(out))
+        in_specs.append(HBM_SPEC)
     return pl.pallas_call(
         functools.partial(relax_kernel, tiles),
-        out_shape=[jax.ShapeDtypeStruct(moved.shape, F32), jax.ShapeDtypeStruct((1,), jnp.int32)],
-        in_specs=[SMEM_SPEC] * 6 + [VMEM_SPEC] * 2 + [ANY_SPEC],
-        out_specs=[ANY_SPEC, SMEM_SPEC],
+        out_shape=pltpu.HBM(moved.shape, F32),
+        in_specs=in_specs,
+        out_specs=HBM_SPEC,
         scratch_shapes=[
             pltpu.VMEM((planes, count, lane_tiles, ROW, LANE), F32),
             pltpu.SemaphoreType.DMA((2 * count,)),
             pltpu.SemaphoreType.DMA((2 * count,)),
         ],
-        compiler_params=params(58),
-        name="relax_inside",
-    )(meta, *small[:4], factor, *sums, moved)
+        input_output_aliases=aliases,
+        compiler_params=params(24),
+        name="relax_tiles",
+    )(*operands)
 
 
 def relax_edges_kernel(cuts, meta_ref, sx_ref, sy_ref, fx_ref, fy_ref, inflow_ref, factor_ref,
@@ -462,7 +474,7 @@
     planes, row_tiles, lane_tiles = planes_ref.shape[:3]
     half = lane_tiles // 2
     row0, first, last, core = (meta_ref[i] for i in range(4))
-    places = 0, 1, row_tiles - 2, row_tiles - 1
+    places = 0, 1, row_tiles - 1
     needs = [low_need(sy_ref[0]), high_need(sy_ref[0])]
     for v in range(1, planes):
         needs = [needs[0] + low_need(sy_ref[v]), needs[1] + high_need(sy_ref[v])]
@@ -477,12 +489,17 @@
 
     for n in range(len(cuts)):
         pl.when(needs[cuts[n][0]] > cuts[n][1])(lambda n=n: pack_copy(n).start())
-    for k in range(4):
+    for k in (0, 2, 1):
         in_copy(k).start()
     prepare_heights(heights_ref, bars)
+    for t in range(lane_tiles + 2):
+        for r in (24, 32):
+            frames[0, t, r : r + ROW, :] = jnp.zeros((ROW, LANE), F32)
+        for r in (16, 24):
+            frames[1, t, r : r + ROW, :] = jnp.zeros((ROW, LANE), F32)
     for n in range(len(cuts)):
         pl.when(needs[cuts[n][0]] > cuts[n][1])(lambda n=n: pack_copy(n).wait())
-    for k in range(4):
+    for k in (0, 2, 1):
         in_copy(k).wait()
 
     def add_masked(v, k, first_row):
@@ -498,29 +515,26 @@
         up = shift >= 0
         scalars = sx_ref[v], shift, fx_ref[v], fy_ref[v]
         borders = (0, lane_tiles + 1)
-        columns = range(lane_tiles + 2)
 
         @pl.when(up & (first == 0))
         def _():
-            fill_rows(frames, v, borders, 8, 16, value)
-            fill_rows(frames, v, columns, 24, 16, 0.0)
+            fill_rows(frames, 0, borders, 8, 16, value)
             for t in range(lane_tiles):
                 for r in range(0, 16, ROW):
                     piece = low_buf[t, pl.ds(low + shift + 1 + r, ROW), :]
-                    frames[v, t + 1, 8 + r : 8 + r + ROW, :] = piece
-            advect(frames, v, scalars, [(24, add_masked(v, 0, row0))])
+                    frames[0, t + 1, 8 + r : 8 + r + ROW, :] = piece
+            advect(frames, 0, scalars, [(24, add_masked(v, 0, row0))])
 
             @pl.when(shift == CFL)
             def _():
-                advect(frames, v, scalars, [(32, add_masked(v, 1, row0 + ROW))])
+                advect(frames, 0, scalars, [(32, add_masked(v, 1, row0 + ROW))])
 
         @pl.when(jnp.logical_not(up) & (last == 0))
         def _():
-            fill_rows(frames, v, borders, 32, 8, value)
-            fill_rows(frames, v, columns, 16, 16, 0.0)
+            fill_rows(frames, 1, borders, 32, 8, value)
             for t in range(lane_tiles):
-                frames[v, t + 1, 32:40, :] = high_buf[t, pl.ds(16 + high, ROW), :]
-            advect(frames, v, scalars, [(24, add_masked(v, 3, row0 + ROW * (row_tiles - 1)))])
+                frames[1, t + 1, 32:40, :] = high_buf[t, pl.ds(16 + high, ROW), :]
+            advect(frames, 1, scalars, [(24, add_masked(v, 2, row0 + ROW * (row_tiles - 1)))])
 
         return low + low_need(shift), high + high_need(shift)
 
@@ -528,44 +542,52 @@
     weights = [velocity(sx_ref, sy_ref, fx_ref, fy_ref, v) for v in range(planes)]
 
     def out_copy(k, h):
-        j = jnp.where(k < 2, k, row_tiles - 4 + k)
+        j = jnp.where(k < 2, k, row_tiles - 1)
         lanes = pl.ds(h * half, half)
         return pltpu.make_async_copy(buf.at[:, k, lanes], out_ref.at[:, j, lanes], sem_out.at[2 * k + h])
 
-    for sums, begin in (((m_low, o_low), 0), ((m_high, o_high), 2)):
-
-        def step(k, _, sums=sums, begin=begin):
-            for h in range(2):
-                relax_tile(buf, sums, (k - begin) * 4 * half, core, factor_ref[0], weights, k, h)
-                out_copy(k, h).start()
-            return 0
-
-        lax.fori_loop(begin, begin + 2, step, 0)
-    for k in range(4):
+    def finish(k, h, sums, base):
+        relax_tile(buf, sums, base, core, factor_ref[0], weights, k, h)
+        out_copy(k, h).start()
+
+    def step(k, _):
+        for h in range(2):
+            finish(k, h, (m_low, o_low), k * 4 * half)
+        return 0
+
+    for h in range(2):
+        finish(2, h, (m_high, o_high), 4 * half)
+    lax.fori_loop(0, 2, step, 0)
+    for k in range(3):
         for h in range(2):
             out_copy(k, h).wait()
 
 
 def relax_edges(meta, small, factor, heights, sums, moved, packs, cuts, out):
     planes, _, lane_tiles = moved.shape[:3]
-    operands = [meta, *small[:5], factor, heights, *sums, moved, *packs, out]
+    fixed = [*in_hbm(meta, *small[:5]), factor, *in_hbm(heights)]
+    operands = [*fixed, *sums, *in_hbm(moved), *packs, *in_hbm(out)]
     return pl.pallas_call(
         functools.partial(relax_edges_kernel, cuts),
-        out_shape=jax.ShapeDtypeStruct(out.shape, F32),
-        in_specs=[SMEM_SPEC] * 7 + [VMEM_SPEC] * 5 + [ANY_SPEC] * (len(cuts) + 2),
-        out_specs=ANY_SPEC,
+        out_shape=pltpu.HBM(out.shape, F32),
+        in_specs=[SMEM_SPEC] * 7
+        + [VMEM_SPEC] * 5
+        + [HBM_SPEC]
+        + [ANY_SPEC] * len(cuts)
+        + [HBM_SPEC],
+        out_specs=HBM_SPEC,
         scratch_shapes=[
-            pltpu.VMEM((planes, lane_tiles + 2, 48, LANE), F32),
-            pltpu.VMEM((planes, 4, lane_tiles, ROW, LANE), F32),
+            pltpu.VMEM((2, lane_tiles + 2, 48, LANE), F32),
+            pltpu.VMEM((planes, 3, lane_tiles, ROW, LANE), F32),
             pltpu.VMEM((lane_tiles, planes * LOW_ROWS + 32, LANE), F32),
             pltpu.VMEM((lane_tiles, planes * HIGH_ROWS + 32, LANE), F32),
             pltpu.VMEM((lane_tiles, ROW, LANE), jnp.int32),
             pltpu.SemaphoreType.DMA((len(cuts),)),
-            pltpu.SemaphoreType.DMA((4,)),
-            pltpu.SemaphoreType.DMA((8,)),
+            pltpu.SemaphoreType.DMA((3,)),
+            pltpu.SemaphoreType.DMA((6,)),
         ],
         input_output_aliases={len(operands) - 1: 0},
-        compiler_params=params(58),
+        compiler_params=params(24),
         name="relax_edges",
     )(*operands)
 
@@ -586,7 +608,6 @@
     factor = impact_frequency_factor.reshape(1)
     bars = heights.reshape(lane_tiles, LANE)
     pop = populations.reshape(planes, row_tiles, ROW, lane_tiles, LANE).transpose(0, 1, 3, 2, 4)
-    pop = pltpu.with_memory_space_constraint(pop, pltpu.HBM)
     low_sent, high_sent = min(LOW_SENT, planes * LOW_ROWS), min(HIGH_SENT, planes * HIGH_ROWS)
     cuts = [
         (0, 0, low_sent),
@@ -613,10 +634,11 @@
 
     more = lax.cond(more_needed[0] > 0, send_more, lambda low, high: (low, high), packs[2], packs[3])
     sums_inside = total(inside)
-    out, done = relax_inside(plan.inside, meta, small, factor, sums_inside, moved)
+    out = relax_tiles(plan.inside, meta, small, factor, sums_inside, moved)
     sums_low = total(small_call(join_low_kernel, "join_low", edge_low, from_low, (), 1))
     sums_high = total(small_call(join_high_kernel, "join_high", edge_high, from_high, (), 1))
 
+    out = relax_tiles([row_tiles - 2], meta, small, factor, sums_high, moved, out)
     halo = low_first, high_first, *more
     out = relax_edges(meta, small, factor, bars, sums_low + sums_high, moved, halo, cuts, out)
     return out.transpose(0, 1, 3, 2, 4).reshape(planes, row_count, col_count)

time: 70.6 us -> 65.5 us (0.928)
  waiting for transfers between devices: 8.95 us -> 6.51 us
  local copies, waits for them, and re-layouts: 2.12 us -> 0.01 us
    unnamed x16 -> x4, local copies, waits for them, and re-layouts: 2.12 us -> 0.01 us
    ppermute x1, waiting for transfers between devices: 2.83 us -> 1.14 us  [per_device(): high_first = lax.ppermute(packs[1], 'space', backward)]
    pallas_call x1, Pallas kernels: 15 us -> 14 us  [advance(): pl.pallas_call(functools.partial(advance_kernel, plan, cuts, group), out_...]
    pallas_call x2 -> x3, Pallas kernels: 15.4 us -> 15.6 us  [the longest x2 8.12 us: relax_tiles(): pl.pallas_call(functools.partial(relax_kernel, tiles), out_shape=pltpu.HB...]
  transfers between devices with their start and end apart: 11 -> 11, of which waited for: 5 -> 4; matrix products, arithmetic and copies ran while one was open for 0% -> 0% of each run, Pallas kernels for 9% -> 13%
where the time goes in v6:
time: 65.5 us; the launch traced here: 65.2 us
  Pallas kernels  30 us (46%)
  starting transfers between devices  26.6 us (41%)
  waiting for transfers between devices  6.51 us (10%)
  between operations  1.45 us (2%)
  other arithmetic  0.66 us (1%)
    pallas_call x1, Pallas kernels, advance(): pl.pallas_call(functools.partial(advance_kernel, plan, cuts, group), out_...  14 us
    ppermute x3, starting transfers between devices, total(): return (whole, lax.ppermute(whole, 'vel', partner))  10.2 us
    pallas_call x2, Pallas kernels, relax_tiles(): pl.pallas_call(functools.partial(relax_kernel, tiles), out_shape=pltpu.HB...  8.12 us
    pallas_call x1, Pallas kernels, relax_edges(): pl.pallas_call(functools.partial(relax_edges_kernel, cuts), out_shape=plt...  7.52 us
    ppermute x1, starting transfers between devices, per_device(): high_first = lax.ppermute(packs[1], 'space', backward)  3.96 us
    ppermute x3, starting transfers between devices, total(): lax.ppermute(sums, 'vel', across)  3.14 us
    ppermute x1, starting transfers between devices, per_device(): from_low = lax.ppermute(up, 'space', forward)  3.11 us
    ppermute x1, starting transfers between devices, per_device(): from_high = lax.ppermute(down, 'space', backward)  3.06 us
  transfers between devices with their start and end apart: 11, of which 4 were waited for; matrix products, arithmetic and copies ran while one was open for 0% of the time, Pallas kernels for 13%

profile of v6, /device:TPU:9, one launch (start us, length us, event | category | flops | bytes accessed | tf_op | source)
XLA Modules:
  0.0 65.2 jit_solution(13404177618021814515)
XLA Ops:
  0.0 0.7 %pad_add_fusion.meta_ref = s32[4]{0:T(128)} fusion(s32[1]{0:T(128)} %bitcast.3, s32[1]{0:T(128)} %bitcast.2, s32[1]{0:T(128)} %bitcast.1, s32[1]{0:T(128)} %bitcast), kind=kLoop, calls=%fused_computation | loop fusion | flops 12 | bytes 32 | tf_op jit(solution)/shard_map/stack | solution.py:606
  0.7 14.0 %advance.1 = (f32[16,8,16,8,128]{4,3,2,1,0:T(8,128)}, f32[324,8,128]{2,1,0:T(8,128)S(1)}, f32[324,8,128]{2,1,0:T(8,128)S(1)}, s32[1]{0:T(128)}, f32[16,72,128]{2...) custom-call(s32[4]{0:T(128)} %pad_add_fusion.meta_ref, s32[16]{0:T(128)} %sx_ref.7, ...), custom_call_target="tpu_custom_call" | custom-call | tf_op jit(solution)/shard_map/advance/pallas_call | solution.py:295
  14.7 0.9 %collective-permute-start.2 = (f32[324,8,128]{2,1,0:T(8,128)S(1)}, f32[324,8,128]{2,1,0:T(8,128)S(1)}, u32[]{:S(2)}, u32[]{:S(2)}) collective-permute-start(f32[324,8,128]{2,1,0:T(8,128)S(1)} %get-tuple-element.31), channel_id=1, source_target_pairs={{0,1},{1,0},{2,3},{3,2},{4,5},{5,4},{6,7},{7,6},{8,9},{9,8},{10,11... | collective-permute-start | bytes 3981320 | tf_op jit(solution)/shard_map/ppermute | solution.py:621
  15.5 2.7 %collective-permute-done.2.received_ref = f32[324,8,128]{2,1,0:T(8,128)S(1)} collective-permute-done((f32[324,8,128]{2,1,0:T(8,128)S(1)}, f32[324,8,128]{2,1,0:T(8,128)S(1)}, u32[]{:S(2)}, u32[]{:S(2)}) %collective-permute-start.2) | collective-permute-done | bytes 1327136 | tf_op jit(solution)/shard_map/ppermute | solution.py:621
  18.2 0.1 fold.1
  18.4 1.5 %collective-permute-start.11 = (f32[128,8,128]{2,1,0:T(8,128)S(1)}, f32[128,8,128]{2,1,0:T(8,128)S(1)}, u32[]{:S(2)}, u32[]{:S(2)}) collective-permute-start(f32[128,8,128]{2,1,0:T(8,128)S(1)} %get-tuple-element.44.a_ref), channel_id=1, source_target_pairs={{0,2},{1,3},{2,0},{3,1},{4,6},{5,7},{6,4},{7,5},{8,10},{9,11},{10,... | collective-permute-start | bytes 1572872 | tf_op jit(solution)/shard_map/ppermute | solution.py:629
  19.9 3.1 %collective-permute-start.3 = (f32[36,8,128]{2,1,0:T(8,128)S(1)}, f32[36,8,128]{2,1,0:T(8,128)S(1)}, u32[]{:S(2)}, u32[]{:S(2)}) collective-permute-start(f32[36,8,128]{2,1,0:T(8,128)S(1)} %get-tuple-element.33), channel_id=1, source_target_pairs={{0,4},{4,8},{8,12},{12,16},{16,20},{20,24},{24,28},{1,5},{5,9},{9,... | collective-permute-start | bytes 442376 | tf_op jit(solution)/shard_map/ppermute | solution.py:623
  23.0 3.1 %collective-permute-start.6 = (f32[32,8,128]{2,1,0:T(8,128)S(1)}, f32[32,8,128]{2,1,0:T(8,128)S(1)}, u32[]{:S(2)}, u32[]{:S(2)}) collective-permute-start(f32[32,8,128]{2,1,0:T(8,128)S(1)} %get-tuple-element.35), channel_id=1, source_target_pairs={{4,0},{8,4},{12,8},{16,12},{20,16},{24,20},{28,24},{5,1},{9,5},{13... | collective-permute-start | bytes 393224 | tf_op jit(solution)/shard_map/ppermute | solution.py:624
  26.8 2.2 %collective-permute-start.9 = (f32[16,72,128]{2,1,0:T(8,128)}, f32[16,72,128]{2,1,0:T(8,128)S(1)}, u32[]{:S(2)}, u32[]{:S(2)}) collective-permute-start(f32[16,72,128]{2,1,0:T(8,128)} %get-tuple-element.37), channel_id=1, source_target_pairs={{0,4},{4,8},{8,12},{12,16},{16,20},{20,24},{24,28},{1,5},{5,9},{9,... | collective-permute-start | bytes 1769480 | tf_op jit(solution)/shard_map/ppermute | solution.py:625
  29.0 4.0 %collective-permute-start.10 = (f32[16,72,128]{2,1,0:T(8,128)}, f32[16,72,128]{2,1,0:T(8,128)S(1)}, u32[]{:S(2)}, u32[]{:S(2)}) collective-permute-start(f32[16,72,128]{2,1,0:T(8,128)} %get-tuple-element.38), channel_id=1, source_target_pairs={{4,0},{8,4},{12,8},{16,12},{20,16},{24,20},{28,24},{5,1},{9,5},{13... | collective-permute-start | bytes 1769480 | tf_op jit(solution)/shard_map/ppermute | solution.py:626
  33.0 0.0 collective-permute-done.6.high_ref
  33.0 0.1 collective-permute-start.7
  33.1 0.0 collective-permute-done.3.low_ref
  33.1 1.5 %collective-permute-start.4 = (f32[65,8,128]{2,1,0:T(8,128)S(1)}, f32[65,8,128]{2,1,0:T(8,128)S(1)}, u32[]{:S(2)}, u32[]{:S(2)}) collective-permute-start(f32[65,8,128]{2,1,0:T(8,128)S(1)} %join_low.1.a_ref), channel_id=1, source_target_pairs={{0,2},{1,3},{2,0},{3,1},{4,6},{5,7},{6,4},{7,5},{8,10},{9,11},{10,... | collective-permute-start | bytes 798728 | tf_op jit(solution)/shard_map/ppermute | solution.py:629
  34.6 0.0 collective-permute-done.11.b_ref
  34.6 0.1 add.16.mine_ref
  34.7 2.4 %collective-permute-start.12 = (f32[128,8,128]{2,1,0:T(8,128)S(1)}, f32[128,8,128]{2,1,0:T(8,128)S(1)}, u32[]{:S(2)}, u32[]{:S(2)}) collective-permute-start(f32[128,8,128]{2,1,0:T(8,128)S(1)} %add.16.mine_ref), channel_id=1, source_target_pairs={{0,1},{1,0},{2,3},{3,2},{4,5},{5,4},{6,7},{7,6},{8,9},{9,8},{10,11... | collective-permute-start | bytes 1572872 | tf_op jit(solution)/shard_map/ppermute | solution.py:630
  37.1 2.1 %collective-permute-done.7.b_ref = f32[65,8,128]{2,1,0:T(8,128)S(1)} collective-permute-done((f32[65,8,128]{2,1,0:T(8,128)S(1)}, f32[65,8,128]{2,1,0:T(8,128)S(1)}, u32[]{:S(2)}, u32[]{:S(2)}) %collective-permute-start.7) | collective-permute-done | bytes 266272 | tf_op jit(solution)/shard_map/ppermute | solution.py:629
  39.2 5.1 %collective-permute-start.8 = (f32[65,8,128]{2,1,0:T(8,128)S(1)}, f32[65,8,128]{2,1,0:T(8,128)S(1)}, u32[]{:S(2)}, u32[]{:S(2)}) collective-permute-start(f32[65,8,128]{2,1,0:T(8,128)S(1)} %add.15.mine_ref.m_high), channel_id=1, source_target_pairs={{0,1},{1,0},{2,3},{3,2},{4,5},{5,4},{6,7},{7,6},{8,9},{9,8},{10,11... | collective-permute-start | bytes 798728 | tf_op jit(solution)/shard_map/ppermute | solution.py:630
  44.3 0.6 collective-permute-done.4.b_ref
  44.9 2.8 %collective-permute-start.5 = (f32[65,8,128]{2,1,0:T(8,128)S(1)}, f32[65,8,128]{2,1,0:T(8,128)S(1)}, u32[]{:S(2)}, u32[]{:S(2)}) collective-permute-start(f32[65,8,128]{2,1,0:T(8,128)S(1)} %add.14.m_low), channel_id=1, source_target_pairs={{0,1},{1,0},{2,3},{3,2},{4,5},{5,4},{6,7},{7,6},{8,9},{9,8},{10,11... | collective-permute-start | bytes 798728 | tf_op jit(solution)/shard_map/ppermute | solution.py:630
  48.3 0.0 collective-permute-done.12.other_ref
  48.3 4.9 %relax_tiles.2.refs_0_ = f32[16,8,16,8,128]{4,3,2,1,0:T(8,128)} custom-call(s32[4]{0:T(128)} %pad_add_fusion.meta_ref, s32[16]{0:T(128)} %sx_ref.7, s32[16]{0:T(128)} %sy_ref.7, f32[16]{0:T(128)} %fx_ref.7, f32[16]{0:T(128)} %fy_ref.7, f32[1]{0:T(128)} %bitcast.13.factor_ref, f32[128,8,128]{2,1,0:T(8,128)S(1)} %add.16.mine_ref, ...), custom_call_target="tpu_custom_call" | custom-call | tf_op jit(solution)/shard_map/relax_tiles/pallas_call | solution.py:454
  53.2 0.0 collective-permute-done.8.other_ref.o_high
  53.2 0.0 copy-start
  53.2 0.0 copy-start.1
  53.3 3.2 %relax_tiles.3.refs_4_ = f32[16,8,16,8,128]{4,3,2,1,0:T(8,128)} custom-call(s32[4]{0:T(128)} %pad_add_fusion.meta_ref, s32[16]{0:T(128)} %sx_ref.7, s32[16]{0:T(128)} %sy_ref.7, f32[16]{0:T(128)} %fx_ref.7, f32[16]{0:T(128)} %fy_ref.7, f32[1]{0:T(128)} %bitcast.14.factor_ref, f32[65,8,128]{2,1,0:T(8,128)S(1)} %add.15.mine_ref.m_high, ...), custom_call_target="tpu_custom_call", output_to_operand_aliasing={{}: (9, {})} | custom-call | tf_op jit(solution)/shard_map/relax_tiles/pallas_call | solution.py:454
  56.5 0.0 collective-permute-done.9.refs_0_
  56.5 1.1 %collective-permute-done.10.refs_1_ = f32[16,72,128]{2,1,0:T(8,128)S(1)} collective-permute-done((f32[16,72,128]{2,1,0:T(8,128)}, f32[16,72,128]{2,1,0:T(8,128)S(1)}, u32[]{:S(2)}, u32[]{:S(2)}) %collective-permute-start.10) | collective-permute-done | bytes 589856 | tf_op jit(solution)/shard_map/ppermute | solution.py:626
  57.7 0.0 collective-permute-done.5.o_low
  57.7 0.0 copy-done
  57.7 0.0 copy-done.1
  57.7 7.5 %relax_edges.1 = f32[16,8,16,8,128]{4,3,2,1,0:T(8,128)} custom-call(s32[4]{0:T(128)} %pad_add_fusion.meta_ref, s32[16]{0:T(128)} %sx_ref.7, s32[16]{0:T(128)} %sy_ref.7, f32[16]{0:T(128)} %fx_ref.7, f32[16]{0:T(128)} %fy_ref.7, f32[16]{0:T(128)} %inflow_ref.3, f32[1]{0:T(128)} %bitcast.15.factor_ref, ...), custom_call_target="tpu_custom_call", output_to_operand_aliasing={{}: (17, {})} | custom-call | tf_op jit(solution)/shard_map/relax_edges/pallas_call | solution.py:570
  (5 shorter events, 0.1 us)
Async XLA Ops:
  14.7 3.5 %collective-permute-start.2 = (f32[324,8,128]{2,1,0:T(8,128)S(1)}, f32[324,8,128]{2,1,0:T(8,128)S(1)}, u32[]{:S(2)}, u32[]{:S(2)}) collective-permute-start(f32[324,8,128]{2,1,0:T(8,128)S(1)} %get-tuple-element.31), channel_id=1, source_target_pairs={{0,1},{1,0},{2,3},{3,2},{4,5},{5,4},{6,7},{7,6},{8,9},{9,8},{10,11... | collective-permute-start | bytes 3981320 | tf_op jit(solution)/shard_map/ppermute | solution.py:621
  18.4 16.3 %collective-permute-start.11 = (f32[128,8,128]{2,1,0:T(8,128)S(1)}, f32[128,8,128]{2,1,0:T(8,128)S(1)}, u32[]{:S(2)}, u32[]{:S(2)}) collective-permute-start(f32[128,8,128]{2,1,0:T(8,128)S(1)} %get-tuple-element.44.a_ref), channel_id=1, source_target_pairs={{0,2},{1,3},{2,0},{3,1},{4,6},{5,7},{6,4},{7,5},{8,10},{9,11},{10,... | collective-permute-start | bytes 1572872 | tf_op jit(solution)/shard_map/ppermute | solution.py:629
  19.9 13.2 %collective-permute-start.3 = (f32[36,8,128]{2,1,0:T(8,128)S(1)}, f32[36,8,128]{2,1,0:T(8,128)S(1)}, u32[]{:S(2)}, u32[]{:S(2)}) collective-permute-start(f32[36,8,128]{2,1,0:T(8,128)S(1)} %get-tuple-element.33), channel_id=1, source_target_pairs={{0,4},{4,8},{8,12},{12,16},{16,20},{20,24},{24,28},{1,5},{5,9},{9,... | collective-permute-start | bytes 442376 | tf_op jit(solution)/shard_map/ppermute | solution.py:623
  23.0 9.9 %collective-permute-start.6 = (f32[32,8,128]{2,1,0:T(8,128)S(1)}, f32[32,8,128]{2,1,0:T(8,128)S(1)}, u32[]{:S(2)}, u32[]{:S(2)}) collective-permute-start(f32[32,8,128]{2,1,0:T(8,128)S(1)} %get-tuple-element.35), channel_id=1, source_target_pairs={{4,0},{8,4},{12,8},{16,12},{20,16},{24,20},{28,24},{5,1},{9,5},{13... | collective-permute-start | bytes 393224 | tf_op jit(solution)/shard_map/ppermute | solution.py:624
  26.8 29.7 %collective-permute-start.9 = (f32[16,72,128]{2,1,0:T(8,128)}, f32[16,72,128]{2,1,0:T(8,128)S(1)}, u32[]{:S(2)}, u32[]{:S(2)}) collective-permute-start(f32[16,72,128]{2,1,0:T(8,128)} %get-tuple-element.37), channel_id=1, source_target_pairs={{0,4},{4,8},{8,12},{12,16},{16,20},{20,24},{24,28},{1,5},{5,9},{9,... | collective-permute-start | bytes 1769480 | tf_op jit(solution)/shard_map/ppermute | solution.py:625
  29.0 28.7 %collective-permute-start.10 = (f32[16,72,128]{2,1,0:T(8,128)}, f32[16,72,128]{2,1,0:T(8,128)S(1)}, u32[]{:S(2)}, u32[]{:S(2)}) collective-permute-start(f32[16,72,128]{2,1,0:T(8,128)} %get-tuple-element.38), channel_id=1, source_target_pairs={{4,0},{8,4},{12,8},{16,12},{20,16},{24,20},{28,24},{5,1},{9,5},{13... | collective-permute-start | bytes 1769480 | tf_op jit(solution)/shard_map/ppermute | solution.py:626
  33.0 6.2 %collective-permute-start.7 = (f32[65,8,128]{2,1,0:T(8,128)S(1)}, f32[65,8,128]{2,1,0:T(8,128)S(1)}, u32[]{:S(2)}, u32[]{:S(2)}) collective-permute-start(f32[65,8,128]{2,1,0:T(8,128)S(1)} %join_high.1.a_ref), channel_id=1, source_target_pairs={{0,2},{1,3},{2,0},{3,1},{4,6},{5,7},{6,4},{7,5},{8,10},{9,11},{10,... | collective-permute-start | bytes 798728 | tf_op jit(solution)/shard_map/ppermute | solution.py:629
  33.1 11.8 %collective-permute-start.4 = (f32[65,8,128]{2,1,0:T(8,128)S(1)}, f32[65,8,128]{2,1,0:T(8,128)S(1)}, u32[]{:S(2)}, u32[]{:S(2)}) collective-permute-start(f32[65,8,128]{2,1,0:T(8,128)S(1)} %join_low.1.a_ref), channel_id=1, source_target_pairs={{0,2},{1,3},{2,0},{3,1},{4,6},{5,7},{6,4},{7,5},{8,10},{9,11},{10,... | collective-permute-start | bytes 798728 | tf_op jit(solution)/shard_map/ppermute | solution.py:629
  34.7 13.6 %collective-permute-start.12 = (f32[128,8,128]{2,1,0:T(8,128)S(1)}, f32[128,8,128]{2,1,0:T(8,128)S(1)}, u32[]{:S(2)}, u32[]{:S(2)}) collective-permute-start(f32[128,8,128]{2,1,0:T(8,128)S(1)} %add.16.mine_ref), channel_id=1, source_target_pairs={{0,1},{1,0},{2,3},{3,2},{4,5},{5,4},{6,7},{7,6},{8,9},{9,8},{10,11... | collective-permute-start | bytes 1572872 | tf_op jit(solution)/shard_map/ppermute | solution.py:630
  39.2 14.0 %collective-permute-start.8 = (f32[65,8,128]{2,1,0:T(8,128)S(1)}, f32[65,8,128]{2,1,0:T(8,128)S(1)}, u32[]{:S(2)}, u32[]{:S(2)}) collective-permute-start(f32[65,8,128]{2,1,0:T(8,128)S(1)} %add.15.mine_ref.m_high), channel_id=1, source_target_pairs={{0,1},{1,0},{2,3},{3,2},{4,5},{5,4},{6,7},{7,6},{8,9},{9,8},{10,11... | collective-permute-start | bytes 798728 | tf_op jit(solution)/shard_map/ppermute | solution.py:630
  44.9 12.7 %collective-permute-start.5 = (f32[65,8,128]{2,1,0:T(8,128)S(1)}, f32[65,8,128]{2,1,0:T(8,128)S(1)}, u32[]{:S(2)}, u32[]{:S(2)}) collective-permute-start(f32[65,8,128]{2,1,0:T(8,128)S(1)} %add.14.m_low), channel_id=1, source_target_pairs={{0,1},{1,0},{2,3},{3,2},{4,5},{5,4},{6,7},{7,6},{8,9},{9,8},{10,11... | collective-permute-start | bytes 798728 | tf_op jit(solution)/shard_map/ppermute | solution.py:630
  53.2 4.4 %copy-start = (f32[16,72,128]{2,1,0:T(8,128)S(1)}, f32[16,72,128]{2,1,0:T(8,128)}, u32[]{:S(2)}) copy-start(f32[16,72,128]{2,1,0:T(8,128)} %get-tuple-element.42.refs_2_) | copy-start | bytes 1769476
  53.2 4.4 %copy-start.1 = (f32[16,56,128]{2,1,0:T(8,128)S(1)}, f32[16,56,128]{2,1,0:T(8,128)}, u32[]{:S(2)}) copy-start(f32[16,56,128]{2,1,0:T(8,128)} %get-tuple-element.43.refs_3_) | copy-start | bytes 1376260

commit v7 on v6

--- a/solution.py
+++ b/solution.py
@@ -66,6 +66,8 @@
         nearer = padded[v, t + 1, pl.ds(start, ROW), :]
         further = padded[v, t + 1, pl.ds(start - 1, ROW), :]
         line = (1.0 - fy) * nearer + fy * further
+        if t < 0 or t == lane_tiles:
+            return line, line
         return pltpu.roll(line, near_roll, 1), pltpu.roll(line, far_roll, 1)
 
     def blend(put, t, near, far):
@@ -408,73 +410,78 @@
         relax_cells(lambda v: buf[v, k, t], put, values, factor, weights)
 
 
-def relax_kernel(tiles, meta_ref, sx_ref, sy_ref, fx_ref, fy_ref, factor_ref, mine_ref, other_ref,
-                 planes_ref, *refs):
+def relax_kernel(sizes, meta_ref, sx_ref, sy_ref, fx_ref, fy_ref, factor_ref, planes_ref, *refs):
+    sums_refs = refs[:-4]
     out_ref, buf, sem_in, sem_out = refs[-4:]
-    planes, _, lane_tiles = planes_ref.shape[:3]
+    planes, row_tiles, lane_tiles = planes_ref.shape[:3]
     half = lane_tiles // 2
-    first_tile, count = tiles[0], len(tiles)
-
-    def copy(k, h, out):
+
+    def copy(j, h, out):
         lanes = pl.ds(h * half, half)
-        here = buf.at[:, k, lanes]
+        here = buf.at[:, j, lanes]
         if out:
-            return pltpu.make_async_copy(here, out_ref.at[:, first_tile + k, lanes], sem_out.at[2 * k + h])
-        return pltpu.make_async_copy(planes_ref.at[:, first_tile + k, lanes], here, sem_in.at[2 * k + h])
-
-    for k in range(count):
+            return pltpu.make_async_copy(here, out_ref.at[:, j, lanes], sem_out.at[2 * j + h])
+        return pltpu.make_async_copy(planes_ref.at[:, j, lanes], here, sem_in.at[2 * j + h])
+
+    def tile(k):
+        return jnp.where(k < row_tiles - 2, k + 2, k + 2 - row_tiles)
+
+    def start(k, _):
         for h in range(2):
-            copy(k, h, False).start()
+            copy(tile(k), h, False).start()
+        return 0
+
+    lax.fori_loop(0, row_tiles, start, 0)
     weights = [velocity(sx_ref, sy_ref, fx_ref, fy_ref, v) for v in range(planes)]
-
-    def step(k, _):
+    begin = 0
+    for pair, size in enumerate(sizes):
+        sums = sums_refs[2 * pair : 2 * pair + 2]
+
+        def step(k, _, begin=begin, sums=sums):
+            j = tile(k)
+            for h in range(2):
+                copy(j, h, False).wait()
+                base = (k - begin) * 4 * half
+                relax_tile(buf, sums, base, meta_ref[3], factor_ref[0], weights, j, h)
+                copy(j, h, True).start()
+            return 0
+
+        lax.fori_loop(begin, begin + size, step, 0)
+        begin += size
+
+    def finish(j, _):
         for h in range(2):
-            copy(k, h, False).wait()
-            sums = mine_ref, other_ref
-            relax_tile(buf, sums, k * 4 * half, meta_ref[3], factor_ref[0], weights, k, h)
-            copy(k, h, True).start()
+            copy(j, h, True).wait()
         return 0
 
-    lax.fori_loop(0, count, step, 0)
-    for k in range(count):
-        for h in range(2):
-            copy(k, h, True).wait()
-
-
-def relax_tiles(tiles, meta, small, factor, sums, moved, out=None):
-    planes, _, lane_tiles = moved.shape[:3]
-    count = len(tiles)
-    operands = [*in_hbm(meta, *small[:4]), factor, *sums, *in_hbm(moved)]
-    in_specs = [SMEM_SPEC] * 6 + [VMEM_SPEC] * 2 + [HBM_SPEC]
-    aliases = {}
-    if out is not None:
-        aliases = {len(operands): 0}
-        operands.extend(in_hbm(out))
-        in_specs.append(HBM_SPEC)
+    lax.fori_loop(0, row_tiles, finish, 0)
+
+
+def relax_all(sizes, meta, small, factor, sums, moved):
+    planes, row_tiles, lane_tiles = moved.shape[:3]
+    operands = [*in_hbm(meta, *small[:4]), factor, *in_hbm(moved), *sums]
     return pl.pallas_call(
-        functools.partial(relax_kernel, tiles),
+        functools.partial(relax_kernel, sizes),
         out_shape=pltpu.HBM(moved.shape, F32),
-        in_specs=in_specs,
+        in_specs=[SMEM_SPEC] * 6 + [HBM_SPEC] + [VMEM_SPEC] * len(sums),
         out_specs=HBM_SPEC,
         scratch_shapes=[
-            pltpu.VMEM((planes, count, lane_tiles, ROW, LANE), F32),
-            pltpu.SemaphoreType.DMA((2 * count,)),
-            pltpu.SemaphoreType.DMA((2 * count,)),
+            pltpu.VMEM((planes, row_tiles, lane_tiles, ROW, LANE), F32),
+            pltpu.SemaphoreType.DMA((2 * row_tiles,)),
+            pltpu.SemaphoreType.DMA((2 * row_tiles,)),
         ],
-        input_output_aliases=aliases,
         compiler_params=params(24),
-        name="relax_tiles",
+        name="relax_all",
     )(*operands)
 
 
-def relax_edges_kernel(cuts, meta_ref, sx_ref, sy_ref, fx_ref, fy_ref, inflow_ref, factor_ref,
-                       heights_ref, m_low, o_low, m_high, o_high, planes_ref, *refs):
+def finish_kernel(cuts, meta_ref, sx_ref, sy_ref, fx_ref, fy_ref, inflow_ref, factor_ref, heights_ref,
+                  m_low, o_low, m_high, o_high, before_ref, *refs):
     pack_refs = refs[: len(cuts)]
-    _, out_ref, frames, buf, low_buf, high_buf, bars, sem_in, sem_planes, sem_out = refs[len(cuts) :]
-    planes, row_tiles, lane_tiles = planes_ref.shape[:3]
+    out_ref, frames, buf, keeps, low_buf, high_buf, bars, sem_in, sem_planes, sem_out = refs[len(cuts) :]
+    planes, row_tiles, lane_tiles = before_ref.shape[:3]
     half = lane_tiles // 2
     row0, first, last, core = (meta_ref[i] for i in range(4))
-    places = 0, 1, row_tiles - 1
     needs = [low_need(sy_ref[0]), high_need(sy_ref[0])]
     for v in range(1, planes):
         needs = [needs[0] + low_need(sy_ref[v]), needs[1] + high_need(sy_ref[v])]
@@ -484,27 +491,54 @@
         target = (low_buf, high_buf)[pack].at[:, 16 + begin : 16 + end, :]
         return pltpu.make_async_copy(pack_refs[n], target, sem_in.at[n])
 
-    def in_copy(k):
-        return pltpu.make_async_copy(planes_ref.at[:, places[k]], buf.at[:, k], sem_planes.at[k])
+    def cases(v):
+        shift = sy_ref[v]
+        from_low = (shift >= 0) & (first == 0)
+        return from_low, (shift < 0) & (last == 0), from_low & (shift == CFL)
+
+    tile_of = 0, row_tiles - 1, 1
+    slot_of = 0, 0, 1
+
+    def copy(v, case, out):
+        here = buf.at[v, slot_of[case]]
+        if out:
+            return pltpu.make_async_copy(here, out_ref.at[v, tile_of[case]], sem_out.at[v, slot_of[case]])
+        there = before_ref.at[v, tile_of[case]]
+        return pltpu.make_async_copy(there, here, sem_planes.at[v, slot_of[case]])
 
     for n in range(len(cuts)):
         pl.when(needs[cuts[n][0]] > cuts[n][1])(lambda n=n: pack_copy(n).start())
-    for k in (0, 2, 1):
-        in_copy(k).start()
+
+    def start(v, _):
+        for case, applies in enumerate(cases(v)):
+            pl.when(applies)(lambda case=case: copy(v, case, False).start())
+        return 0
+
+    lax.fori_loop(0, planes, start, 0)
     prepare_heights(heights_ref, bars)
     for t in range(lane_tiles + 2):
         for r in (24, 32):
             frames[0, t, r : r + ROW, :] = jnp.zeros((ROW, LANE), F32)
         for r in (16, 24):
             frames[1, t, r : r + ROW, :] = jnp.zeros((ROW, LANE), F32)
+    edges = ((m_low, o_low), 0), ((m_high, o_high), 4 * half), ((m_low, o_low), 4 * half)
+    for case, (sums, base) in enumerate(edges):
+        for t in range(lane_tiles):
+            h, n = divmod(t, half)
+            values = []
+            for m in range(4):
+                index = base + m * half + n
+                values.append(jnp.where(core == h, sums[0][index], sums[1][index]))
+            keeps[case, t] = profile(*values, factor_ref[0])[4]
     for n in range(len(cuts)):
         pl.when(needs[cuts[n][0]] > cuts[n][1])(lambda n=n: pack_copy(n).wait())
-    for k in (0, 2, 1):
-        in_copy(k).wait()
-
-    def add_masked(v, k, first_row):
+
+    def add_masked(v, case):
+        first_row = row0 + ROW * tile_of[case]
+
         def put(t, value):
-            buf[v, k, t] = buf[v, k, t] + jnp.where(first_row < bars[t], 0.0, value)
+            part = jnp.where(first_row < bars[t], 0.0, value)
+            buf[v, slot_of[case], t] = buf[v, slot_of[case], t] + keeps[case, t] * part
 
         return put
 
@@ -512,83 +546,71 @@
         low, high = offsets
         value = inflow_ref[v]
         shift = sy_ref[v]
-        up = shift >= 0
         scalars = sx_ref[v], shift, fx_ref[v], fy_ref[v]
         borders = (0, lane_tiles + 1)
-
-        @pl.when(up & (first == 0))
+        from_low, from_high, reaches_second = cases(v)
+
+        @pl.when(from_low)
         def _():
             fill_rows(frames, 0, borders, 8, 16, value)
             for t in range(lane_tiles):
                 for r in range(0, 16, ROW):
                     piece = low_buf[t, pl.ds(low + shift + 1 + r, ROW), :]
                     frames[0, t + 1, 8 + r : 8 + r + ROW, :] = piece
-            advect(frames, 0, scalars, [(24, add_masked(v, 0, row0))])
-
-            @pl.when(shift == CFL)
-            def _():
-                advect(frames, 0, scalars, [(32, add_masked(v, 1, row0 + ROW))])
-
-        @pl.when(jnp.logical_not(up) & (last == 0))
+            copy(v, 0, False).wait()
+            advect(frames, 0, scalars, [(24, add_masked(v, 0))])
+            copy(v, 0, True).start()
+
+        @pl.when(reaches_second)
+        def _():
+            copy(v, 2, False).wait()
+            advect(frames, 0, scalars, [(32, add_masked(v, 2))])
+            copy(v, 2, True).start()
+
+        @pl.when(from_high)
         def _():
             fill_rows(frames, 1, borders, 32, 8, value)
             for t in range(lane_tiles):
                 frames[1, t + 1, 32:40, :] = high_buf[t, pl.ds(16 + high, ROW), :]
-            advect(frames, 1, scalars, [(24, add_masked(v, 2, row0 + ROW * (row_tiles - 1)))])
+            copy(v, 1, False).wait()
+            advect(frames, 1, scalars, [(24, add_masked(v, 1))])
+            copy(v, 1, True).start()
 
         return low + low_need(shift), high + high_need(shift)
 
     lax.fori_loop(0, planes, one, (jnp.int32(0), jnp.int32(0)))
-    weights = [velocity(sx_ref, sy_ref, fx_ref, fy_ref, v) for v in range(planes)]
-
-    def out_copy(k, h):
-        j = jnp.where(k < 2, k, row_tiles - 1)
-        lanes = pl.ds(h * half, half)
-        return pltpu.make_async_copy(buf.at[:, k, lanes], out_ref.at[:, j, lanes], sem_out.at[2 * k + h])
-
-    def finish(k, h, sums, base):
-        relax_tile(buf, sums, base, core, factor_ref[0], weights, k, h)
-        out_copy(k, h).start()
-
-    def step(k, _):
-        for h in range(2):
-            finish(k, h, (m_low, o_low), k * 4 * half)
+
+    def end(v, _):
+        for case, applies in enumerate(cases(v)):
+            pl.when(applies)(lambda case=case: copy(v, case, True).wait())
         return 0
 
-    for h in range(2):
-        finish(2, h, (m_high, o_high), 4 * half)
-    lax.fori_loop(0, 2, step, 0)
-    for k in range(3):
-        for h in range(2):
-            out_copy(k, h).wait()
-
-
-def relax_edges(meta, small, factor, heights, sums, moved, packs, cuts, out):
-    planes, _, lane_tiles = moved.shape[:3]
+    lax.fori_loop(0, planes, end, 0)
+
+
+def finish_edges(meta, small, factor, heights, sums, packs, cuts, out):
+    planes, _, lane_tiles = out.shape[:3]
     fixed = [*in_hbm(meta, *small[:5]), factor, *in_hbm(heights)]
-    operands = [*fixed, *sums, *in_hbm(moved), *packs, *in_hbm(out)]
+    operands = [*fixed, *sums, *in_hbm(out), *packs]
     return pl.pallas_call(
-        functools.partial(relax_edges_kernel, cuts),
+        functools.partial(finish_kernel, cuts),
         out_shape=pltpu.HBM(out.shape, F32),
-        in_specs=[SMEM_SPEC] * 7
-        + [VMEM_SPEC] * 5
-        + [HBM_SPEC]
-        + [ANY_SPEC] * len(cuts)
-        + [HBM_SPEC],
+        in_specs=[SMEM_SPEC] * 7 + [VMEM_SPEC] * 5 + [HBM_SPEC] + [ANY_SPEC] * len(cuts),
         out_specs=HBM_SPEC,
         scratch_shapes=[
             pltpu.VMEM((2, lane_tiles + 2, 48, LANE), F32),
-            pltpu.VMEM((planes, 3, lane_tiles, ROW, LANE), F32),
+            pltpu.VMEM((planes, 2, lane_tiles, ROW, LANE), F32),
+            pltpu.VMEM((3, lane_tiles, ROW, LANE), F32),
             pltpu.VMEM((lane_tiles, planes * LOW_ROWS + 32, LANE), F32),
             pltpu.VMEM((lane_tiles, planes * HIGH_ROWS + 32, LANE), F32),
             pltpu.VMEM((lane_tiles, ROW, LANE), jnp.int32),
             pltpu.SemaphoreType.DMA((len(cuts),)),
-            pltpu.SemaphoreType.DMA((3,)),
-            pltpu.SemaphoreType.DMA((6,)),
+            pltpu.SemaphoreType.DMA((planes, 2)),
+            pltpu.SemaphoreType.DMA((planes, 2)),
         ],
-        input_output_aliases={len(operands) - 1: 0},
+        input_output_aliases={len(fixed) + len(sums): 0},
         compiler_params=params(24),
-        name="relax_edges",
+        name="finish_edges",
     )(*operands)
 
 
@@ -634,13 +656,12 @@
 
     more = lax.cond(more_needed[0] > 0, send_more, lambda low, high: (low, high), packs[2], packs[3])
     sums_inside = total(inside)
-    out = relax_tiles(plan.inside, meta, small, factor, sums_inside, moved)
     sums_low = total(small_call(join_low_kernel, "join_low", edge_low, from_low, (), 1))
     sums_high = total(small_call(join_high_kernel, "join_high", edge_high, from_high, (), 1))
-
-    out = relax_tiles([row_tiles - 2], meta, small, factor, sums_high, moved, out)
+    sizes = len(plan.inside), 2, 2
+    out = relax_all(sizes, meta, small, factor, sums_inside + sums_high + sums_low, moved)
     halo = low_first, high_first, *more
-    out = relax_edges(meta, small, factor, bars, sums_low + sums_high, moved, halo, cuts, out)
+    out = finish_edges(meta, small, factor, bars, sums_low + sums_high, halo, cuts, out)
     return out.transpose(0, 1, 3, 2, 4).reshape(planes, row_count, col_count)
 
 

time: 65.5 us -> 63.6 us (0.971)
  Pallas kernels: 30 us -> 28.3 us
    pallas_call x3 -> x2, Pallas kernels: 15.6 us -> 13.3 us  [the longest x1 7.81 us: relax_all(): pl.pallas_call(functools.partial(relax_kernel, sizes), out_shape=pltpu.HB...]
    pallas_call x1, Pallas kernels: 0.13 us -> 0.79 us  [fold(): pl.pallas_call(fold_kernel, out_shape=[jax.ShapeDtypeStruct((n, ROW, LANE...]
  transfers between devices with their start and end apart: 11 -> 11, of which waited for: 4 -> 5; matrix products, arithmetic and copies ran while one was open for 0% -> 0% of each run, Pallas kernels for 13% -> 13%
where the time goes in v7:
time: 63.6 us; the launch traced here: 63.2 us
  Pallas kernels  28.3 us (44%)
  starting transfers between devices  26 us (41%)
  waiting for transfers between devices  6.86 us (11%)
  between operations  1.38 us (2%)
  other arithmetic  0.66 us (1%)
    pallas_call x1, Pallas kernels, advance(): pl.pallas_call(functools.partial(advance_kernel, plan, cuts, group), out_...  13.9 us
    ppermute x3, starting transfers between devices, total(): return (whole, lax.ppermute(whole, 'vel', partner))  10.2 us
    pallas_call x1, Pallas kernels, relax_all(): pl.pallas_call(functools.partial(relax_kernel, sizes), out_shape=pltpu.HB...  7.81 us
    pallas_call x1, Pallas kernels, finish_edges(): pl.pallas_call(functools.partial(finish_kernel, cuts), out_shape=pltpu.HB...  5.53 us
    ppermute x1, starting transfers between devices, per_device(): high_first = lax.ppermute(packs[1], 'space', backward)  3.96 us
    ppermute x1, starting transfers between devices, per_device(): from_low = lax.ppermute(up, 'space', forward)  3.11 us
    ppermute x1, starting transfers between devices, per_device(): from_high = lax.ppermute(down, 'space', backward)  3.06 us
    ppermute x3, starting transfers between devices, total(): lax.ppermute(sums, 'vel', across)  2.93 us
  transfers between devices with their start and end apart: 11, of which 5 were waited for; matrix products, arithmetic and copies ran while one was open for 0% of the time, Pallas kernels for 13%

profile of v7, /device:TPU:9, one launch (start us, length us, event | category | flops | bytes accessed | tf_op | source)
XLA Modules:
  0.0 63.2 jit_solution(12264859698353062563)
XLA Ops:
  0.0 0.7 %pad_add_fusion.meta_ref = s32[4]{0:T(128)} fusion(s32[1]{0:T(128)} %bitcast.3, s32[1]{0:T(128)} %bitcast.2, s32[1]{0:T(128)} %bitcast.1, s32[1]{0:T(128)} %bitcast), kind=kLoop, calls=%fused_computation | loop fusion | flops 12 | bytes 32 | tf_op jit(solution)/shard_map/stack | solution.py:628
  0.7 13.9 %advance.1 = (f32[16,8,16,8,128]{4,3,2,1,0:T(8,128)}, f32[324,8,128]{2,1,0:T(8,128)S(1)}, f32[324,8,128]{2,1,0:T(8,128)S(1)}, s32[1]{0:T(128)}, f32[16,72,128]{2...) custom-call(s32[4]{0:T(128)} %pad_add_fusion.meta_ref, s32[16]{0:T(128)} %sx_ref.5, ...), custom_call_target="tpu_custom_call" | custom-call | tf_op jit(solution)/shard_map/advance/pallas_call | solution.py:297
  14.6 0.5 collective-permute-start.2
  15.1 2.7 %collective-permute-done.2.received_ref = f32[324,8,128]{2,1,0:T(8,128)S(1)} collective-permute-done((f32[324,8,128]{2,1,0:T(8,128)S(1)}, f32[324,8,128]{2,1,0:T(8,128)S(1)}, u32[]{:S(2)}, u32[]{:S(2)}) %collective-permute-start.2) | collective-permute-done | bytes 1327136 | tf_op jit(solution)/shard_map/ppermute | solution.py:643
  17.8 0.8 %fold.1 = (f32[36,8,128]{2,1,0:T(8,128)}, f32[32,8,128]{2,1,0:T(8,128)S(1)}, f32[128,8,128]{2,1,0:T(8,128)S(1)}, f32[64,8,128]{2,1,0:T(8,128)S(1)}, f32[64,8,128]{2,1,0:T(8,128)S(1)}) custom-call(f32[324,8,128]{2,1,0:T(8,128)S(1)} %get-tuple-element.30.mine_ref, f32[324,8,128]{2,1,0:T(8,128)S(1)} %collective-permute-done.2.received_ref), custom_call_target="tpu_custom_call" | custom-call | tf_op jit(solution)/shard_map/fold/pallas_call | solution.py:329
  18.6 1.3 %collective-permute-start.9 = (f32[128,8,128]{2,1,0:T(8,128)S(1)}, f32[128,8,128]{2,1,0:T(8,128)S(1)}, u32[]{:S(2)}, u32[]{:S(2)}) collective-permute-start(f32[128,8,128]{2,1,0:T(8,128)S(1)} %get-tuple-element.37.a_ref), channel_id=1, source_target_pairs={{0,2},{1,3},{2,0},{3,1},{4,6},{5,7},{6,4},{7,5},{8,10},{9,11},{10,... | collective-permute-start | bytes 1572872 | tf_op jit(solution)/shard_map/ppermute | solution.py:651
  19.9 3.1 %collective-permute-start.3 = (f32[36,8,128]{2,1,0:T(8,128)}, f32[36,8,128]{2,1,0:T(8,128)S(1)}, u32[]{:S(2)}, u32[]{:S(2)}) collective-permute-start(f32[36,8,128]{2,1,0:T(8,128)} %get-tuple-element.33), channel_id=1, source_target_pairs={{0,4},{4,8},{8,12},{12,16},{16,20},{20,24},{24,28},{1,5},{5,9},{9,... | collective-permute-start | bytes 442376 | tf_op jit(solution)/shard_map/ppermute | solution.py:645
  23.1 3.1 %collective-permute-start.6 = (f32[32,8,128]{2,1,0:T(8,128)S(1)}, f32[32,8,128]{2,1,0:T(8,128)S(1)}, u32[]{:S(2)}, u32[]{:S(2)}) collective-permute-start(f32[32,8,128]{2,1,0:T(8,128)S(1)} %get-tuple-element.35), channel_id=1, source_target_pairs={{4,0},{8,4},{12,8},{16,12},{20,16},{24,20},{28,24},{5,1},{9,5},{13... | collective-permute-start | bytes 393224 | tf_op jit(solution)/shard_map/ppermute | solution.py:646
  26.8 2.2 %collective-permute-start.11 = (f32[16,72,128]{2,1,0:T(8,128)}, f32[16,72,128]{2,1,0:T(8,128)S(1)}, u32[]{:S(2)}, u32[]{:S(2)}) collective-permute-start(f32[16,72,128]{2,1,0:T(8,128)} %get-tuple-element.38), channel_id=1, source_target_pairs={{0,4},{4,8},{8,12},{12,16},{16,20},{20,24},{24,28},{1,5},{5,9},{9,... | collective-permute-start | bytes 1769480 | tf_op jit(solution)/shard_map/ppermute | solution.py:647
  29.0 4.0 %collective-permute-start.12 = (f32[16,72,128]{2,1,0:T(8,128)}, f32[16,72,128]{2,1,0:T(8,128)S(1)}, u32[]{:S(2)}, u32[]{:S(2)}) collective-permute-start(f32[16,72,128]{2,1,0:T(8,128)} %get-tuple-element.39), channel_id=1, source_target_pairs={{4,0},{8,4},{12,8},{16,12},{20,16},{24,20},{28,24},{5,1},{9,5},{13... | collective-permute-start | bytes 1769480 | tf_op jit(solution)/shard_map/ppermute | solution.py:648
  32.9 0.0 collective-permute-done.6.high_ref
  33.0 0.2 collective-permute-start.7
  33.2 0.0 collective-permute-done.3.low_ref
  33.2 1.4 %collective-permute-start.4 = (f32[65,8,128]{2,1,0:T(8,128)S(1)}, f32[65,8,128]{2,1,0:T(8,128)S(1)}, u32[]{:S(2)}, u32[]{:S(2)}) collective-permute-start(f32[65,8,128]{2,1,0:T(8,128)S(1)} %join_low.1.a_ref), channel_id=1, source_target_pairs={{0,2},{1,3},{2,0},{3,1},{4,6},{5,7},{6,4},{7,5},{8,10},{9,11},{10,... | collective-permute-start | bytes 798728 | tf_op jit(solution)/shard_map/ppermute | solution.py:651
  34.6 0.0 collective-permute-done.9.b_ref
  34.6 0.1 add.16.refs_0_
  34.7 2.4 %collective-permute-start.10 = (f32[128,8,128]{2,1,0:T(8,128)S(1)}, f32[128,8,128]{2,1,0:T(8,128)S(1)}, u32[]{:S(2)}, u32[]{:S(2)}) collective-permute-start(f32[128,8,128]{2,1,0:T(8,128)S(1)} %add.16.refs_0_), channel_id=1, source_target_pairs={{0,1},{1,0},{2,3},{3,2},{4,5},{5,4},{6,7},{7,6},{8,9},{9,8},{10,11... | collective-permute-start | bytes 1572872 | tf_op jit(solution)/shard_map/ppermute | solution.py:652
  37.1 2.1 %collective-permute-done.7.b_ref = f32[65,8,128]{2,1,0:T(8,128)S(1)} collective-permute-done((f32[65,8,128]{2,1,0:T(8,128)S(1)}, f32[65,8,128]{2,1,0:T(8,128)S(1)}, u32[]{:S(2)}, u32[]{:S(2)}) %collective-permute-start.7) | collective-permute-done | bytes 266272 | tf_op jit(solution)/shard_map/ppermute | solution.py:651
  39.2 5.1 %collective-permute-start.8 = (f32[65,8,128]{2,1,0:T(8,128)S(1)}, f32[65,8,128]{2,1,0:T(8,128)S(1)}, u32[]{:S(2)}, u32[]{:S(2)}) collective-permute-start(f32[65,8,128]{2,1,0:T(8,128)S(1)} %add.15.refs_2_.m_high), channel_id=1, source_target_pairs={{0,1},{1,0},{2,3},{3,2},{4,5},{5,4},{6,7},{7,6},{8,9},{9,8},{10,11... | collective-permute-start | bytes 798728 | tf_op jit(solution)/shard_map/ppermute | solution.py:652
  44.3 0.6 collective-permute-done.4.b_ref
  44.9 2.8 %collective-permute-start.5 = (f32[65,8,128]{2,1,0:T(8,128)S(1)}, f32[65,8,128]{2,1,0:T(8,128)S(1)}, u32[]{:S(2)}, u32[]{:S(2)}) collective-permute-start(f32[65,8,128]{2,1,0:T(8,128)S(1)} %add.14.refs_4_.m_low), channel_id=1, source_target_pairs={{0,1},{1,0},{2,3},{3,2},{4,5},{5,4},{6,7},{7,6},{8,9},{9,8},{10,11... | collective-permute-start | bytes 798728 | tf_op jit(solution)/shard_map/ppermute | solution.py:652
  48.3 0.0 collective-permute-done.8.refs_3_.o_high
  48.3 0.5 collective-permute-done.5.refs_5_.o_low
  48.8 0.0 collective-permute-done.10.refs_1_
  48.8 0.0 copy-start
  48.9 0.0 copy-start.1
  48.9 7.8 %relax_all.1.before_ref = f32[16,8,16,8,128]{4,3,2,1,0:T(8,128)} custom-call(s32[4]{0:T(128)} %pad_add_fusion.meta_ref, s32[16]{0:T(128)} %sx_ref.5, s32[16]{0:T(128)} %sy_ref.5, f32[16]{0:T(128)} %fx_ref.5, f32[16]{0:T(128)} %fy_ref.5, f32[1]{0:T(128)} %bitcast.13.factor_ref, f32[16,8,16,8,128]{4,3,2,1,0:T(8,128)} %get-tuple-element.36.planes_ref, ...), custom_call_target="tpu_custom_call" | custom-call | tf_op jit(solution)/shard_map/relax_all/pallas_call | solution.py:463
  56.7 0.0 collective-permute-done.11.refs_0_
  56.7 1.0 %collective-permute-done.12.refs_1_ = f32[16,72,128]{2,1,0:T(8,128)S(1)} collective-permute-done((f32[16,72,128]{2,1,0:T(8,128)}, f32[16,72,128]{2,1,0:T(8,128)S(1)}, u32[]{:S(2)}, u32[]{:S(2)}) %collective-permute-start.12) | collective-permute-done | bytes 589856 | tf_op jit(solution)/shard_map/ppermute | solution.py:648
  57.6 0.0 copy-done
  57.6 0.0 copy-done.1
  57.7 5.5 %finish_edges.1 = f32[16,8,16,8,128]{4,3,2,1,0:T(8,128)} custom-call(s32[4]{0:T(128)} %pad_add_fusion.meta_ref, s32[16]{0:T(128)} %sx_ref.5, s32[16]{0:T(128)} %sy_ref.5, f32[16]{0:T(128)} %fx_ref.5, f32[16]{0:T(128)} %fy_ref.5, f32[16]{0:T(128)} %inflow_ref.3, f32[1]{0:T(128)} %bitcast.14.factor_ref, ...), custom_call_target="tpu_custom_call", output_to_operand_aliasing={{}: (12, {})} | custom-call | tf_op jit(solution)/shard_map/finish_edges/pallas_call | solution.py:595
  (5 shorter events, 0.1 us)
Async XLA Ops:
  14.6 3.2 %collective-permute-start.2 = (f32[324,8,128]{2,1,0:T(8,128)S(1)}, f32[324,8,128]{2,1,0:T(8,128)S(1)}, u32[]{:S(2)}, u32[]{:S(2)}) collective-permute-start(f32[324,8,128]{2,1,0:T(8,128)S(1)} %get-tuple-element.31), channel_id=1, source_target_pairs={{0,1},{1,0},{2,3},{3,2},{4,5},{5,4},{6,7},{7,6},{8,9},{9,8},{10,11... | collective-permute-start | bytes 3981320 | tf_op jit(solution)/shard_map/ppermute | solution.py:643
  18.6 16.0 %collective-permute-start.9 = (f32[128,8,128]{2,1,0:T(8,128)S(1)}, f32[128,8,128]{2,1,0:T(8,128)S(1)}, u32[]{:S(2)}, u32[]{:S(2)}) collective-permute-start(f32[128,8,128]{2,1,0:T(8,128)S(1)} %get-tuple-element.37.a_ref), channel_id=1, source_target_pairs={{0,2},{1,3},{2,0},{3,1},{4,6},{5,7},{6,4},{7,5},{8,10},{9,11},{10,... | collective-permute-start | bytes 1572872 | tf_op jit(solution)/shard_map/ppermute | solution.py:651
  19.9 13.3 %collective-permute-start.3 = (f32[36,8,128]{2,1,0:T(8,128)}, f32[36,8,128]{2,1,0:T(8,128)S(1)}, u32[]{:S(2)}, u32[]{:S(2)}) collective-permute-start(f32[36,8,128]{2,1,0:T(8,128)} %get-tuple-element.33), channel_id=1, source_target_pairs={{0,4},{4,8},{8,12},{12,16},{16,20},{20,24},{24,28},{1,5},{5,9},{9,... | collective-permute-start | bytes 442376 | tf_op jit(solution)/shard_map/ppermute | solution.py:645
  23.1 9.9 %collective-permute-start.6 = (f32[32,8,128]{2,1,0:T(8,128)S(1)}, f32[32,8,128]{2,1,0:T(8,128)S(1)}, u32[]{:S(2)}, u32[]{:S(2)}) collective-permute-start(f32[32,8,128]{2,1,0:T(8,128)S(1)} %get-tuple-element.35), channel_id=1, source_target_pairs={{4,0},{8,4},{12,8},{16,12},{20,16},{24,20},{28,24},{5,1},{9,5},{13... | collective-permute-start | bytes 393224 | tf_op jit(solution)/shard_map/ppermute | solution.py:646
  26.8 29.9 %collective-permute-start.11 = (f32[16,72,128]{2,1,0:T(8,128)}, f32[16,72,128]{2,1,0:T(8,128)S(1)}, u32[]{:S(2)}, u32[]{:S(2)}) collective-permute-start(f32[16,72,128]{2,1,0:T(8,128)} %get-tuple-element.38), channel_id=1, source_target_pairs={{0,4},{4,8},{8,12},{12,16},{16,20},{20,24},{24,28},{1,5},{5,9},{9,... | collective-permute-start | bytes 1769480 | tf_op jit(solution)/shard_map/ppermute | solution.py:647
  29.0 28.7 %collective-permute-start.12 = (f32[16,72,128]{2,1,0:T(8,128)}, f32[16,72,128]{2,1,0:T(8,128)S(1)}, u32[]{:S(2)}, u32[]{:S(2)}) collective-permute-start(f32[16,72,128]{2,1,0:T(8,128)} %get-tuple-element.39), channel_id=1, source_target_pairs={{4,0},{8,4},{12,8},{16,12},{20,16},{24,20},{28,24},{5,1},{9,5},{13... | collective-permute-start | bytes 1769480 | tf_op jit(solution)/shard_map/ppermute | solution.py:648
  33.0 6.2 %collective-permute-start.7 = (f32[65,8,128]{2,1,0:T(8,128)S(1)}, f32[65,8,128]{2,1,0:T(8,128)S(1)}, u32[]{:S(2)}, u32[]{:S(2)}) collective-permute-start(f32[65,8,128]{2,1,0:T(8,128)S(1)} %join_high.1.a_ref), channel_id=1, source_target_pairs={{0,2},{1,3},{2,0},{3,1},{4,6},{5,7},{6,4},{7,5},{8,10},{9,11},{10,... | collective-permute-start | bytes 798728 | tf_op jit(solution)/shard_map/ppermute | solution.py:651
  33.2 11.6 %collective-permute-start.4 = (f32[65,8,128]{2,1,0:T(8,128)S(1)}, f32[65,8,128]{2,1,0:T(8,128)S(1)}, u32[]{:S(2)}, u32[]{:S(2)}) collective-permute-start(f32[65,8,128]{2,1,0:T(8,128)S(1)} %join_low.1.a_ref), channel_id=1, source_target_pairs={{0,2},{1,3},{2,0},{3,1},{4,6},{5,7},{6,4},{7,5},{8,10},{9,11},{10,... | collective-permute-start | bytes 798728 | tf_op jit(solution)/shard_map/ppermute | solution.py:651
  34.7 14.2 %collective-permute-start.10 = (f32[128,8,128]{2,1,0:T(8,128)S(1)}, f32[128,8,128]{2,1,0:T(8,128)S(1)}, u32[]{:S(2)}, u32[]{:S(2)}) collective-permute-start(f32[128,8,128]{2,1,0:T(8,128)S(1)} %add.16.refs_0_), channel_id=1, source_target_pairs={{0,1},{1,0},{2,3},{3,2},{4,5},{5,4},{6,7},{7,6},{8,9},{9,8},{10,11... | collective-permute-start | bytes 1572872 | tf_op jit(solution)/shard_map/ppermute | solution.py:652
  39.2 9.1 %collective-permute-start.8 = (f32[65,8,128]{2,1,0:T(8,128)S(1)}, f32[65,8,128]{2,1,0:T(8,128)S(1)}, u32[]{:S(2)}, u32[]{:S(2)}) collective-permute-start(f32[65,8,128]{2,1,0:T(8,128)S(1)} %add.15.refs_2_.m_high), channel_id=1, source_target_pairs={{0,1},{1,0},{2,3},{3,2},{4,5},{5,4},{6,7},{7,6},{8,9},{9,8},{10,11... | collective-permute-start | bytes 798728 | tf_op jit(solution)/shard_map/ppermute | solution.py:652
  44.9 3.9 %collective-permute-start.5 = (f32[65,8,128]{2,1,0:T(8,128)S(1)}, f32[65,8,128]{2,1,0:T(8,128)S(1)}, u32[]{:S(2)}, u32[]{:S(2)}) collective-permute-start(f32[65,8,128]{2,1,0:T(8,128)S(1)} %add.14.refs_4_.m_low), channel_id=1, source_target_pairs={{0,1},{1,0},{2,3},{3,2},{4,5},{5,4},{6,7},{7,6},{8,9},{9,8},{10,11... | collective-permute-start | bytes 798728 | tf_op jit(solution)/shard_map/ppermute | solution.py:652
  48.8 8.8 %copy-start = (f32[16,72,128]{2,1,0:T(8,128)S(1)}, f32[16,72,128]{2,1,0:T(8,128)}, u32[]{:S(2)}) copy-start(f32[16,72,128]{2,1,0:T(8,128)} %get-tuple-element.43.refs_2_) | copy-start | bytes 1769476
  48.9 8.8 %copy-start.1 = (f32[16,56,128]{2,1,0:T(8,128)S(1)}, f32[16,56,128]{2,1,0:T(8,128)}, u32[]{:S(2)}) copy-start(f32[16,56,128]{2,1,0:T(8,128)} %get-tuple-element.44.refs_3_) | copy-start | bytes 1376260
